TPU v7x, 128 devices: a whole 4x4x4 slice. The times are simulated.
128 devices in a mesh: row: 4 (over y), col: 32 (over z, x, core).
Axes of the slice: x: 4, y: 4, z: 4, core: 2. Of those that a mesh axis runs over, the one named last changes fastest.
Arguments:
- tokens_in: bfloat16 [32768, 1024], P(('row', 'col')), may hold values from -6 to 6
- out_cot: bfloat16 [32768, 1024], P(('row', 'col')), may hold values from -6 to 6
- long_lengths: int32 [32], P('col'), may hold values from 385 to 512, as said below
- short_lengths: int32 [128], P(('row', 'col')), may hold values from 32 to 128, as said below
- routes: int32 [32768, 2], P(('row', 'col')), may hold values from 0 to 31, all different within a row; in each aligned block of 256 rows (0 to 255, 256 to 511, ...) at most 20 rows name the same one
- gain_attn: float32 [1024], replicated, may hold values from 0.5 to 1.5
- w_query: bfloat16 [1024, 1024], replicated, may hold values from -0.1875 to 0.1875
- w_key: bfloat16 [1024, 1024], replicated, may hold values from -0.1875 to 0.1875
- w_value: bfloat16 [1024, 1024], replicated, may hold values from -0.1875 to 0.1875
- w_out: bfloat16 [1024, 1024], replicated, may hold values from -1 to 1
- rel_bias: float32 [32, 16], replicated, may hold values from -4 to 4
- gain_moe: float32 [1024], replicated, may hold values from 0.5 to 1.5
- router: float32 [1024, 32], replicated, may hold values from -0.125 to 0.125
- w_gate: bfloat16 [32, 1024, 2816], P('col', None, 'row'), may hold values from -0.1875 to 0.1875
- w_up: bfloat16 [32, 1024, 2816], P('col', None, 'row'), may hold values from -0.1875 to 0.1875
- w_down: bfloat16 [32, 2816, 1024], P('col', 'row'), may hold values from -0.15625 to 0.15625
Outputs:
- block_out: float32 [32768, 1024], P(('row', 'col'))
- tokens_grad: float32 [32768, 1024], P(('row', 'col'))
- gain_attn_grad: float32 [1024], replicated
- query_grad: float32 [1024, 1024], replicated
- key_grad: float32 [1024, 1024], replicated
- value_grad: float32 [1024, 1024], replicated
- out_proj_grad: float32 [1024, 1024], replicated
- bias_grad: float32 [32, 16], replicated
- gain_moe_grad: float32 [1024], replicated
- router_grad: float32 [1024, 32], replicated
- gate_grad: float32 [32, 1024, 2816], P('col', None, 'row')
- up_grad: float32 [32, 1024, 2816], P('col', None, 'row')
- down_grad: float32 [32, 2816, 1024], P('col', 'row')
- statistics: float32 [3], replicated
Inputs may be any that keep to these rules, and one draw needn't show every extreme that they name: `routes`: each row names two different experts. Within the rows of one device no expert is named by more than 20 rows, and in some device one expert is named by exactly 20. `long_lengths`: one long sequence has all 512 positions live. `short_lengths`: one short sequence has all 128 positions live.
All inputs are finite; a program needn't handle non-finite values.
Results may differ from a plain program's by a relative error of at most 0.017.
Values may be sent and summed in bfloat16 or wider, within the bound.
A program may use at most 192 MiB of HBM per device.

v0:
```python
import jax
import jax.numpy as jnp
from jax import lax
from jax.sharding import PartitionSpec as P

HEADS = 16
HEAD_DIM = 64
LONG_DEV = 128
SHORT_LEN = 128
UNITS = 1


bucket_edges = (1, 2, 3, 4, 5, 6, 7, 8, 12, 16, 23, 32, 46, 64, 91)
norm_eps = 1e-06
balance_coef = 0.01
zloss_coef = 0.001
masked_score = -1e30
highest = lax.Precision.HIGHEST


def rms_norm(values, gain):
    return values * lax.rsqrt(jnp.mean(values * values, axis=-1, keepdims=True) + norm_eps) * gain


def geglu(gate_pre, up_pre):
    return jax.nn.gelu(gate_pre, approximate=True) * up_pre


def geglu_back(gate_pre, up_pre, d_act):
    unused, back = jax.vjp(geglu, gate_pre, up_pre)
    d_gate, d_up = back(d_act)
    return (d_gate.astype(jnp.bfloat16), d_up.astype(jnp.bfloat16))


def rel_buckets(query_pos, key_pos):
    relative = key_pos[None, :] - query_pos[:, None]
    magnitude = jnp.abs(relative)
    edges = jnp.array(bucket_edges, jnp.int32)
    level = jnp.sum((magnitude[:, :, None] >= edges[None, None, :]).astype(jnp.int32), axis=2)
    return level + jnp.where(relative > 0, len(bucket_edges) + 1, 0)


def bucket_table(query_pos, key_pos, count):
    buckets = rel_buckets(query_pos, key_pos)
    return (buckets[None, :, :] == jnp.arange(count, dtype=jnp.int32)[:, None, None]).astype(
        jnp.float32
    )


def score_block(query, keys, bias, valid):
    raw = jnp.einsum("bqhe,bkhe->bhqk", query, keys, preferred_element_type=jnp.float32)
    raw = raw * query.shape[-1] ** (-0.5) + bias[None]
    return jnp.where(valid[:, None, None, :], raw, masked_score)


def attend_forward(query, keys, values, bias, valid):
    scores = score_block(query, keys, bias, valid)
    row_max = jnp.max(scores, axis=-1, keepdims=True)
    exp_terms = jnp.exp(scores - row_max)
    row_total = jnp.sum(exp_terms, axis=-1, keepdims=True)
    probs = (exp_terms / row_total).astype(jnp.bfloat16)
    mixed = jnp.einsum("bhqk,bkhe->bqhe", probs, values, preferred_element_type=jnp.float32)
    return (mixed.astype(jnp.bfloat16), row_max + jnp.log(row_total))


def attend_backward(query, keys, values, bias, valid, log_norm, d_mixed):
    scale = query.shape[-1] ** (-0.5)
    scores = score_block(query, keys, bias, valid)
    probs = jnp.exp(scores - log_norm)
    d_values = jnp.einsum(
        "bhqk,bqhe->bkhe", probs.astype(jnp.bfloat16), d_mixed, preferred_element_type=jnp.float32
    )
    d_probs = jnp.einsum("bqhe,bkhe->bhqk", d_mixed, values, preferred_element_type=jnp.float32)
    spread = jnp.sum(probs * d_probs, axis=-1, keepdims=True)
    d_scores = (probs * (d_probs - spread)).astype(jnp.bfloat16)
    d_query = (
        jnp.einsum("bhqk,bkhe->bqhe", d_scores, keys, preferred_element_type=jnp.float32) * scale
    )
    d_keys = (
        jnp.einsum("bhqk,bqhe->bkhe", d_scores, query, preferred_element_type=jnp.float32) * scale
    )
    return (d_query, d_keys, d_values, d_scores)


def per_device(
    tokens_in,
    out_cot,
    long_lengths,
    short_lengths,
    routes,
    gain_attn,
    w_query,
    w_key,
    w_value,
    w_out,
    rel_bias,
    gain_moe,
    router,
    w_gate,
    w_up,
    w_down,
):
    tok_dev, width = tokens_in.shape
    experts = router.shape[1]
    local_experts = w_gate.shape[0]
    buckets_count = rel_bias.shape[0]
    topk = routes.shape[1]
    long_rows = UNITS * LONG_DEV
    long_len = LONG_DEV * lax.axis_size("row")
    capacity = (10 * tok_dev + 4 * experts - 1) // (4 * experts)

    def heads(rows, count, length):
        return rows.reshape(count, length, HEADS, HEAD_DIM)

    inputs = tokens_in.astype(jnp.float32)
    normed_a, norm_a_back = jax.vjp(rms_norm, inputs, gain_attn)
    normed_ab = normed_a.astype(jnp.bfloat16)
    query = jnp.dot(normed_ab, w_query, preferred_element_type=jnp.float32).astype(jnp.bfloat16)
    keys = jnp.dot(normed_ab, w_key, preferred_element_type=jnp.float32).astype(jnp.bfloat16)
    values = jnp.dot(normed_ab, w_value, preferred_element_type=jnp.float32).astype(jnp.bfloat16)
    long_kg, long_vg = (
        lax.all_gather(keys[:long_rows].reshape(UNITS, LONG_DEV, width), "row", axis=1, tiled=True),
        lax.all_gather(
            values[:long_rows].reshape(UNITS, LONG_DEV, width), "row", axis=1, tiled=True
        ),
    )
    long_q = heads(query[:long_rows], UNITS, LONG_DEV)
    long_k = heads(long_kg, UNITS, long_len)
    long_v = heads(long_vg, UNITS, long_len)
    short_q = heads(query[long_rows:], UNITS, SHORT_LEN)
    short_k = heads(keys[long_rows:], UNITS, SHORT_LEN)
    short_v = heads(values[long_rows:], UNITS, SHORT_LEN)
    long_qpos = lax.axis_index("row") * LONG_DEV + jnp.arange(LONG_DEV, dtype=jnp.int32)
    long_kpos = jnp.arange(long_len, dtype=jnp.int32)
    short_pos = jnp.arange(SHORT_LEN, dtype=jnp.int32)
    long_hot = bucket_table(long_qpos, long_kpos, buckets_count)
    short_hot = bucket_table(short_pos, short_pos, buckets_count)
    long_bias = jnp.einsum("nqk,nh->hqk", long_hot, rel_bias, precision=highest)
    short_bias = jnp.einsum("nqk,nh->hqk", short_hot, rel_bias, precision=highest)
    long_valid = long_kpos[None, :] < long_lengths[:, None]
    short_valid = short_pos[None, :] < short_lengths[:, None]
    long_o, long_norm = attend_forward(long_q, long_k, long_v, long_bias, long_valid)
    short_o, short_norm = attend_forward(short_q, short_k, short_v, short_bias, short_valid)
    mixed = jnp.concatenate([long_o.reshape(long_rows, width), short_o.reshape(-1, width)], axis=0)
    branch_a = jnp.dot(mixed, w_out, preferred_element_type=jnp.float32)
    resid = inputs + branch_a
    normed_m, norm_m_back = jax.vjp(rms_norm, resid, gain_moe)
    normed_mb = normed_m.astype(jnp.bfloat16)
    logits = jnp.dot(normed_m, router, precision=highest, preferred_element_type=jnp.float32)
    row_max = jnp.max(logits, axis=1, keepdims=True)
    exp_terms = jnp.exp(logits - row_max)
    row_total = jnp.sum(exp_terms, axis=1, keepdims=True)
    probs = exp_terms / row_total
    router_norm = row_max[:, 0] + jnp.log(row_total[:, 0])
    expert_ids = jnp.arange(experts, dtype=jnp.int32)
    route_match = routes[:, :, None] == expert_ids[None, None, :]
    route_hot = route_match.astype(jnp.float32)
    picked = jnp.sum(probs[:, None, :] * route_hot, axis=2)
    picked_sum = jnp.sum(picked, axis=1, keepdims=True)
    gates = picked / picked_sum
    fraction = jnp.sum(route_hot, axis=(0, 1)) / (topk * tok_dev)
    flat_hot = route_match.astype(jnp.int32).reshape(-1, experts)
    earlier = jnp.cumsum(flat_hot, axis=0) - flat_hot
    slots = jnp.sum(earlier * flat_hot, axis=1).reshape(tok_dev, topk)
    place = routes * capacity + slots
    slot_ids = jnp.arange(experts * capacity, dtype=jnp.int32)
    place_hot = (jnp.transpose(place)[:, :, None] == slot_ids[None, None, :]).astype(jnp.bfloat16)
    buffer = jnp.einsum(
        "ktp,td->pd", place_hot, normed_mb, preferred_element_type=jnp.float32
    ).astype(jnp.bfloat16)
    received = lax.all_to_all(
        buffer.reshape(experts, capacity, width), "col", split_axis=0, concat_axis=0, tiled=True
    )
    received = received.reshape(-1, local_experts, capacity, width)
    gate_full, up_full, down_full = (
        lax.all_gather(w_gate, "row", axis=2, tiled=True),
        lax.all_gather(w_up, "row", axis=2, tiled=True),
        lax.all_gather(w_down, "row", axis=1, tiled=True),
    )
    gate_pre = jnp.einsum("sjcd,jdf->sjcf", received, gate_full, preferred_element_type=jnp.float32)
    up_pre = jnp.einsum("sjcd,jdf->sjcf", received, up_full, preferred_element_type=jnp.float32)
    act_b = geglu(gate_pre, up_pre).astype(jnp.bfloat16)
    expert_out = jnp.einsum("sjcf,jfd->sjcd", act_b, down_full, preferred_element_type=jnp.float32)
    returned = lax.all_to_all(
        expert_out.astype(jnp.bfloat16), "col", split_axis=0, concat_axis=0, tiled=True
    ).reshape(experts * capacity, width)
    chosen = jnp.einsum("ktp,pd->tkd", place_hot, returned, preferred_element_type=jnp.float32)
    branch_m = jnp.sum(gates[:, :, None] * chosen, axis=1)
    outputs = resid + branch_m
    long_live = (long_qpos[None, :] < long_lengths[:, None]).reshape(-1)
    short_live = (short_pos[None, :] < short_lengths[:, None]).reshape(-1)
    live = jnp.concatenate([long_live, short_live]).astype(jnp.float32)

    def live_squares(field):
        return jnp.sum(live * jnp.sum(field * field, axis=1))

    tallies = jnp.stack(
        [live_squares(outputs), live_squares(branch_a), live_squares(branch_m), jnp.sum(live)]
    )
    d_out = out_cot.astype(jnp.float32)
    weighted = (gates[:, :, None] * d_out[:, None, :]).astype(jnp.bfloat16)
    d_returned = jnp.einsum(
        "ktp,tkd->pd", place_hot, weighted, preferred_element_type=jnp.float32
    ).astype(jnp.bfloat16)
    d_gates = jnp.sum(chosen * d_out[:, None, :], axis=2)
    d_picked = d_gates / picked_sum - jnp.sum(d_gates * picked, axis=1, keepdims=True) / (
        picked_sum * picked_sum
    )
    d_probs = (
        jnp.sum(d_picked[:, :, None] * route_hot, axis=1)
        + balance_coef * experts * fraction[None, :]
    )
    d_logits = (
        probs * (d_probs - jnp.sum(d_probs * probs, axis=1, keepdims=True))
        + 2.0 * zloss_coef * router_norm[:, None] * probs
    )
    d_router = jnp.einsum(
        "td,te->de", normed_m, d_logits, precision=highest, preferred_element_type=jnp.float32
    )
    d_normed = jnp.einsum(
        "te,de->td", d_logits, router, precision=highest, preferred_element_type=jnp.float32
    )
    d_received = lax.all_to_all(
        d_returned.reshape(experts, capacity, width), "col", split_axis=0, concat_axis=0, tiled=True
    )
    d_received = d_received.reshape(-1, local_experts, capacity, width)
    d_act = jnp.einsum("sjcd,jfd->sjcf", d_received, down_full, preferred_element_type=jnp.float32)
    d_gate_b, d_up_b = geglu_back(gate_pre, up_pre, d_act)
    d_down_full = jnp.einsum(
        "sjcf,sjcd->jfd", act_b, d_received, preferred_element_type=jnp.float32
    )
    d_gate_full = jnp.einsum(
        "sjcd,sjcf->jdf", received, d_gate_b, preferred_element_type=jnp.float32
    )
    d_up_full = jnp.einsum("sjcd,sjcf->jdf", received, d_up_b, preferred_element_type=jnp.float32)
    d_rows = jnp.einsum("sjcf,jdf->sjcd", d_gate_b, gate_full, preferred_element_type=jnp.float32)
    d_rows = d_rows + jnp.einsum(
        "sjcf,jdf->sjcd", d_up_b, up_full, preferred_element_type=jnp.float32
    )
    d_gate_w, d_up_w, d_down_w = (
        lax.psum_scatter(
            d_gate_full.astype(jnp.bfloat16), "row", scatter_dimension=2, tiled=True
        ).astype(jnp.float32),
        lax.psum_scatter(
            d_up_full.astype(jnp.bfloat16), "row", scatter_dimension=2, tiled=True
        ).astype(jnp.float32),
        lax.psum_scatter(
            d_down_full.astype(jnp.bfloat16), "row", scatter_dimension=1, tiled=True
        ).astype(jnp.float32),
    )
    d_sent = lax.all_to_all(
        d_rows.astype(jnp.bfloat16), "col", split_axis=0, concat_axis=0, tiled=True
    ).reshape(experts * capacity, width)
    d_normed = d_normed + jnp.einsum(
        "ktp,pd->td", place_hot, d_sent, preferred_element_type=jnp.float32
    )
    d_resid_norm, d_gain_m = norm_m_back(d_normed)
    d_resid = d_out + d_resid_norm
    d_branch = d_resid.astype(jnp.bfloat16)
    d_w_out = jnp.einsum("td,te->de", mixed, d_branch, preferred_element_type=jnp.float32)
    d_mixed = jnp.einsum("te,de->td", d_branch, w_out, preferred_element_type=jnp.float32).astype(
        jnp.bfloat16
    )
    long_dq, long_dk, long_dv, long_ds = attend_backward(
        long_q,
        long_k,
        long_v,
        long_bias,
        long_valid,
        long_norm,
        heads(d_mixed[:long_rows], UNITS, LONG_DEV),
    )
    short_dq, short_dk, short_dv, short_ds = attend_backward(
        short_q,
        short_k,
        short_v,
        short_bias,
        short_valid,
        short_norm,
        heads(d_mixed[long_rows:], UNITS, SHORT_LEN),
    )
    own_dk, own_dv = (
        lax.psum_scatter(
            long_dk.reshape(UNITS, long_len, width).astype(jnp.bfloat16),
            "row",
            scatter_dimension=1,
            tiled=True,
        ).astype(jnp.float32),
        lax.psum_scatter(
            long_dv.reshape(UNITS, long_len, width).astype(jnp.bfloat16),
            "row",
            scatter_dimension=1,
            tiled=True,
        ).astype(jnp.float32),
    )
    d_bias = jnp.einsum(
        "bhqk,nqk->nh", long_ds, long_hot.astype(jnp.bfloat16), preferred_element_type=jnp.float32
    )
    d_bias = d_bias + jnp.einsum(
        "bhqk,nqk->nh", short_ds, short_hot.astype(jnp.bfloat16), preferred_element_type=jnp.float32
    )
    d_query = jnp.concatenate(
        [long_dq.reshape(long_rows, width), short_dq.reshape(-1, width)], axis=0
    ).astype(jnp.bfloat16)
    d_keys = jnp.concatenate(
        [own_dk.reshape(long_rows, width), short_dk.reshape(-1, width)], axis=0
    ).astype(jnp.bfloat16)
    d_values = jnp.concatenate(
        [own_dv.reshape(long_rows, width), short_dv.reshape(-1, width)], axis=0
    ).astype(jnp.bfloat16)
    d_w_query = jnp.einsum("td,te->de", normed_ab, d_query, preferred_element_type=jnp.float32)
    d_w_key = jnp.einsum("td,te->de", normed_ab, d_keys, preferred_element_type=jnp.float32)
    d_w_value = jnp.einsum("td,te->de", normed_ab, d_values, preferred_element_type=jnp.float32)
    d_normed_a = jnp.einsum("te,de->td", d_query, w_query, preferred_element_type=jnp.float32)
    d_normed_a = d_normed_a + jnp.einsum(
        "te,de->td", d_keys, w_key, preferred_element_type=jnp.float32
    )
    d_normed_a = d_normed_a + jnp.einsum(
        "te,de->td", d_values, w_value, preferred_element_type=jnp.float32
    )
    d_inputs_norm, d_gain_a = norm_a_back(d_normed_a)
    d_inputs = d_resid + d_inputs_norm
    summed = lax.psum(
        (d_gain_a, d_w_query, d_w_key, d_w_value, d_w_out, d_bias, d_gain_m, d_router, tallies),
        ("row", "col"),
    )
    totals = summed[8]
    statistics = jnp.stack(
        [
            jnp.sqrt(totals[0] / (totals[3] * width)),
            jnp.sqrt(totals[1] / (totals[3] * width)),
            jnp.sqrt(totals[2] / (totals[3] * width)),
        ]
    )
    return (
        outputs,
        d_inputs,
        summed[0],
        summed[1],
        summed[2],
        summed[3],
        summed[4],
        summed[5],
        summed[6],
        summed[7],
        d_gate_w,
        d_up_w,
        d_down_w,
        statistics,
    )


def solution(mesh):
    placed = (
        P(("row", "col"), None),
        P(("row", "col"), None),
        P("col"),
        P(("row", "col")),
        P(("row", "col"), None),
        P(),
        P(),
        P(),
        P(),
        P(),
        P(),
        P(),
        P(),
        P("col", None, "row"),
        P("col", None, "row"),
        P("col", "row", None),
    )
    return jax.shard_map(
        per_device,
        mesh=mesh,
        in_specs=placed,
        out_specs=(
            P(("row", "col"), None),
            P(("row", "col"), None),
            P(),
            P(),
            P(),
            P(),
            P(),
            P(),
            P(),
            P(),
            P("col", None, "row"),
            P("col", None, "row"),
            P("col", "row", None),
            P(),
        ),
        check_vma=False,
    )
```

profile of v0, /device:TPU:1, one launch (start us, length us, event | category | flops | bytes accessed | tf_op | source)
XLA Modules:
  0.0 854.3 jit_solution(18128816207400747295)
XLA Ops:
  34.6 5.2 copy.202
  45.6 20.0 %all-gather.14.cloned.1.call-done = bf16[512,1024]{1,0:T(8,128)(2,1)} async-done(((bf16[128,1024]{1,0:T(8,128)(2,1)}), bf16[512,1024]{1,0:T(8,128)(2,1)}) %all-gather.14.cloned.1.call-update) | async-done | bytes 1048592 | tf_op jit(solution)/shard_map/all_gather | solution.py:123
  81.5 9.3 %all-to-all-start = ((bf16[32,20,1024]{2,1,0:T(8,128)(2,1)}), bf16[32,20,1024]{2,1,0:T(8,128)(2,1)}, u32[]{:S(2)}, u32[]{:S(2)}) async-start(bf16[32,20,1024]{2,1,0:T(8,128)(2,1)} %reshape.614), calls=%async_computation | async-start | bytes 3145728 | tf_op jit(solution)/shard_map/all_to_all | solution.py:171
  104.1 8.6 %all-to-all-done = bf16[32,20,1024]{2,1,0:T(8,128)(2,1)} async-done(((bf16[32,20,1024]{2,1,0:T(8,128)(2,1)}), bf16[32,20,1024]{2,1,0:T(8,128)(2,1)}, u32[]{:S(2)}, u32[]{:S(2)}) %all-to-all-start) | async-done | bytes 1310752 | tf_op jit(solution)/shard_map/all_to_all | solution.py:171
  112.7 6.4 all-to-all-start.2
  119.1 10.8 %all-gather.10.cloned.1.call-done = bf16[1,1024,2816]{1,2,0:T(8,128)(2,1)} async-done(((bf16[1,1024,704]{1,2,0:T(8,128)(2,1)}), bf16[1,1024,2816]{1,2,0:T(8,128)(2,1)}) %all-gather.10.cloned.1.call-update) | async-done | bytes 5767184 | tf_op jit(solution)/shard_map/all_gather | solution.py:177
  129.9 10.6 %fusion.14 = f32[32,20,2816]{2,0,1:T(8,128)} fusion(bf16[1,1024,2816]{1,2,0:T(8,128)(2,1)} %all-gather.10.cloned.1.call-done, bf16[32,20,1024]{2,1,0:T(8,128)(2,1)} %all-to-all-done), kind=kOutput, calls=%fused_computation.26 | convolution fusion | flops 3690987520 | bytes 14286848 | tf_op jit(solution)/shard_map/sjcd,jdf->sjcf/dot_general | solution.py:181
  140.4 52.9 %all-gather.8.cloned.1.call-done = bf16[1,1024,2816]{1,2,0:T(8,128)(2,1)} async-done(((bf16[1,1024,704]{1,2,0:T(8,128)(2,1)}), bf16[1,1024,2816]{1,2,0:T(8,128)(2,1)}) %all-gather.8.cloned.1.call-update) | async-done | bytes 5767184 | tf_op jit(solution)/shard_map/all_gather | solution.py:176
  193.3 10.5 %fusion.18 = f32[32,20,2816]{2,0,1:T(8,128)} fusion(bf16[1,1024,2816]{1,2,0:T(8,128)(2,1)} %all-gather.8.cloned.1.call-done, bf16[32,20,1024]{2,1,0:T(8,128)(2,1)} %all-to-all-done), kind=kOutput, calls=%fused_computation.30 | convolution fusion | flops 3690987520 | bytes 14286848 | tf_op jit(solution)/shard_map/sjcd,jdf->sjcf/dot_general | solution.py:180
  203.8 53.0 %all-gather.12.cloned.1.call-done = bf16[1,2816,1024]{2,1,0:T(8,128)(2,1)} async-done(((bf16[1,704,1024]{2,1,0:T(8,128)(2,1)}), bf16[1,2816,1024]{2,1,0:T(8,128)(2,1)}) %all-gather.12.cloned.1.call-update) | async-done | bytes 5767184 | tf_op jit(solution)/shard_map/all_gather | solution.py:178
  256.8 17.3 %fusion.36 = (bf16[32,20,2816]{2,0,1:T(8,128)(2,1)}, bf16[32,20,2816]{2,0,1:T(8,128)(2,1)}, bf16[32,20,2816]{2,0,1:T(8,128)(2,1)S(1)}) fusion(f32[32,20,2816]{2,0,1:T(8,128)} %fusion.18, f32[32,20,2816]{2,0,1:T(8,128)} %fusion.14, bf16[1,2816,1024]{2,1,0:T(8,128)(2,1)} %all-gather.12.cloned.1.call-done, bf16[32,20,1024]{2,1,0:T(8,128)(2,1)} %all-to-all-done.2), kind=kOutput, calls=%fused_computation.57 | convolution fusion | flops 3737845760 | bytes 32309248 | tf_op jit(solution)/shard_map/sjcd,jfd->sjcf/dot_general | solution.py:227
  279.9 7.8 all-to-all-start.1
  287.7 7.1 fusion.12
  294.8 6.5 fusion.56
  303.2 6.7 all-to-all-done.1
  309.9 6.3 all-to-all-start.3
  333.2 5.3 all-to-all-done.3
  353.5 6.0 copy.247
  376.4 10.2 %fusion.26 = bf16[1,1024,2816]{2,1,0:T(8,128)(2,1)} fusion(bf16[32,20,1024]{2,1,0:T(8,128)(2,1)} %all-to-all-done, bf16[32,20,2816]{2,0,1:T(8,128)(2,1)} %get-tuple-element.111), kind=kOutput, calls=%fused_computation.40 | convolution fusion | flops 3693871104 | bytes 10682368 | tf_op jit(solution)/shard_map/sjcd,sjcf->jdf/dot_general | solution.py:235
  386.6 26.6 %copy.251 = bf16[1,1024,2816]{1,0,2:T(2,128)(2,1)} copy(bf16[1,1024,2816]{2,1,0:T(8,128)(2,1)} %fusion.26) | data formatting | bytes 11534336
  413.1 9.1 %copy.280 = bf16[2816,1,1024]{2,0,1:T(8,128)(2,1)} copy(bf16[2816,1,1024]{2,1,0:T(2,128)(2,1)} %bitcast.300) | data formatting | bytes 11534336
  422.5 10.1 %fusion.25 = bf16[1,1024,2816]{2,1,0:T(8,128)(2,1)} fusion(bf16[32,20,1024]{2,1,0:T(8,128)(2,1)} %all-to-all-done, bf16[32,20,2816]{2,0,1:T(8,128)(2,1)} %get-tuple-element.110), kind=kOutput, calls=%fused_computation.39 | convolution fusion | flops 3693871104 | bytes 10682368 | tf_op jit(solution)/shard_map/sjcd,sjcf->jdf/dot_general | solution.py:232
  432.6 26.6 %copy.249 = bf16[1,1024,2816]{1,0,2:T(2,128)(2,1)} copy(bf16[1,1024,2816]{2,1,0:T(8,128)(2,1)} %fusion.25) | data formatting | bytes 11534336
  459.2 9.3 %copy.281 = bf16[2816,1,1024]{2,0,1:T(8,128)(2,1)} copy(bf16[2816,1,1024]{2,1,0:T(2,128)(2,1)} %bitcast.301) | data formatting | bytes 11534336
  468.6 9.8 %fusion.24 = bf16[1,2816,1024]{2,1,0:T(8,128)(2,1)} fusion(bf16[32,20,2816]{2,0,1:T(8,128)(2,1)} %copy-done.95, bf16[32,20,1024]{2,1,0:T(8,128)(2,1)} %all-to-all-done.2), kind=kOutput, calls=%fused_computation.38 | convolution fusion | flops 3693871104 | bytes 10682368 | tf_op jit(solution)/shard_map/sjcf,sjcd->jfd/dot_general | solution.py:229
  507.7 4.5 copy.230
  524.5 67.6 %all-reduce = (f32[1024]{0:T(1024)}, f32[32,16]{0,1:T(8,128)}, f32[1024]{0:T(1024)}, f32[4]{0:T(128)S(1)}) all-reduce(f32[1024]{0:T(1024)S(1)} %get-tuple-element.88, f32[32,16]{0,1:T(8,128)S(1)} %fusion.70, f32[1024]{0:T(1024)S(1)} %copy-done.76, f32[4]{0:T(128)S(1)} %pad_maximum_fusion.12), channel_id=1, replica_groups=mesh['row'=4,'col'=32] {'row','col'}, use_global_device_ids=true, to_apply=%region_29.30 | all-reduce | flops 2564 | bytes 20512 | tf_op jit(solution)/shard_map/psum | solution.py:323
  598.8 4.4 reshape_bitcast_fusion
  603.2 8.1 copy.252
  618.8 8.2 copy.250
  633.3 198.9 %all-reduce.4.cloned.1.call-done = (f32[1024,1024]{1,0:T(8,128)}, f32[1024,1024]{1,0:T(8,128)}, f32[1024,1024]{1,0:T(8,128)}, f32[1024,1024]{1,0:T(8,128)}, f32[1024,32]{0,1:T(8,128)}) async-done(((f32[1024,1024]{1,0:T(8,128)}, f32[1024,1024]{1,0:T(8,128)}, f32[1024,1024]{1,0:T(8,128)}, f32[1024,1024]{1,0:T(8,128)}, f32[1024,32]{0,1:T(8,128)}), (f32[1024,1024]{1,0:T(8,128)}, f32[1024,1024]{1,0:T(8,128)}, ...) | async-done | bytes 16908304 | tf_op jit(solution)/shard_map/psum | solution.py:323
  832.3 4.9 copy.291
  (345 shorter events, 186.0 us)
Async XLA Ops:
  7.2 36.9 %all-gather.16.cloned.1.call-start = ((), (), s32[]{:S(2)}) async-start(), calls=%async_computation.14 | async-start | bytes 1310720 | tf_op jit(solution)/shard_map/all_gather | solution.py:122
  9.2 13.4 %copy-start.61 = (f32[256]{0:T(256)}, f32[256]{0:T(256)S(1)}, u32[]{:S(2)}) copy-start(f32[256]{0:T(256)S(1)} %fusion.123) | copy-start | bytes 3076
  12.6 53.0 %all-gather.14.cloned.1.call-start = ((), (), s32[]{:S(2)}) async-start(), calls=%async_computation.13 | async-start | bytes 1310720 | tf_op jit(solution)/shard_map/all_gather | solution.py:123
  14.4 115.5 %all-gather.10.cloned.1.call-start = ((), (), s32[]{:S(2)}) async-start(), calls=%async_computation.10 | async-start | bytes 7208960 | tf_op jit(solution)/shard_map/all_gather | solution.py:177
  15.1 178.2 %all-gather.8.cloned.1.call-start = ((), (), s32[]{:S(2)}) async-start(), calls=%async_computation.9 | async-start | bytes 7208960 | tf_op jit(solution)/shard_map/all_gather | solution.py:176
  15.7 241.1 %all-gather.12.cloned.1.call-start = ((), (), s32[]{:S(2)}) async-start(), calls=%async_computation.11 | async-start | bytes 7208960 | tf_op jit(solution)/shard_map/all_gather | solution.py:178
  20.5 20.2 %copy-start.53 = (s32[128,128]{0,1:T(8,128)}, s32[128,128]{0,1:T(8,128)S(1)}, u32[]{:S(2)}) copy-start(s32[128,128]{0,1:T(8,128)S(1)} %copy.206) | copy-start | bytes 196612
  22.7 7.9 copy-start.40
  26.2 15.3 %copy-start.29 = (bf16[128,1024]{0,1:T(8,128)(2,1)}, bf16[128,1024]{0,1:T(8,128)(2,1)S(1)}, u32[]{:S(2)}) copy-start(bf16[128,1024]{0,1:T(8,128)(2,1)S(1)} %copy.204) | copy-start | bytes 786436
  27.4 14.0 %copy-start.31 = (bf16[128,1024]{0,1:T(8,128)(2,1)}, bf16[128,1024]{0,1:T(8,128)(2,1)S(1)}, u32[]{:S(2)}) copy-start(bf16[128,1024]{0,1:T(8,128)(2,1)S(1)} %copy.205) | copy-start | bytes 786436
  45.6 25.5 %copy-start.15 = (bf16[512,1024]{0,1:T(8,128)(2,1)}, bf16[512,1024]{0,1:T(8,128)(2,1)S(1)}, u32[]{:S(2)}) copy-start(bf16[512,1024]{0,1:T(8,128)(2,1)S(1)} %copy.200) | copy-start | bytes 3145732
  76.5 268.4 %copy-start.3 = (f32[256,1024]{1,0:T(8,128)}, f32[256,1024]{1,0:T(8,128)S(1)}, u32[]{:S(2)}) copy-start(f32[256,1024]{1,0:T(8,128)S(1)} %get-tuple-element.109) | copy-start | bytes 3145732
  76.5 268.4 %copy-start.63 = (f32[256]{0:T(256)}, f32[256]{0:T(256)S(1)}, u32[]{:S(2)}) copy-start(f32[256]{0:T(256)S(1)} %fusion.124) | copy-start | bytes 3076
  78.2 15.2 %copy-start.70 = (s32[256,2]{0,1:T(2,128)S(1)}, s32[256,2]{0,1:T(2,128)}, u32[]{:S(2)}) copy-start(s32[256,2]{0,1:T(2,128)} %param.22) | copy-start | bytes 6148
  81.5 31.2 %all-to-all-start = ((bf16[32,20,1024]{2,1,0:T(8,128)(2,1)}), bf16[32,20,1024]{2,1,0:T(8,128)(2,1)}, u32[]{:S(2)}, u32[]{:S(2)}) async-start(bf16[32,20,1024]{2,1,0:T(8,128)(2,1)} %reshape.614), calls=%async_computation | async-start | bytes 3145728 | tf_op jit(solution)/shard_map/all_to_all | solution.py:171
  92.7 10.1 %copy-start.71 = (f32[256]{0:T(256)}, f32[256]{0:T(256)S(1)}, u32[]{:S(2)}) copy-start(f32[256]{0:T(256)S(1)} %get-tuple-element.131) | copy-start | bytes 3076
  93.4 236.2 %copy-start.49 = (f32[256,32]{0,1:T(8,128)}, f32[256,32]{0,1:T(8,128)S(1)}, u32[]{:S(2)}) copy-start(f32[256,32]{0,1:T(8,128)S(1)} %fusion.119) | copy-start | bytes 98308
  94.0 8.8 %copy-start.74 = (f32[256]{0:T(256)S(1)}, f32[256]{0:T(256)}, u32[]{:S(2)}) copy-start(f32[256]{0:T(256)} %copy-done.73) | copy-start | bytes 3076
  112.7 91.2 %all-to-all-start.2 = ((bf16[32,20,1024]{2,1,0:T(8,128)(2,1)}), bf16[32,20,1024]{2,1,0:T(8,128)(2,1)}, u32[]{:S(2)}, u32[]{:S(2)}) async-start(bf16[32,20,1024]{2,1,0:T(8,128)(2,1)} %reshape.620), calls=%async_computation.2 | async-start | bytes 3145728 | tf_op jit(solution)/shard_map/all_to_all | solution.py:223
  256.8 17.3 %copy-start.93 = (bf16[1,2816,1024]{2,1,0:T(8,128)(2,1)S(1)}, bf16[1,2816,1024]{2,1,0:T(8,128)(2,1)}, u32[]{:S(2)}) copy-start(bf16[1,2816,1024]{2,1,0:T(8,128)(2,1)} %all-gather.12.cloned.1.call-done) | copy-start | bytes 17301508
  279.9 30.0 %all-to-all-start.1 = ((bf16[32,1,20,1024]{3,2,1,0:T(8,128)(2,1)}), bf16[32,1,20,1024]{3,2,1,0:T(8,128)(2,1)}, u32[]{:S(2)}, u32[]{:S(2)}) async-start(bf16[32,1,20,1024]{3,2,1,0:T(8,128)(2,1)} %copy.217), calls=%async_computation.1 | async-start | bytes 3145728 | tf_op jit(solution)/shard_map/all_to_all | solution.py:184
  309.9 28.6 %all-to-all-start.3 = ((bf16[32,1,20,1024]{3,2,1,0:T(8,128)(2,1)}), bf16[32,1,20,1024]{3,2,1,0:T(8,128)(2,1)}, u32[]{:S(2)}, u32[]{:S(2)}) async-start(bf16[32,1,20,1024]{3,2,1,0:T(8,128)(2,1)} %copy.224), calls=%async_computation.3 | async-start | bytes 3145728 | tf_op jit(solution)/shard_map/all_to_all | solution.py:251
  316.2 177.4 %reduce-scatter.18.cloned.1.call-start = ((), (), s32[]{:S(2)}) async-start(), calls=%async_computation.16 | async-start | bytes 1310720
  333.2 11.7 %copy-start.83 = (f32[256]{0:T(256)S(1)}, f32[256]{0:T(256)}, u32[]{:S(2)}) copy-start(f32[256]{0:T(256)} %copy-done.82) | copy-start | bytes 3076
  353.5 9.0 %copy-start.22 = (bf16[512,1024]{0,1:T(8,128)(2,1)S(1)}, bf16[512,1024]{0,1:T(8,128)(2,1)}, u32[]{:S(2)}) copy-start(bf16[512,1024]{0,1:T(8,128)(2,1)} %copy.198) | copy-start | bytes 3145732
  362.5 135.0 %reduce-scatter.16.cloned.1.call-start = ((), (), s32[]{:S(2)}) async-start(), calls=%async_computation.15 | async-start | bytes 1310720
  375.9 222.9 %reduce-scatter.22.cloned.1.call-start = ((), (), s32[]{:S(2)}) async-start(), calls=%async_computation.18 | async-start | bytes 7208960
  422.3 192.0 %reduce-scatter.20.cloned.1.call-start = ((), (), s32[]{:S(2)}) async-start(), calls=%async_computation.17 | async-start | bytes 7208960
  468.5 161.5 %reduce-scatter.14.cloned.1.call-start = ((), (), s32[]{:S(2)}) async-start(), calls=%async_computation.12 | async-start | bytes 7208960 | tf_op jit(solution)/shard_map/reduce_scatter | solution.py:247
  478.4 353.8 %all-reduce.4.cloned.1.call-start = ((), (), s32[]{:S(2)}) async-start(), calls=%async_computation.19 | async-start | bytes 33816576 | tf_op jit(solution)/shard_map/psum | solution.py:323
  512.2 8.3 copy-start.37
  522.6 73.4 %copy-start.78 = (f32[256]{0:T(256)S(1)}, f32[256]{0:T(256)}, u32[]{:S(2)}) copy-start(f32[256]{0:T(256)} %copy-done.77) | copy-start | bytes 3076
  (79 other events, 251.9 us)
Sparse Core Ops, SparseCore 0:
  12.8 26.2 all-gather.15
  41.3 24.2 all-gather.13
  67.3 62.5 all-gather.9
  131.4 61.8 all-gather.7
  194.9 61.8 all-gather.11
  362.6 19.7 reduce-scatter.17
  385.5 23.2 reduce-scatter.15
  422.4 57.3 reduce-scatter.21
  482.2 59.7 reduce-scatter.19
  544.2 60.7 reduce-scatter.13
  612.6 219.5 all-reduce.3
where the time goes:
time: 868 us; the launch traced here: 854 us
  waiting for transfers between devices  358 us (41%)
  local copies, waits for them, and re-layouts  194 us (22%)
  matrix products  156 us (18%)
  blocking collectives  67.6 us (8%)
  starting transfers between devices  31 us (4%)
  other arithmetic  27.9 us (3%)
  between operations  19.6 us (2%)
    psum x1, waiting for transfers between devices, per_device(): lax.psum((d_gain_a, d_w_query, d_w_key, d_w_value, d_w_out, d_bias, d_gai...  199 us
    unnamed x216, local copies, waits for them, and re-layouts  149 us
    psum x1, blocking collectives, per_device(): lax.psum((d_gain_a, d_w_query, d_w_key, d_w_value, d_w_out, d_bias, d_gai...  67.6 us
    all_gather x1, waiting for transfers between devices, per_device(): lax.all_gather(w_down, 'row', axis=1, tiled=True)  53 us
    all_gather x1, waiting for transfers between devices, per_device(): lax.all_gather(w_gate, 'row', axis=2, tiled=True)  52.9 us
    all_gather x1, waiting for transfers between devices, per_device(): lax.all_gather(values[:long_rows].reshape(UNITS, LONG_DEV, width), 'row',...  20 us
  transfers between devices with their start and end apart: 15, of which 8 were waited for; matrix products, arithmetic and copies ran while one was open for 36% of the time, Pallas kernels for 0%

commit v1 on v0

--- a/solution.py
+++ b/solution.py
@@ -1,6 +1,8 @@
 import jax
 import jax.numpy as jnp
 from jax import lax
+from jax.experimental import pallas as pl
+from jax.experimental.pallas import tpu as pltpu
 from jax.sharding import PartitionSpec as P
 
 HEADS = 16
@@ -80,6 +82,256 @@
         jnp.einsum("bhqk,bqhe->bkhe", d_scores, query, preferred_element_type=jnp.float32) * scale
     )
     return (d_query, d_keys, d_values, d_scores)
+
+
+MESH_ID = pl.DeviceIdType.MESH
+
+SUM_PARTS = (
+    (5120, 0, ("x", "y", "z"), 0),
+    (5120, 5120, ("y", "z", "x"), 0),
+    (6144, 10240, ("z", "x", "y"), 0),
+    (512, 0, ("y", "x", "z"), 1),
+)
+SUM_ROWS = (16384, 512)
+
+
+def torus_place():
+    row = lax.axis_index("row")
+    col = lax.axis_index("col")
+    core = lax.rem(col, 2)
+    x = lax.rem(lax.div(col, 2), 4)
+    z = lax.div(col, 8)
+    return row, z, x, core
+
+
+def axis_peer(axis, step):
+    row, z, x, core = torus_place()
+    if axis == "y":
+        row = lax.rem(row + step, 4)
+    elif axis == "x":
+        x = lax.rem(x + step, 4)
+    elif axis == "z":
+        z = lax.rem(z + step, 4)
+    else:
+        core = 1 - core
+    return (row, (z * 4 + x) * 2 + core)
+
+
+def sum_kernel(*refs):
+    inputs = refs[0:2]
+    results = refs[2:4]
+    held = refs[4:6]
+    other = refs[6:8]
+    slots = refs[8:8 + 3 * len(SUM_PARTS)]
+    load_sem, core_send, core_recv, hop_send, hop_recv, gather_send, gather_recv, copy_sem, last_send, last_recv = refs[
+        8 + 3 * len(SUM_PARTS):
+    ]
+    row, z, x, core = torus_place()
+    place = {"x": x, "y": row, "z": z}
+    barrier = pltpu.get_barrier_semaphore()
+    pl.semaphore_signal(barrier, inc=1, device_id=axis_peer("core", 1), device_id_type=MESH_ID)
+    for axis in ("x", "y", "z"):
+        for step in (1, 2, 3):
+            pl.semaphore_signal(barrier, inc=1, device_id=axis_peer(axis, step), device_id_type=MESH_ID)
+    loads = []
+    for p, (rows, first, order, kind) in enumerate(SUM_PARTS):
+        mine = pl.multiple_of(core * SUM_ROWS[kind] + first, 256)
+        load = pltpu.make_async_copy(
+            inputs[kind].at[pl.ds(mine, rows)], held[kind].at[pl.ds(first, rows)], load_sem.at[p]
+        )
+        load.start()
+        loads.append(load)
+    pl.semaphore_wait(barrier, 10)
+    swaps = []
+    for p, (rows, first, order, kind) in enumerate(SUM_PARTS):
+        yours = pl.multiple_of((1 - core) * SUM_ROWS[kind] + first, 256)
+        swap = pltpu.make_async_remote_copy(
+            inputs[kind].at[pl.ds(yours, rows)],
+            other[kind].at[pl.ds(first, rows)],
+            core_send.at[p],
+            core_recv.at[p],
+            device_id=axis_peer("core", 1),
+            device_id_type=MESH_ID,
+        )
+        swap.start()
+        swaps.append(swap)
+
+    def add_rows(kind, start, rows, terms):
+        if kind == 1:
+            tile = min(rows, 128)
+        else:
+            tile = 80 if rows % 80 == 0 else 96
+            tile = tile * 4 if rows % (tile * 4) == 0 else tile
+
+        def body(i, carry):
+            offset = pl.multiple_of(i * tile, 8 if kind == 1 else 16)
+            here = pl.ds(pl.multiple_of(start + offset, 8 if kind == 1 else 16), tile)
+            total = held[kind][here, :].astype(jnp.float32)
+            for ref, base in terms:
+                total = total + ref[pl.ds(pl.multiple_of(base + offset, 8 if kind == 1 else 16), tile), :].astype(jnp.float32)
+            held[kind][here, :] = total.astype(held[kind].dtype)
+            return carry
+
+        lax.fori_loop(0, rows // tile, body, 0)
+
+    def start_hop(p, level):
+        rows, first, order, kind = SUM_PARTS[p]
+        size = rows // 4 ** (level + 1)
+        base = first
+        for done in range(level):
+            base = base + place[order[done]] * (rows // 4 ** (done + 1))
+        axis = order[level]
+        hops = []
+        for step in (1, 2, 3):
+            block = lax.rem(place[axis] + step, 4)
+            hop = pltpu.make_async_remote_copy(
+                held[kind].at[pl.ds(pl.multiple_of(base + block * size, 8 if kind == 1 else 16), size)],
+                slots[p * 3 + level].at[pl.ds((step - 1) * size, size)],
+                hop_send.at[p, level, step - 1],
+                hop_recv.at[p, level, step - 1],
+                device_id=axis_peer(axis, step),
+                device_id_type=MESH_ID,
+            )
+            hop.start()
+            hops.append(hop)
+        return hops
+
+    def end_hop(p, level, hops):
+        rows, first, order, kind = SUM_PARTS[p]
+        size = rows // 4 ** (level + 1)
+        base = first
+        for done in range(level + 1):
+            base = base + place[order[done]] * (rows // 4 ** (done + 1))
+        for hop in hops:
+            hop.wait()
+        add_rows(kind, base, size, [(slots[p * 3 + level], step * size) for step in range(3)])
+
+    count = len(SUM_PARTS)
+    flight = [None] * count
+    for p in range(count):
+        rows, first, order, kind = SUM_PARTS[p]
+        loads[p].wait()
+        swaps[p].wait()
+        add_rows(kind, first, rows, [(other[kind], first)])
+        flight[p] = start_hop(p, 0)
+    for level in (1, 2):
+        for p in range(count):
+            end_hop(p, level - 1, flight[p])
+            flight[p] = start_hop(p, level)
+
+    def place_of(p, levels):
+        rows, first, order, kind = SUM_PARTS[p]
+        base = first
+        for done in range(levels):
+            base = base + place[order[done]] * (rows // 4 ** (done + 1))
+        return base
+
+    def gather(p, level):
+        rows, first, order, kind = SUM_PARTS[p]
+        size = rows // 4 ** (level + 1)
+        align = 8 if kind == 1 else 16
+        here = pl.multiple_of(place_of(p, level + 1), align)
+        there = pl.multiple_of(place_of(p, level + 1) + core * SUM_ROWS[kind], align)
+        source = held[kind].at[pl.ds(here, size)] if level == 2 else results[kind].at[pl.ds(there, size)]
+        moves = []
+        for step in (1, 2, 3):
+            move = pltpu.make_async_remote_copy(
+                source,
+                results[kind].at[pl.ds(there, size)],
+                gather_send.at[p, level, step - 1],
+                gather_recv.at[p, level, step - 1],
+                device_id=axis_peer(order[level], step),
+                device_id_type=MESH_ID,
+            )
+            move.start()
+            moves.append(move)
+        if level == 2:
+            keep = pltpu.make_async_copy(source, results[kind].at[pl.ds(there, size)], copy_sem.at[p])
+            keep.start()
+            keep.wait()
+        return moves
+
+    for p in range(count):
+        end_hop(p, 2, flight[p])
+        flight[p] = gather(p, 2)
+    for level in (1, 0):
+        for p in range(count):
+            for move in flight[p]:
+                move.wait()
+            flight[p] = gather(p, level)
+    lasts = []
+    for p in range(count):
+        rows, first, order, kind = SUM_PARTS[p]
+        size = rows // 4
+        for index in range(4):
+            if index > 0:
+                flight[p][index - 1].wait()
+            block = lax.rem(place[order[0]] + 4 - index, 4)
+            there = pl.ds(pl.multiple_of(first + block * size + core * SUM_ROWS[kind], 8 if kind == 1 else 16), size)
+            last = pltpu.make_async_remote_copy(
+                results[kind].at[there],
+                results[kind].at[there],
+                last_send.at[p, index],
+                last_recv.at[p, index],
+                device_id=axis_peer("core", 1),
+                device_id_type=MESH_ID,
+            )
+            last.start()
+            lasts.append(last)
+    for last in lasts:
+        last.wait()
+
+
+def sum_over_devices(weights, small):
+    scratch = [
+        pltpu.VMEM((SUM_ROWS[0], 128), jnp.bfloat16),
+        pltpu.VMEM((SUM_ROWS[1], 128), jnp.float32),
+        pltpu.VMEM((SUM_ROWS[0], 128), jnp.bfloat16),
+        pltpu.VMEM((SUM_ROWS[1], 128), jnp.float32),
+    ]
+    for rows, first, order, kind in SUM_PARTS:
+        for level in range(3):
+            scratch.append(
+                pltpu.VMEM((3 * rows // 4 ** (level + 1), 128), jnp.float32 if kind == 1 else jnp.bfloat16)
+            )
+    count = len(SUM_PARTS)
+    dma = pltpu.SemaphoreType.DMA
+    scratch += [
+        dma((count,)),
+        dma((count,)),
+        dma((count,)),
+        dma((count, 3, 3)),
+        dma((count, 3, 3)),
+        dma((count, 3, 3)),
+        dma((count, 3, 3)),
+        dma((count,)),
+        dma((count, 4)),
+        dma((count, 4)),
+    ]
+    return pl.pallas_call(
+        sum_kernel,
+        out_shape=(
+            jax.ShapeDtypeStruct((2 * SUM_ROWS[0], 128), jnp.bfloat16),
+            jax.ShapeDtypeStruct((2 * SUM_ROWS[1], 128), jnp.float32),
+        ),
+        in_specs=[pl.BlockSpec(memory_space=pl.ANY)] * 2,
+        out_specs=[pl.BlockSpec(memory_space=pl.ANY)] * 2,
+        scratch_shapes=scratch,
+        compiler_params=pltpu.CompilerParams(
+            collective_id=4, has_side_effects=True, vmem_limit_bytes=48 * 1024 * 1024
+        ),
+        name="sum_over_devices",
+    )(weights, small)
+
+
+def pack_small(parts):
+    rows = []
+    for part in parts:
+        flat = part.reshape(-1)
+        pad = -flat.shape[0] % 1024
+        rows.append(jnp.pad(flat, (0, pad)).reshape(-1, 128))
+    packed = jnp.concatenate(rows, axis=0)
+    return jnp.pad(packed, ((0, 2 * SUM_ROWS[1] - packed.shape[0]), (0, 0)))
 
 
 def per_device(
@@ -320,9 +572,22 @@
     )
     d_inputs_norm, d_gain_a = norm_a_back(d_normed_a)
     d_inputs = d_resid + d_inputs_norm
-    summed = lax.psum(
-        (d_gain_a, d_w_query, d_w_key, d_w_value, d_w_out, d_bias, d_gain_m, d_router, tallies),
-        ("row", "col"),
+    grads = jnp.stack([d_w_query, d_w_key, d_w_value, d_w_out]).astype(jnp.bfloat16)
+    grads = grads.reshape(4, width, 8, 128).transpose(0, 2, 1, 3).reshape(-1, 128)
+    small = pack_small([jnp.transpose(d_router), d_gain_a, d_gain_m, d_bias, tallies])
+    grads, small = sum_over_devices(grads, small)
+    grads = grads.reshape(4, 8, width, 128).transpose(0, 2, 1, 3).reshape(4, width, width)
+    grads = grads.astype(jnp.float32)
+    summed = (
+        small[256:264].reshape(-1),
+        grads[0],
+        grads[1],
+        grads[2],
+        grads[3],
+        small[272:276].reshape(buckets_count, HEADS),
+        small[264:272].reshape(-1),
+        jnp.transpose(small[0:256].reshape(experts, width)),
+        small[280],
     )
     totals = summed[8]
     statistics = jnp.stack(

time: 868 us -> 752 us (0.87)
  waiting for transfers between devices: 358 us -> 159 us
  Pallas kernels: 0 us -> 100 us
  blocking collectives: 67.6 us -> 0 us
  local copies, waits for them, and re-layouts: 194 us -> 225 us
  other arithmetic: 27.9 us -> 41.5 us
    psum x1 -> x0, waiting for transfers between devices: 199 us -> none  [per_device(): lax.psum((d_gain_a, d_w_query, d_w_key, d_w_value, d_w_out, d_bias, d_gai...]
    pallas_call x0 -> x1, Pallas kernels: none -> 100 us  [sum_over_devices(): pl.pallas_call(sum_kernel, out_shape=(jax.ShapeDtypeStruct((2 * SUM_ROWS[...]
    psum x1 -> x0, blocking collectives: 67.6 us -> none  [per_device(): lax.psum((d_gain_a, d_w_query, d_w_key, d_w_value, d_w_out, d_bias, d_gai...]
    slice x1 -> x8, local copies, waits for them, and re-layouts: 0.22 us -> 16.9 us  [the longest x2 9.14 us: per_device(): grads[3]]
    another operation x1 -> x5, local copies, waits for them, and re-layouts: 0.01 us -> 15.9 us  [the longest x4 15.9 us: per_device(): jnp.stack([d_w_query, d_w_key, d_w_value, d_w_out]).astype(jnp.bfloat16)]
    convert_element_type x0 -> x1, other arithmetic: none -> 11.1 us  [per_device(): grads = grads.astype(jnp.float32)]
    unnamed x216 -> x224, local copies, waits for them, and re-layouts: 149 us -> 145 us
  transfers between devices with their start and end apart: 15 -> 14, of which waited for: 8 -> 7; matrix products, arithmetic and copies ran while one was open for 36% -> 50% of each run, Pallas kernels for 0% -> 14%
where the time goes in v1:
time: 752 us; the launch traced here: 738 us
  local copies, waits for them, and re-layouts  225 us (30%)
  matrix products  162 us (22%)
  waiting for transfers between devices  159 us (21%)
  Pallas kernels  100 us (13%)
  other arithmetic  41.5 us (6%)
  starting transfers between devices  30.5 us (4%)
  between operations  20.1 us (3%)
    unnamed x224, local copies, waits for them, and re-layouts  145 us
    pallas_call x1, Pallas kernels, sum_over_devices(): pl.pallas_call(sum_kernel, out_shape=(jax.ShapeDtypeStruct((2 * SUM_ROWS[...  100 us
    all_gather x1, waiting for transfers between devices, per_device(): lax.all_gather(w_down, 'row', axis=1, tiled=True)  53 us
    all_gather x1, waiting for transfers between devices, per_device(): lax.all_gather(w_gate, 'row', axis=2, tiled=True)  52.9 us
    all_gather x1, waiting for transfers between devices, per_device(): lax.all_gather(values[:long_rows].reshape(UNITS, LONG_DEV, width), 'row',...  20 us
    dot_general x1, matrix products, per_device(): jnp.einsum('sjcd,jfd->sjcf', d_received, down_full, preferred_element_typ...  17.5 us
    another operation x4, local copies, waits for them, and re-layouts, per_device(): jnp.stack([d_w_query, d_w_key, d_w_value, d_w_out]).astype(jnp.bfloat16)  15.9 us
  transfers between devices with their start and end apart: 14, of which 7 were waited for; matrix products, arithmetic and copies ran while one was open for 50% of the time, Pallas kernels for 14%

profile of v1, /device:TPU:1, one launch (start us, length us, event | category | flops | bytes accessed | tf_op | source)
XLA Modules:
  0.0 738.2 jit_solution(7364834465141169799)
XLA Ops:
  34.0 5.2 copy.241
  45.1 20.0 %all-gather.14.cloned.1.call-done = bf16[512,1024]{1,0:T(8,128)(2,1)} async-done(((bf16[128,1024]{1,0:T(8,128)(2,1)}), bf16[512,1024]{1,0:T(8,128)(2,1)}) %all-gather.14.cloned.1.call-update) | async-done | bytes 1048592 | tf_op jit(solution)/shard_map/all_gather | solution.py:375
  80.8 9.0 %all-to-all-start = ((bf16[32,20,1024]{2,1,0:T(8,128)(2,1)}), bf16[32,20,1024]{2,1,0:T(8,128)(2,1)}, u32[]{:S(2)}, u32[]{:S(2)}) async-start(bf16[32,20,1024]{2,1,0:T(8,128)(2,1)} %reshape.685), calls=%async_computation | async-start | bytes 3145728 | tf_op jit(solution)/shard_map/all_to_all | solution.py:423
  103.2 8.6 %all-to-all-done = bf16[32,20,1024]{2,1,0:T(8,128)(2,1)} async-done(((bf16[32,20,1024]{2,1,0:T(8,128)(2,1)}), bf16[32,20,1024]{2,1,0:T(8,128)(2,1)}, u32[]{:S(2)}, u32[]{:S(2)}) %all-to-all-start) | async-done | bytes 1310752 | tf_op jit(solution)/shard_map/all_to_all | solution.py:423
  111.8 6.4 all-to-all-start.2
  118.2 11.1 %all-gather.10.cloned.1.call-done = bf16[1,1024,2816]{1,2,0:T(8,128)(2,1)} async-done(((bf16[1,1024,704]{1,2,0:T(8,128)(2,1)}), bf16[1,1024,2816]{1,2,0:T(8,128)(2,1)}) %all-gather.10.cloned.1.call-update) | async-done | bytes 5767184 | tf_op jit(solution)/shard_map/all_gather | solution.py:429
  129.3 10.6 %fusion.14 = f32[32,20,2816]{2,0,1:T(8,128)} fusion(bf16[1,1024,2816]{1,2,0:T(8,128)(2,1)} %all-gather.10.cloned.1.call-done, bf16[32,20,1024]{2,1,0:T(8,128)(2,1)} %all-to-all-done), kind=kOutput, calls=%fused_computation.28 | convolution fusion | flops 3690987520 | bytes 14286848 | tf_op jit(solution)/shard_map/sjcd,jdf->sjcf/dot_general | solution.py:433
  139.9 52.9 %all-gather.8.cloned.1.call-done = bf16[1,1024,2816]{1,2,0:T(8,128)(2,1)} async-done(((bf16[1,1024,704]{1,2,0:T(8,128)(2,1)}), bf16[1,1024,2816]{1,2,0:T(8,128)(2,1)}) %all-gather.8.cloned.1.call-update) | async-done | bytes 5767184 | tf_op jit(solution)/shard_map/all_gather | solution.py:428
  192.8 10.5 %fusion.18 = f32[32,20,2816]{2,0,1:T(8,128)} fusion(bf16[1,1024,2816]{1,2,0:T(8,128)(2,1)} %all-gather.8.cloned.1.call-done, bf16[32,20,1024]{2,1,0:T(8,128)(2,1)} %all-to-all-done), kind=kOutput, calls=%fused_computation.32 | convolution fusion | flops 3690987520 | bytes 14286848 | tf_op jit(solution)/shard_map/sjcd,jdf->sjcf/dot_general | solution.py:432
  203.3 53.0 %all-gather.12.cloned.1.call-done = bf16[1,2816,1024]{2,1,0:T(8,128)(2,1)} async-done(((bf16[1,704,1024]{2,1,0:T(8,128)(2,1)}), bf16[1,2816,1024]{2,1,0:T(8,128)(2,1)}) %all-gather.12.cloned.1.call-update) | async-done | bytes 5767184 | tf_op jit(solution)/shard_map/all_gather | solution.py:430
  256.2 17.5 %fusion.36 = (bf16[32,20,2816]{2,0,1:T(8,128)(2,1)}, bf16[32,20,2816]{2,0,1:T(8,128)(2,1)}, bf16[32,20,2816]{2,0,1:T(8,128)(2,1)S(1)}) fusion(f32[32,20,2816]{2,0,1:T(8,128)} %fusion.18, f32[32,20,2816]{2,0,1:T(8,128)} %fusion.14, bf16[1,2816,1024]{2,1,0:T(8,128)(2,1)} %all-gather.12.cloned.1.call-done, bf16[32,20,1024]{2,1,0:T(8,128)(2,1)} %all-to-all-done.2), kind=kOutput, calls=%fused_computation.63 | convolution fusion | flops 3737845760 | bytes 32309248 | tf_op jit(solution)/shard_map/sjcd,jfd->sjcf/dot_general | solution.py:479
  279.6 7.8 %all-to-all-start.1 = ((bf16[32,1,20,1024]{3,2,1,0:T(8,128)(2,1)}), bf16[32,1,20,1024]{3,2,1,0:T(8,128)(2,1)}, u32[]{:S(2)}, u32[]{:S(2)}) async-start(bf16[32,1,20,1024]{3,2,1,0:T(8,128)(2,1)} %copy.256), calls=%async_computation.1 | async-start | bytes 3145728 | tf_op jit(solution)/shard_map/all_to_all | solution.py:436
  287.4 7.1 fusion.12
  294.5 6.5 fusion.56
  302.9 6.7 all-to-all-done.1
  309.6 6.3 all-to-all-start.3
  332.8 5.3 all-to-all-done.3
  353.2 6.0 copy.296
  375.9 10.1 %fusion.26 = bf16[1,1024,2816]{2,1,0:T(8,128)(2,1)} fusion(bf16[32,20,1024]{2,1,0:T(8,128)(2,1)} %all-to-all-done, bf16[32,20,2816]{2,0,1:T(8,128)(2,1)} %get-tuple-element.110), kind=kOutput, calls=%fused_computation.42 | convolution fusion | flops 3693871104 | bytes 10682368 | tf_op jit(solution)/shard_map/sjcd,sjcf->jdf/dot_general | solution.py:487
  386.1 26.5 %copy.300 = bf16[1,1024,2816]{1,0,2:T(2,128)(2,1)} copy(bf16[1,1024,2816]{2,1,0:T(8,128)(2,1)} %fusion.26) | data formatting | bytes 11534336
  412.6 9.2 %copy.337 = bf16[2816,1,1024]{2,0,1:T(8,128)(2,1)} copy(bf16[2816,1,1024]{2,1,0:T(2,128)(2,1)} %bitcast.349) | data formatting | bytes 11534336
  422.3 10.1 %fusion.25 = bf16[1,1024,2816]{2,1,0:T(8,128)(2,1)} fusion(bf16[32,20,1024]{2,1,0:T(8,128)(2,1)} %all-to-all-done, bf16[32,20,2816]{2,0,1:T(8,128)(2,1)} %get-tuple-element.109), kind=kOutput, calls=%fused_computation.41 | convolution fusion | flops 3693871104 | bytes 10682368 | tf_op jit(solution)/shard_map/sjcd,sjcf->jdf/dot_general | solution.py:484
  432.4 26.6 %copy.298 = bf16[1,1024,2816]{1,0,2:T(2,128)(2,1)} copy(bf16[1,1024,2816]{2,1,0:T(8,128)(2,1)} %fusion.25) | data formatting | bytes 11534336
  458.9 9.2 %copy.338 = bf16[2816,1,1024]{2,0,1:T(8,128)(2,1)} copy(bf16[2816,1,1024]{2,1,0:T(2,128)(2,1)} %bitcast.350) | data formatting | bytes 11534336
  468.2 9.8 %fusion.24 = bf16[1,2816,1024]{2,1,0:T(8,128)(2,1)} fusion(bf16[32,20,2816]{2,0,1:T(8,128)(2,1)} %copy-done.97, bf16[32,20,1024]{2,1,0:T(8,128)(2,1)} %all-to-all-done.2), kind=kOutput, calls=%fused_computation.40 | convolution fusion | flops 3693871104 | bytes 10682368 | tf_op jit(solution)/shard_map/sjcf,sjcd->jfd/dot_general | solution.py:481
  478.8 4.7 copy.273
  548.9 100.3 %sum_over_devices.1 = (bf16[32768,128]{1,0:T(8,128)(2,1)}, f32[1024,128]{1,0:T(8,128)S(1)}) custom-call(bf16[32768,128]{1,0:T(8,128)(2,1)} %bitcast.351, f32[1024,128]{1,0:T(8,128)S(1)} %pad.14.refs_1_), custom_call_target="tpu_custom_call" | custom-call | tf_op jit(solution)/shard_map/sum_over_devices/pallas_call | solution.py:311
  654.0 11.1 %convert_bitcast_fusion = f32[4,1024,8,128]{3,1,2,0:T(8,128)} fusion(bf16[4,8,1024,128]{3,2,1,0:T(8,128)(2,1)} %bitcast.360), kind=kLoop, calls=%fused_computation | loop fusion | flops 4194304 | bytes 25165824 | tf_op jit(solution)/shard_map/convert_element_type | solution.py:580
  665.2 6.7 fusion.137
  696.5 4.4 reshape_bitcast_fusion
  700.9 8.1 %copy.301 = bf16[1,1024,704]{2,1,0:T(8,128)(2,1)} copy(bf16[1,1024,704]{1,0,2:T(2,128)(2,1)} %reshape_bitcast_fusion) | data formatting | bytes 2883584
  716.5 8.2 %copy.299 = bf16[1,1024,704]{2,1,0:T(8,128)(2,1)} copy(bf16[1,1024,704]{1,0,2:T(2,128)(2,1)} %reshape_bitcast_fusion.1) | data formatting | bytes 2883584
  (370 shorter events, 222.4 us)
Async XLA Ops:
  7.2 36.3 %all-gather.16.cloned.1.call-start = ((), (), s32[]{:S(2)}) async-start(), calls=%async_computation.14 | async-start | bytes 1310720 | tf_op jit(solution)/shard_map/all_gather | solution.py:374
  8.7 13.4 %copy-start.68 = (f32[256]{0:T(256)}, f32[256]{0:T(256)S(1)}, u32[]{:S(2)}) copy-start(f32[256]{0:T(256)S(1)} %fusion.120) | copy-start | bytes 3076
  12.1 53.0 %all-gather.14.cloned.1.call-start = ((), (), s32[]{:S(2)}) async-start(), calls=%async_computation.13 | async-start | bytes 1310720 | tf_op jit(solution)/shard_map/all_gather | solution.py:375
  13.8 115.5 %all-gather.10.cloned.1.call-start = ((), (), s32[]{:S(2)}) async-start(), calls=%async_computation.10 | async-start | bytes 7208960 | tf_op jit(solution)/shard_map/all_gather | solution.py:429
  14.5 178.2 %all-gather.8.cloned.1.call-start = ((), (), s32[]{:S(2)}) async-start(), calls=%async_computation.9 | async-start | bytes 7208960 | tf_op jit(solution)/shard_map/all_gather | solution.py:428
  15.1 241.1 %all-gather.12.cloned.1.call-start = ((), (), s32[]{:S(2)}) async-start(), calls=%async_computation.11 | async-start | bytes 7208960 | tf_op jit(solution)/shard_map/all_gather | solution.py:430
  19.9 20.2 %copy-start.47 = (s32[128,128]{0,1:T(8,128)}, s32[128,128]{0,1:T(8,128)S(1)}, u32[]{:S(2)}) copy-start(s32[128,128]{0,1:T(8,128)S(1)} %copy.245) | copy-start | bytes 196612
  22.1 7.9 %copy-start.36 = (s32[128,512]{0,1:T(8,128)}, s32[128,512]{0,1:T(8,128)S(1)}, u32[]{:S(2)}) copy-start(s32[128,512]{0,1:T(8,128)S(1)} %copy.240) | copy-start | bytes 786436
  22.1 7.9 %copy-start.61 = (f32[32,16]{0,1:T(8,128)S(1)}, f32[32,16]{0,1:T(8,128)}, u32[]{:S(2)}) copy-start(f32[32,16]{0,1:T(8,128)} %param.28) | copy-start | bytes 6148
  25.7 15.2 %copy-start.28 = (bf16[128,1024]{0,1:T(8,128)(2,1)}, bf16[128,1024]{0,1:T(8,128)(2,1)S(1)}, u32[]{:S(2)}) copy-start(bf16[128,1024]{0,1:T(8,128)(2,1)S(1)} %copy.243) | copy-start | bytes 786436
  26.9 14.0 %copy-start.29 = (bf16[128,1024]{0,1:T(8,128)(2,1)}, bf16[128,1024]{0,1:T(8,128)(2,1)S(1)}, u32[]{:S(2)}) copy-start(bf16[128,1024]{0,1:T(8,128)(2,1)S(1)} %copy.244) | copy-start | bytes 786436
  45.0 25.5 %copy-start.14 = (bf16[512,1024]{0,1:T(8,128)(2,1)}, bf16[512,1024]{0,1:T(8,128)(2,1)S(1)}, u32[]{:S(2)}) copy-start(bf16[512,1024]{0,1:T(8,128)(2,1)S(1)} %copy.239) | copy-start | bytes 3145732
  75.9 268.7 %copy-start.3 = (f32[256,1024]{1,0:T(8,128)}, f32[256,1024]{1,0:T(8,128)S(1)}, u32[]{:S(2)}) copy-start(f32[256,1024]{1,0:T(8,128)S(1)} %get-tuple-element.104) | copy-start | bytes 3145732
  75.9 268.7 %copy-start.59 = (f32[256]{0:T(256)}, f32[256]{0:T(256)S(1)}, u32[]{:S(2)}) copy-start(f32[256]{0:T(256)S(1)} %fusion.121) | copy-start | bytes 3076
  77.5 14.9 %copy-start.66 = (s32[256,2]{0,1:T(2,128)S(1)}, s32[256,2]{0,1:T(2,128)}, u32[]{:S(2)}) copy-start(s32[256,2]{0,1:T(2,128)} %param.22) | copy-start | bytes 6148
  80.8 30.9 %all-to-all-start = ((bf16[32,20,1024]{2,1,0:T(8,128)(2,1)}), bf16[32,20,1024]{2,1,0:T(8,128)(2,1)}, u32[]{:S(2)}, u32[]{:S(2)}) async-start(bf16[32,20,1024]{2,1,0:T(8,128)(2,1)} %reshape.685), calls=%async_computation | async-start | bytes 3145728 | tf_op jit(solution)/shard_map/all_to_all | solution.py:423
  91.8 10.0 %copy-start.67 = (f32[256]{0:T(256)}, f32[256]{0:T(256)S(1)}, u32[]{:S(2)}) copy-start(f32[256]{0:T(256)S(1)} %get-tuple-element.132) | copy-start | bytes 3076
  92.5 236.8 %copy-start.43 = (f32[256,32]{0,1:T(8,128)}, f32[256,32]{0,1:T(8,128)S(1)}, u32[]{:S(2)}) copy-start(f32[256,32]{0,1:T(8,128)S(1)} %fusion.115) | copy-start | bytes 98308
  93.1 8.7 %copy-start.74 = (f32[256]{0:T(256)S(1)}, f32[256]{0:T(256)}, u32[]{:S(2)}) copy-start(f32[256]{0:T(256)} %copy-done.73) | copy-start | bytes 3076
  111.8 91.5 %all-to-all-start.2 = ((bf16[32,20,1024]{2,1,0:T(8,128)(2,1)}), bf16[32,20,1024]{2,1,0:T(8,128)(2,1)}, u32[]{:S(2)}, u32[]{:S(2)}) async-start(bf16[32,20,1024]{2,1,0:T(8,128)(2,1)} %reshape.691), calls=%async_computation.2 | async-start | bytes 3145728 | tf_op jit(solution)/shard_map/all_to_all | solution.py:475
  256.2 17.6 %copy-start.95 = (bf16[1,2816,1024]{2,1,0:T(8,128)(2,1)S(1)}, bf16[1,2816,1024]{2,1,0:T(8,128)(2,1)}, u32[]{:S(2)}) copy-start(bf16[1,2816,1024]{2,1,0:T(8,128)(2,1)} %all-gather.12.cloned.1.call-done) | copy-start | bytes 17301508
  279.6 30.0 %all-to-all-start.1 = ((bf16[32,1,20,1024]{3,2,1,0:T(8,128)(2,1)}), bf16[32,1,20,1024]{3,2,1,0:T(8,128)(2,1)}, u32[]{:S(2)}, u32[]{:S(2)}) async-start(bf16[32,1,20,1024]{3,2,1,0:T(8,128)(2,1)} %copy.256), calls=%async_computation.1 | async-start | bytes 3145728 | tf_op jit(solution)/shard_map/all_to_all | solution.py:436
  309.6 28.6 %all-to-all-start.3 = ((bf16[32,1,20,1024]{3,2,1,0:T(8,128)(2,1)}), bf16[32,1,20,1024]{3,2,1,0:T(8,128)(2,1)}, u32[]{:S(2)}, u32[]{:S(2)}) async-start(bf16[32,1,20,1024]{3,2,1,0:T(8,128)(2,1)} %copy.263), calls=%async_computation.3 | async-start | bytes 3145728 | tf_op jit(solution)/shard_map/all_to_all | solution.py:503
  315.9 202.0 %reduce-scatter.18.cloned.1.call-start = ((), (), s32[]{:S(2)}) async-start(), calls=%async_computation.16 | async-start | bytes 1310720
  332.8 11.7 %copy-start.83 = (f32[256]{0:T(256)S(1)}, f32[256]{0:T(256)}, u32[]{:S(2)}) copy-start(f32[256]{0:T(256)} %copy-done.82) | copy-start | bytes 3076
  353.2 9.1 %copy-start.23 = (bf16[512,1024]{0,1:T(8,128)(2,1)S(1)}, bf16[512,1024]{0,1:T(8,128)(2,1)}, u32[]{:S(2)}) copy-start(bf16[512,1024]{0,1:T(8,128)(2,1)} %copy.237) | copy-start | bytes 3145732
  362.2 164.4 %reduce-scatter.16.cloned.1.call-start = ((), (), s32[]{:S(2)}) async-start(), calls=%async_computation.15 | async-start | bytes 1310720
  375.7 320.8 %reduce-scatter.22.cloned.1.call-start = ((), (), s32[]{:S(2)}) async-start(), calls=%async_computation.18 | async-start | bytes 7208960
  421.8 290.2 %reduce-scatter.20.cloned.1.call-start = ((), (), s32[]{:S(2)}) async-start(), calls=%async_computation.17 | async-start | bytes 7208960
  468.2 259.4 %reduce-scatter.14.cloned.1.call-start = ((), (), s32[]{:S(2)}) async-start(), calls=%async_computation.12 | async-start | bytes 7208960 | tf_op jit(solution)/shard_map/reduce_scatter | solution.py:499
  478.8 16.6 %copy-start.49 = (f32[16,128]{1,0:T(8,128)}, f32[16,128]{1,0:T(8,128)S(1)}, u32[]{:S(2)}) copy-start(f32[16,128]{1,0:T(8,128)S(1)} %log_add_fusion) | copy-start | bytes 24580
  536.8 8.0 %copy-start.20 = (bf16[1,1024,8,128]{3,1,2,0:T(8,128)(2,1)S(1)}, bf16[1,1024,8,128]{3,1,2,0:T(8,128)(2,1)}, u32[]{:S(2)}) copy-start(bf16[1,1024,8,128]{3,1,2,0:T(8,128)(2,1)} %copy.270) | copy-start | bytes 6291460
  (80 other events, 299.6 us)
Sparse Core Ops, SparseCore 0:
  12.2 26.2 all-gather.15
  40.7 24.2 all-gather.13
  66.7 62.5 all-gather.9
  130.8 61.8 all-gather.7
  194.3 61.8 all-gather.11
  362.3 19.0 reduce-scatter.17
  384.0 23.5 reduce-scatter.15
  421.9 57.3 reduce-scatter.21
  481.7 59.3 reduce-scatter.19
  543.4 94.2 reduce-scatter.13

commit v2 on v1

v2 whole, which is shorter than its diff:
```python
import functools

import numpy as np
import jax
import jax.numpy as jnp
from jax import lax
from jax.experimental import pallas as pl
from jax.experimental.pallas import tpu as pltpu
from jax.sharding import PartitionSpec as P

HEADS = 16
HEAD_DIM = 64
WIDTH = 1024
ROWS = 256
LONG = 128
EXPERTS = 32
SLOTS = 20
FOLDED = 80
QUARTER = 256
PIECES = EXPERTS * FOLDED
TABLE = 640
SHARD = 704
HALF = 2 * SHARD

bucket_edges = (1, 2, 3, 4, 5, 6, 7, 8, 12, 16, 23, 32, 46, 64, 91)
norm_eps = 1e-06
balance_coef = 0.01
zloss_coef = 0.001
masked_score = -1e30
highest = lax.Precision.HIGHEST
MESH_ID = pl.DeviceIdType.MESH
F32 = jnp.float32
BF16 = jnp.bfloat16
VMEM_SPEC = pl.BlockSpec(memory_space=pltpu.VMEM)
HBM_SPEC = pl.BlockSpec(memory_space=pl.ANY)
SMEM_SPEC = pl.BlockSpec(memory_space=pltpu.SMEM)
DMA = pltpu.SemaphoreType.DMA


def piece_ids():
    row = np.arange(PIECES)
    slot = (row // FOLDED) * SLOTS + row % SLOTS
    quarter = (row % FOLDED) // SLOTS
    return np.stack([slot, quarter]).astype(np.float32)


def unfold_matrix():
    out = np.arange(320)
    quarter, message, slot = out // 80, (out % 80) // SLOTS, out % SLOTS
    hot = np.zeros((320, 320), np.float32)
    hot[out, message * FOLDED + quarter * SLOTS + slot] = 1
    return hot


def nt(left, right, precision=None):
    return lax.dot_general(
        left, right, (((1,), (1,)), ((), ())), preferred_element_type=F32, precision=precision
    )


def tn(left, right):
    return lax.dot_general(left, right, (((0,), (0,)), ((), ())), preferred_element_type=F32)


def nn(left, right, precision=None):
    return jnp.dot(left, right, preferred_element_type=F32, precision=precision)


def iota(shape, dim):
    return lax.broadcasted_iota(jnp.int32, shape, dim)


def block(index, size):
    return pl.ds(pl.multiple_of(index * size, size), size)


def bucket_hot(relative):
    magnitude = jnp.abs(relative)
    level = jnp.zeros_like(relative)
    for edge in bucket_edges:
        level = level + (magnitude >= edge).astype(jnp.int32)
    level = level + jnp.where(relative > 0, len(bucket_edges) + 1, 0)
    return (iota((32, relative.shape[1]), 0) == level).astype(F32)


def route_places(routes_t):
    hots = [(iota((EXPERTS, ROWS), 0) == routes_t[k : k + 1, :]).astype(F32) for k in range(2)]
    both = hots[0] + hots[1]
    before = (iota((ROWS, ROWS), 0) < iota((ROWS, ROWS), 1)).astype(BF16)
    earlier = nn(both.astype(BF16), before)
    slots = [jnp.sum(earlier * hot, axis=0, keepdims=True) for hot in hots]
    places = [routes_t[k : k + 1, :].astype(F32) * SLOTS + slots[k] for k in range(2)]
    return hots, both, slots, places


def slot_hot(slots_row):
    return (iota((128, ROWS), 0).astype(F32) == slots_row).astype(F32)


def live_column(long_len, short_len, row):
    position = iota((ROWS, 1), 0)
    is_long = position < LONG
    here = jnp.where(is_long, position + row * LONG, position - LONG)
    limit = jnp.where(is_long, long_len, short_len)
    return (here < limit).astype(F32)


def forward_kernel(
    long_len, short_len, tokens, cot, routes_t, gain_a, gain_m, rel_bias_t, router_t, ids, wq, wk, wv, wo,
    x_slots, o_slots, g_slots, query, long_kv, short_kv, mixed, norm_l, norm_s, resid, probs_t, rnorm_t,
    normed, buffer_o, buffer_x, gate_out, table_l, table_s,
    o_send, o_recv, x_send, x_recv, g_send, g_recv, own_sem, kv_send, kv_recv, t_send, t_recv,
):
    row = lax.axis_index("row")
    col = lax.axis_index("col")
    mate = 3 - row
    barrier = pltpu.get_barrier_semaphore()
    for step in (1, 2, 3):
        pl.semaphore_signal(barrier, inc=1, device_id=(lax.rem(row + step, 4), col), device_id_type=MESH_ID)

    def greet(step, carry):
        pl.semaphore_signal(barrier, inc=1, device_id=(row, lax.rem(col + step, EXPERTS)), device_id_type=MESH_ID)
        return carry

    lax.fori_loop(1, EXPERTS, greet, 0)

    hots, both, slots, places = route_places(routes_t[...])

    def message(buffer, slots_ref, send, recv, dest, source):
        return pltpu.make_async_remote_copy(
            buffer.at[block(dest, FOLDED)],
            slots_ref.at[0, block(source, FOLDED)],
            send.at[dest],
            recv.at[source],
            device_id=(row, dest),
            device_id_type=MESH_ID,
        )

    def dispatch(source, buffer, slots_ref, send, recv, own):
        def one_group(i, carry):
            group = lax.rem(lax.div(col, 4) + i, 8)
            rows = block(group, 320)
            slot_id = ids[rows, 0:1]
            quarter = ids[rows, 1:2]
            match = (slot_id == places[0]) | (slot_id == places[1])
            total = jnp.zeros((320, QUARTER), F32)
            for q in range(4):
                hot = jnp.where(match & (quarter == q), 1.0, 0.0).astype(BF16)
                total = total + nn(hot, source[:, q * QUARTER : (q + 1) * QUARTER])
            buffer[rows, :] = total.astype(BF16)
            for j in range(4):
                dest = group * 4 + j

                @pl.when(dest != col)
                def _():
                    message(buffer, slots_ref, send, recv, dest, col).start()

                @pl.when(dest == col)
                def _():
                    pltpu.make_async_copy(
                        buffer.at[block(dest, FOLDED)], slots_ref.at[0, block(dest, FOLDED)], own
                    ).start()

            return carry

        lax.fori_loop(0, 8, one_group, 0)

    def wait_source(buffer, slots_ref, send, recv, own, source):
        @pl.when(source != col)
        def _():
            message(buffer, slots_ref, send, recv, col, source).wait_recv()

        @pl.when(source == col)
        def _():
            pltpu.make_async_copy(
                buffer.at[block(col, FOLDED)], slots_ref.at[0, block(col, FOLDED)], own
            ).wait()

    def wait_sends(buffer, slots_ref, send, recv):
        def one(step, carry):
            message(buffer, slots_ref, send, recv, lax.rem(col + step, EXPERTS), col).wait_send()
            return carry

        lax.fori_loop(1, EXPERTS, one, 0)

    pl.semaphore_wait(barrier, EXPERTS + 2)

    def norm_rows(i, carry):
        rows = block(i, 64)
        x = tokens[rows, :].astype(F32)
        scale = lax.rsqrt(jnp.mean(x * x, axis=1, keepdims=True) + norm_eps)
        normed[rows, :] = (x * scale * gain_a[...]).astype(BF16)
        return carry

    lax.fori_loop(0, 4, norm_rows, 0)

    def project_kv(i, carry):
        lanes = block(i, 256)
        for offset, weight in ((0, wk), (WIDTH, wv)):
            part = nn(normed[...], weight[:, lanes]).astype(BF16)
            out = pl.ds(pl.multiple_of(i * 256 + offset, 256), 256)
            long_kv[row, :, out] = part[:LONG]
            short_kv[:, out] = part[LONG:]
        return carry

    lax.fori_loop(0, 4, project_kv, 0)

    def kv_move(step):
        return pltpu.make_async_remote_copy(
            long_kv.at[row],
            long_kv.at[row],
            kv_send.at[step - 1],
            kv_recv.at[step - 1],
            device_id=(lax.rem(row + step, 4), col),
            device_id_type=MESH_ID,
        )

    def kv_arrival(step):
        source = lax.rem(row + 4 - step, 4)
        return pltpu.make_async_remote_copy(
            long_kv.at[source],
            long_kv.at[source],
            kv_send.at[step - 1],
            kv_recv.at[step - 1],
            device_id=(source, col),
            device_id_type=MESH_ID,
        )

    for step in (1, 2, 3):
        kv_move(step).start()

    dispatch(cot, buffer_o, o_slots, o_send, o_recv, own_sem.at[0])

    def project_q(i, carry):
        lanes = block(i, 256)
        query[:, lanes] = nn(normed[...], wq[:, lanes]).astype(BF16)
        return carry

    lax.fori_loop(0, 4, project_q, 0)

    place_l = iota((1, TABLE), 1)
    place_l = jnp.where(place_l < 512, place_l, place_l - TABLE) - row * LONG
    place_s = iota((1, 256), 1)
    place_s = jnp.where(place_s < 128, place_s, place_s - 256)
    table_l[...] = nn(rel_bias_t[...], bucket_hot(place_l), highest)
    table_s[...] = nn(rel_bias_t[...], bucket_hot(place_s), highest)

    lane = iota((1, 128), 1)

    def attend(q2, k2, v2, table, head, keep, count, width):
        bias = pltpu.roll(
            jnp.broadcast_to(table[pl.ds(head, 1), :], (128, width)), 0, 1, stride=1, stride_axis=0
        )[:, :count]
        scores = jnp.where(keep, nt(q2, k2) * 0.125 + bias, masked_score)
        row_max = jnp.max(scores, axis=1, keepdims=True)
        terms = jnp.exp(scores - row_max)
        total = jnp.sum(terms, axis=1, keepdims=True)
        return nn((terms / total).astype(BF16), v2), row_max + jnp.log(total)

    def attend_pairs(q_first, keys_of, table, keep, count, width, norm_out):
        def one_pair(pair, carry):
            lanes = block(pair, 128)
            values = pl.ds(pl.multiple_of(pair * 128 + WIDTH, 128), 128)
            q2 = query[q_first : q_first + 128, lanes]
            k2, v2 = keys_of(lanes), keys_of(values)
            outs = []
            norms = norm_out[...]
            for side in range(2):
                here = (lane >= 64) if side else (lane < 64)
                out, norm = attend(
                    jnp.where(here, q2, jnp.zeros_like(q2)), k2, v2, table, pair * 2 + side, keep, count, width
                )
                outs.append(out)
                norms = jnp.where(lane == pair * 2 + side, norm, norms)
            norm_out[...] = norms
            mixed[q_first : q_first + 128, lanes] = jnp.where(lane < 64, outs[0], outs[1]).astype(BF16)
            return carry

        lax.fori_loop(0, HEADS // 2, one_pair, 0)

    norm_l[...] = jnp.zeros_like(norm_l)
    norm_s[...] = jnp.zeros_like(norm_s)
    attend_pairs(LONG, lambda lanes: short_kv[:, lanes], table_s, iota((1, 128), 1) < short_len[0], 128, 256, norm_s)

    def wait_o(source, carry):
        wait_source(buffer_o, o_slots, o_send, o_recv, own_sem.at[0], source)
        return carry

    lax.fori_loop(0, EXPERTS, wait_o, 0)

    def to_mate(source, target, index):
        return pltpu.make_async_remote_copy(
            source, target, t_send.at[index], t_recv.at[index], device_id=(mate, col), device_id_type=MESH_ID
        )

    for step in (1, 2, 3):
        kv_arrival(step).wait_recv()
    o_move = to_mate(o_slots.at[0], o_slots.at[1], 8)
    o_move.start()
    attend_pairs(
        0,
        lambda lanes: long_kv[:, :, lanes].reshape(512, 128),
        table_l,
        iota((1, 512), 1) < long_len[0],
        512,
        TABLE,
        norm_l,
    )

    def project_out(i, carry):
        lanes = block(i, 256)
        resid[:, lanes] = tokens[:, lanes].astype(F32) + nn(mixed[...], wo[:, lanes])
        return carry

    lax.fori_loop(0, 4, project_out, 0)

    def norm_again(i, carry):
        rows = block(i, 64)
        x = resid[rows, :]
        scale = lax.rsqrt(jnp.mean(x * x, axis=1, keepdims=True) + norm_eps)
        normed[rows, :] = (x * scale * gain_m[...]).astype(BF16)
        return carry

    lax.fori_loop(0, 4, norm_again, 0)
    dispatch(normed, buffer_x, x_slots, x_send, x_recv, own_sem.at[1])

    x = resid[...]
    scale = lax.rsqrt(jnp.mean(x * x, axis=1, keepdims=True) + norm_eps)
    logits = nt(router_t[...], x * scale * gain_m[...], highest)
    row_max = jnp.max(logits, axis=0, keepdims=True)
    terms = jnp.exp(logits - row_max)
    total = jnp.sum(terms, axis=0, keepdims=True)
    probs = terms / total
    probs_t[...] = probs
    rnorm_t[...] = row_max + jnp.log(total)
    picked = [jnp.sum(probs * hot, axis=0, keepdims=True) for hot in hots]
    picked_sum = picked[0] + picked[1]
    gate_slots = jnp.zeros((EXPERTS, 128), F32)
    for k in range(2):
        gate_slots = gate_slots + nt(hots[k] * (picked[k] / picked_sum), slot_hot(slots[k]), highest)
    for e in range(EXPERTS):
        gate_out[e] = jnp.broadcast_to(gate_slots[e : e + 1, :], (8, 128))

    def gate_message(dest, source):
        return pltpu.make_async_remote_copy(
            gate_out.at[dest],
            g_slots.at[0, source],
            g_send.at[dest],
            g_recv.at[source],
            device_id=(row, dest),
            device_id_type=MESH_ID,
        )

    def send_gates(step, carry):
        gate_message(lax.rem(col + step, EXPERTS), col).start()
        return carry

    lax.fori_loop(1, EXPERTS, send_gates, 0)
    own_gates = pltpu.make_async_copy(gate_out.at[col], g_slots.at[0, col], own_sem.at[2])
    own_gates.start()

    def x_move(group):
        rows = block(group, 320)
        return to_mate(x_slots.at[0, rows], x_slots.at[1, rows], group)

    def forward_x(i, carry):
        group = lax.rem(lax.div(col, 4) + 8 - i, 8)
        for j in range(4):
            wait_source(buffer_x, x_slots, x_send, x_recv, own_sem.at[1], group * 4 + j)
        x_move(group).start()
        return carry

    lax.fori_loop(0, 8, forward_x, 0)

    def wait_gates(step, carry):
        gate_message(col, lax.rem(col + step, EXPERTS)).wait_recv()
        return carry

    lax.fori_loop(1, EXPERTS, wait_gates, 0)
    own_gates.wait()
    g_move = to_mate(g_slots.at[0], g_slots.at[1], 9)
    g_move.start()

    for step in (1, 2, 3):
        kv_move(step).wait_send()
    wait_sends(buffer_o, o_slots, o_send, o_recv)
    wait_sends(buffer_x, x_slots, x_send, x_recv)

    def wait_gate_sends(step, carry):
        gate_message(lax.rem(col + step, EXPERTS), col).wait_send()
        return carry

    lax.fori_loop(1, EXPERTS, wait_gate_sends, 0)
    o_move.wait()

    def wait_x(group, carry):
        x_move(group).wait()
        return carry

    lax.fori_loop(0, 8, wait_x, 0)
    g_move.wait()


def forward(long_lengths, short_lengths, tokens, cot, routes_t, gain_a, gain_m, rel_bias_t, router_t, ids, wq, wk, wv, wo):
    def out(shape, dtype):
        return jax.ShapeDtypeStruct(shape, dtype)

    return pl.pallas_call(
        forward_kernel,
        out_shape=(
            out((2, PIECES, QUARTER), BF16),
            out((2, PIECES, QUARTER), BF16),
            out((2, EXPERTS, 8, 128), F32),
            out((ROWS, WIDTH), BF16),
            out((4, LONG, 2 * WIDTH), BF16),
            out((LONG, 2 * WIDTH), BF16),
            out((ROWS, WIDTH), BF16),
            out((128, 128), F32),
            out((128, 128), F32),
            out((ROWS, WIDTH), F32),
            out((EXPERTS, ROWS), F32),
            out((1, ROWS), F32),
        ),
        in_specs=[SMEM_SPEC] * 2 + [VMEM_SPEC] * 12,
        out_specs=[HBM_SPEC] * 3 + [VMEM_SPEC] * 9,
        scratch_shapes=[
            pltpu.VMEM((ROWS, WIDTH), BF16),
            pltpu.VMEM((PIECES, QUARTER), BF16),
            pltpu.VMEM((PIECES, QUARTER), BF16),
            pltpu.VMEM((EXPERTS, 8, 128), F32),
            pltpu.VMEM((HEADS, TABLE), F32),
            pltpu.VMEM((HEADS, 256), F32),
            DMA((EXPERTS,)),
            DMA((EXPERTS,)),
            DMA((EXPERTS,)),
            DMA((EXPERTS,)),
            DMA((EXPERTS,)),
            DMA((EXPERTS,)),
            DMA((3,)),
            DMA((3,)),
            DMA((3,)),
            DMA((10,)),
            DMA((10,)),
        ],
        compiler_params=pltpu.CompilerParams(
            collective_id=1, has_side_effects=True, vmem_limit_bytes=56 * 1024 * 1024
        ),
        name="forward_and_dispatch",
    )(long_lengths, short_lengths, tokens, cot, routes_t, gain_a, gain_m, rel_bias_t, router_t, ids, wq, wk, wv, wo)


def expert_kernel(
    x_slots, o_slots, g_slots, unfold, fold, row_hot, slot_of, wg_own, wu_own, wd_own, wg_mate, wu_mate, wd_mate,
    dx_back, dg_back, outs, wg_grad, wu_grad, wd_grad, wg_send, wu_send, wd_send,
    stage, xs, os, dys, wg, wu, wd, act, dg, du, part, arrived, gate_part, gate_arrived, gate_out, grad_stage, grad_half,
    stage_sem, weight_sem, t_send, t_recv, m_send, m_recv, r_send, r_recv, own_sem, out_sem,
):
    row = lax.axis_index("row")
    col = lax.axis_index("col")
    mate = 3 - row
    barrier = pltpu.get_barrier_semaphore()
    pl.semaphore_signal(barrier, inc=1, device_id=(mate, col), device_id_type=MESH_ID)

    def greet(step, carry):
        pl.semaphore_signal(barrier, inc=1, device_id=(row, lax.rem(col + step, EXPERTS)), device_id_type=MESH_ID)
        return carry

    lax.fori_loop(1, EXPERTS, greet, 0)

    def load(source, which, index):
        return pltpu.make_async_copy(source.at[which], stage.at[index], stage_sem.at[index])

    load(x_slots, 1, 0).start()
    load(o_slots, 1, 1).start()
    weights = []
    for i, (own, other, held) in enumerate(((wg_own, wg_mate, wg), (wu_own, wu_mate, wu), (wd_own, wd_mate, wd))):
        for j, source in enumerate((own, other)):
            copy = pltpu.make_async_copy(source, held.at[pl.ds(j * SHARD, SHARD)], weight_sem.at[i, j])
            copy.start()
            weights.append(copy)

    def spread(index, target, first):
        def one(group, carry):
            wide = nn(unfold[...], stage[index, block(group, 320), :]).astype(BF16)
            rows = pl.ds(pl.multiple_of(first + group * 80, 16), 80)
            for q in range(4):
                target[rows, q * QUARTER : (q + 1) * QUARTER] = wide[q * 80 : (q + 1) * 80]
            return carry

        lax.fori_loop(0, 8, one, 0)

    def gate_column(which):
        gates = jnp.concatenate([g_slots[which, e, 0:1, :] for e in range(EXPERTS)], axis=0)
        wide = nn(row_hot[...], gates, highest)
        lanes = iota((640, 128), 1)
        return jnp.sum(jnp.where(lanes == slot_of[...], wide, 0.0), axis=1, keepdims=True)

    def hidden_tile(first, start, width):
        lanes = pl.ds(start, width)
        for part_rows in range(2):
            rows = pl.ds(first + part_rows * 320, 320)
            x = xs[rows, :]
            gate_pre = nt(x, wg[lanes, :])
            up_pre = nt(x, wu[lanes, :])
            d_act = nt(dys[rows, :], wd[lanes, :])
            square = gate_pre * gate_pre
            bend = jnp.tanh(0.7978845608028654 * gate_pre * (1.0 + 0.044715 * square))
            half = 0.5 * (1.0 + bend)
            gelu = gate_pre * half
            slope = half + 0.5 * gate_pre * (1.0 - bend * bend) * (
                0.7978845608028654 * (1.0 + 3.0 * 0.044715 * square)
            )
            act[rows, lanes] = (gelu * up_pre).astype(BF16)
            du[rows, lanes] = (d_act * gelu).astype(BF16)
            dg[rows, lanes] = (d_act * up_pre * slope).astype(BF16)

    def first_half(first):
        def one(i, carry):
            hidden_tile(first, pl.multiple_of(i * 256, 256), 256)
            return carry

        lax.fori_loop(0, 5, one, 0)
        hidden_tile(first, 1280, 128)

    def input_gradient(first, lanes):
        rows = pl.ds(first, 640)
        return nn(dg[rows, :], wg[:, lanes]) + nn(du[rows, :], wu[:, lanes])

    def to_mate(source, target, index):
        return pltpu.make_async_remote_copy(
            source, target, t_send.at[index], t_recv.at[index], device_id=(mate, col), device_id_type=MESH_ID
        )

    def output_part(first, which):
        def one(n, total):
            lanes = block(n, QUARTER)
            rows = pl.ds(first, 640)
            value = nn(act[rows, :], wd[:, lanes])
            stage[0, block(n, 640), :] = value.astype(BF16)
            return total + jnp.sum(value * os[rows, lanes].astype(F32), axis=1, keepdims=True)

        total = lax.fori_loop(0, 4, one, jnp.zeros((640, 1), F32))

        def fold_one(group, carry):
            tall = jnp.concatenate(
                [stage[0, pl.ds(pl.multiple_of(q * 640 + group * 80, 16), 80), :] for q in range(4)], axis=0
            )
            outs[which, block(group, 320), :] = nn(fold[...], tall).astype(BF16)
            return carry

        lax.fori_loop(0, 8, fold_one, 0)
        spread_out = jnp.where(iota((640, 128), 1) == slot_of[...], total, 0.0)
        return lax.dot_general(
            row_hot[...], spread_out, (((0,), (0,)), ((), ())), preferred_element_type=F32, precision=highest
        )

    load(x_slots, 1, 0).wait()
    spread(0, xs, 640)
    load(x_slots, 0, 0).start()
    load(o_slots, 1, 1).wait()
    spread(1, os, 640)
    load(o_slots, 0, 1).start()
    dys[640:1280, :] = (os[640:1280, :].astype(F32) * gate_column(1)).astype(BF16)
    load(x_slots, 0, 0).wait()
    spread(0, xs, 0)
    load(o_slots, 0, 1).wait()
    spread(1, os, 0)
    dys[0:640, :] = (os[0:640, :].astype(F32) * gate_column(0)).astype(BF16)
    for copy in weights:
        copy.wait()
    first_half(640)
    pl.semaphore_wait(barrier, EXPERTS)

    def part_move(n):
        return to_mate(part.at[block(n, 640)], arrived.at[block(n, 640)], n)

    def mate_gradient(n, carry):
        part[block(n, 640), :] = input_gradient(640, block(n, QUARTER)).astype(BF16)
        part_move(n).start()
        return carry

    lax.fori_loop(0, 4, mate_gradient, 0)
    gate_part[...] = output_part(640, 1)
    gate_move = to_mate(gate_part, gate_arrived, 4)
    gate_move.start()
    first_half(0)
    gates = output_part(0, 0)

    def own_gradient(n, carry):
        value = input_gradient(0, block(n, QUARTER))
        part_move(n).wait_recv()
        stage[1, block(n, 640), :] = (value + arrived[block(n, 640), :].astype(F32)).astype(BF16)
        return carry

    lax.fori_loop(0, 4, own_gradient, 0)
    gate_move.wait_recv()
    gates = gates + gate_arrived[...]
    for e in range(EXPERTS):
        gate_out[e] = jnp.broadcast_to(gates[e : e + 1, :], (8, 128))

    def message(dest, source):
        return pltpu.make_async_remote_copy(
            stage.at[0, block(dest, FOLDED)],
            dx_back.at[block(source, FOLDED)],
            m_send.at[dest],
            m_recv.at[source],
            device_id=(row, dest),
            device_id_type=MESH_ID,
        )

    def gate_message(dest, source):
        return pltpu.make_async_remote_copy(
            gate_out.at[dest],
            dg_back.at[source],
            r_send.at[dest],
            r_recv.at[source],
            device_id=(row, dest),
            device_id_type=MESH_ID,
        )

    own_dx = pltpu.make_async_copy(stage.at[0, block(col, FOLDED)], dx_back.at[block(col, FOLDED)], own_sem.at[0])
    own_dg = pltpu.make_async_copy(gate_out.at[col], dg_back.at[col], own_sem.at[1])

    def return_group(i, carry):
        group = lax.rem(lax.div(col, 4) + i, 8)
        tall = jnp.concatenate(
            [stage[1, pl.ds(pl.multiple_of(q * 640 + group * 80, 16), 80), :] for q in range(4)], axis=0
        )
        stage[0, block(group, 320), :] = nn(fold[...], tall).astype(BF16)
        for j in range(4):
            dest = group * 4 + j

            @pl.when(dest != col)
            def _():
                message(dest, col).start()
                gate_message(dest, col).start()

            @pl.when(dest == col)
            def _():
                own_dx.start()
                own_dg.start()

        return carry

    lax.fori_loop(0, 8, return_group, 0)

    grads = ((dg, xs, wg_grad, wg_send), (du, xs, wu_grad, wu_send), (act, dys, wd_grad, wd_send))

    def grad_copies(slot, start, width, result, send):
        copies = []
        if start < SHARD:
            rows = min(width, SHARD - start)
            copies.append((grad_stage.at[slot, pl.ds(0, rows)], result.at[pl.ds(start, rows)], out_sem.at[slot, 0]))
        if start + width > SHARD:
            skip = max(0, SHARD - start)
            copies.append(
                (
                    grad_half.at[slot, pl.ds(skip, width - skip)],
                    send.at[pl.ds(start + skip - SHARD, width - skip)],
                    out_sem.at[slot, 1],
                )
            )
        return [pltpu.make_async_copy(*copy) for copy in copies]

    pending = [[], []]
    turn = 0
    for left, right, result, send in grads:
        for start in range(0, HALF, 256):
            width = min(256, HALF - start)
            slot = turn % 2
            turn += 1
            for copy in pending[slot]:
                copy.wait()
            value = tn(left[:, start : start + width], right[...])
            if start < SHARD:
                grad_stage[slot, 0:width, :] = value
            if start + width > SHARD:
                grad_half[slot, 0:width, :] = value.astype(BF16)
            pending[slot] = grad_copies(slot, start, width, result, send)
            for copy in pending[slot]:
                copy.start()
    for copies in pending:
        for copy in copies:
            copy.wait()

    def wait_source(step, carry):
        source = lax.rem(col + step, EXPERTS)
        message(col, source).wait_recv()
        gate_message(col, source).wait_recv()
        message(source, col).wait_send()
        gate_message(source, col).wait_send()
        return carry

    lax.fori_loop(1, EXPERTS, wait_source, 0)
    own_dx.wait()
    own_dg.wait()

    def wait_parts(n, carry):
        part_move(n).wait_send()
        return carry

    lax.fori_loop(0, 4, wait_parts, 0)
    gate_move.wait_send()


def experts(x_slots, o_slots, g_slots, consts, own, other):
    def out(shape, dtype):
        return jax.ShapeDtypeStruct(shape, dtype)

    hidden = (2 * 640, HALF)
    return pl.pallas_call(
        expert_kernel,
        out_shape=(
            out((PIECES, QUARTER), BF16),
            out((EXPERTS, 8, 128), F32),
            out((2, PIECES, QUARTER), BF16),
        )
        + (out((SHARD, WIDTH), F32),) * 3
        + (out((SHARD, WIDTH), BF16),) * 3,
        in_specs=[HBM_SPEC] * 2 + [VMEM_SPEC] * 5 + [HBM_SPEC] * 6,
        out_specs=[HBM_SPEC] * 2 + [VMEM_SPEC] + [HBM_SPEC] * 6,
        scratch_shapes=[
            pltpu.VMEM((2, PIECES, QUARTER), BF16),
            pltpu.VMEM((1280, WIDTH), BF16),
            pltpu.VMEM((1280, WIDTH), BF16),
            pltpu.VMEM((1280, WIDTH), BF16),
            pltpu.VMEM((HALF, WIDTH), BF16),
            pltpu.VMEM((HALF, WIDTH), BF16),
            pltpu.VMEM((HALF, WIDTH), BF16),
            pltpu.VMEM(hidden, BF16),
            pltpu.VMEM(hidden, BF16),
            pltpu.VMEM(hidden, BF16),
            pltpu.VMEM((PIECES, QUARTER), BF16),
            pltpu.VMEM((PIECES, QUARTER), BF16),
            pltpu.VMEM((EXPERTS, 128), F32),
            pltpu.VMEM((EXPERTS, 128), F32),
            pltpu.VMEM((EXPERTS, 8, 128), F32),
            pltpu.VMEM((2, 256, WIDTH), F32),
            pltpu.VMEM((2, 256, WIDTH), BF16),
            DMA((2,)),
            DMA((3, 2)),
            DMA((5,)),
            DMA((5,)),
            DMA((EXPERTS,)),
            DMA((EXPERTS,)),
            DMA((EXPERTS,)),
            DMA((EXPERTS,)),
            DMA((2,)),
            DMA((2, 2)),
        ],
        compiler_params=pltpu.CompilerParams(
            collective_id=2, has_side_effects=True, vmem_limit_bytes=60 * 1024 * 1024
        ),
        name="experts",
    )(x_slots, o_slots, g_slots, *consts, *own, *other)


def backward_kernel(
    long_len, short_len, tokens, cot, routes, routes_t, gain_a, gain_m, rel_bias_t, router_t, ids_t, wq, wk, wv, wo,
    resid, probs_t, rnorm_t, query, long_kv, short_kv, mixed, norm_l, norm_s, dx_back, dg_back, outs,
    block_out, tokens_grad, grads, small,
    total, branch, d_mixed, normed, flipped, d_query, d_kv, d_long, d_arrived, table_l, table_s, diag_l, diag_s,
    turned, out_arrived, out_sum, out_back,
    t_send, t_recv, kv_send, kv_recv, m_send, m_recv, own_sem,
):
    row = lax.axis_index("row")
    col = lax.axis_index("col")
    mate = 3 - row
    barrier = pltpu.get_barrier_semaphore()
    for step in (1, 2, 3):
        pl.semaphore_signal(barrier, inc=1, device_id=(lax.rem(row + step, 4), col), device_id_type=MESH_ID)

    def greet(step, carry):
        pl.semaphore_signal(barrier, inc=1, device_id=(row, lax.rem(col + step, EXPERTS)), device_id_type=MESH_ID)
        return carry

    lax.fori_loop(1, EXPERTS, greet, 0)
    pl.semaphore_wait(barrier, EXPERTS + 2)

    out_move = pltpu.make_async_remote_copy(
        outs.at[1], out_arrived, t_send, t_recv, device_id=(mate, col), device_id_type=MESH_ID
    )
    out_move.start()

    def message(dest, source):
        return pltpu.make_async_remote_copy(
            out_sum.at[block(dest, FOLDED)],
            out_back.at[block(source, FOLDED)],
            m_send.at[dest],
            m_recv.at[source],
            device_id=(row, dest),
            device_id_type=MESH_ID,
        )

    own_out = pltpu.make_async_copy(out_sum.at[block(col, FOLDED)], out_back.at[block(col, FOLDED)], own_sem)

    hot_rows = [(iota((ROWS, EXPERTS), 1) == routes[:, k : k + 1]).astype(F32) for k in range(2)]
    before = (iota((ROWS, ROWS), 1) < iota((ROWS, ROWS), 0)).astype(BF16)
    earlier = nn(before, (hot_rows[0] + hot_rows[1]).astype(BF16))
    place = [
        routes[:, k : k + 1].astype(F32) * SLOTS + jnp.sum(earlier * hot_rows[k], axis=1, keepdims=True)
        for k in range(2)
    ]

    def gather_back(source):
        total[...] = jnp.zeros_like(total)

        def one(i, carry):
            here = block(i, 512)
            slot_id, quarter = ids_t[0:1, here], ids_t[1:2, here]
            match = (slot_id == place[0]) | (slot_id == place[1])
            values = source[here, :]
            for q in range(4):
                hot = jnp.where(match & (quarter == q), 1.0, 0.0).astype(BF16)
                total[:, q * QUARTER : (q + 1) * QUARTER] += nn(hot, values)
            return carry

        lax.fori_loop(0, PIECES // 512, one, 0)

    gather_back(dx_back)

    hots, both, slots, unused = route_places(routes_t[...])
    probs = probs_t[...]
    picked = [jnp.sum(probs * hot, axis=0, keepdims=True) for hot in hots]
    picked_sum = picked[0] + picked[1]
    gate_slots = jnp.concatenate([dg_back[e, 0:1, :] for e in range(EXPERTS)], axis=0)
    d_gates = [
        jnp.sum(hots[k] * nn(gate_slots, slot_hot(slots[k]), highest), axis=0, keepdims=True) for k in range(2)
    ]
    shared = (d_gates[0] * picked[0] + d_gates[1] * picked[1]) / (picked_sum * picked_sum)
    fraction = jnp.sum(both, axis=1, keepdims=True) / (2 * ROWS)
    d_probs = balance_coef * EXPERTS * fraction
    for k in range(2):
        d_probs = d_probs + (d_gates[k] / picked_sum - shared) * hots[k]
    d_logits = probs * (d_probs - jnp.sum(d_probs * probs, axis=0, keepdims=True))
    d_logits = d_logits + 2.0 * zloss_coef * rnorm_t[...] * probs

    x = resid[...]
    scale = lax.rsqrt(jnp.mean(x * x, axis=1, keepdims=True) + norm_eps)
    router_grad = nn(d_logits, x * scale * gain_m[...], highest)
    small[...] = jnp.zeros_like(small)
    for i in range(8):
        small[i * 32 : (i + 1) * 32, :] = router_grad[:, i * 128 : (i + 1) * 128]
    d_normed = total[...] + nn(d_logits.T, router_t[...], highest)
    gain_grad = jnp.sum(d_normed * (x * scale), axis=0, keepdims=True)
    for i in range(8):
        small[264 + i : 265 + i, :] = gain_grad[:, i * 128 : (i + 1) * 128]
    d_normed = d_normed * gain_m[...]
    shrink = jnp.mean(d_normed * x, axis=1, keepdims=True)
    d_resid = cot[...].astype(F32) + scale * d_normed - x * (scale * scale * scale * shrink)
    tokens_grad[...] = d_resid
    branch[...] = d_resid.astype(BF16)

    def flip(source):
        def one(i, carry):
            flipped[block(i, 128), :] = source[:, block(i, 128)].T
            return carry

        lax.fori_loop(0, 8, one, 0)

    def weight_gradient(which, value_of):
        def one(n, carry):
            out = nn(flipped[...], value_of(n)).astype(BF16)
            first = which * 8192 + n * 2048
            grads[pl.ds(pl.multiple_of(first, 1024), 1024), :] = out[:, 0:128]
            grads[pl.ds(pl.multiple_of(first + 1024, 1024), 1024), :] = out[:, 128:256]
            return carry

        lax.fori_loop(0, 4, one, 0)

    def back_mixed(n, carry):
        rows = block(n, 256)
        d_mixed[:, rows] = nt(branch[...], wo[rows, :]).astype(BF16)
        return carry

    lax.fori_loop(0, 4, back_mixed, 0)

    place_l = iota((1, TABLE), 1)
    place_l = jnp.where(place_l < 512, place_l, place_l - TABLE) - row * LONG
    place_s = iota((1, 256), 1)
    place_s = jnp.where(place_s < 128, place_s, place_s - 256)
    table_l[...] = nn(rel_bias_t[...], bucket_hot(place_l), highest)
    table_s[...] = nn(rel_bias_t[...], bucket_hot(place_s), highest)
    turned[...] = (iota((128, 128), 0) + iota((128, 128), 1) == 127).astype(BF16)
    lane = iota((1, 128), 1)

    def attend_back(first, keys_of, store_kv, table, diag, keep, count, width, norm_in):
        def one_pair(pair, carry):
            lanes = block(pair, 128)
            values = pl.ds(pl.multiple_of(pair * 128 + WIDTH, 128), 128)
            q2 = query[first : first + 128, lanes]
            m2 = d_mixed[first : first + 128, lanes]
            k2, v2 = keys_of(lanes), keys_of(values)
            d_k = jnp.zeros((count, 128), F32)
            d_v = jnp.zeros((count, 128), F32)
            d_q = []
            for side in range(2):
                head = pair * 2 + side
                here = (lane >= 64) if side else (lane < 64)
                q1 = jnp.where(here, q2, jnp.zeros_like(q2))
                m1 = jnp.where(here, m2, jnp.zeros_like(m2))
                norm = jnp.sum(jnp.where(lane == head, norm_in[...], 0.0), axis=1, keepdims=True)
                bias = pltpu.roll(
                    jnp.broadcast_to(table[pl.ds(head, 1), :], (128, width)), 0, 1, stride=1, stride_axis=0
                )[:, :count]
                scores = jnp.where(keep, nt(q1, k2) * 0.125 + bias, masked_score)
                probs = jnp.exp(scores - norm)
                d_probs = nt(m1, v2)
                shift = jnp.sum(probs * d_probs, axis=1, keepdims=True)
                d_scores = (probs * (d_probs - shift)).astype(BF16)
                d_v = d_v + tn(probs.astype(BF16), m1)
                d_k = d_k + tn(d_scores, q1)
                d_q.append(nn(d_scores, k2))
                reverse = nn(turned[...], d_scores)
                reverse = jnp.concatenate([reverse, jnp.zeros((128, width - count), F32)], axis=1)
                reverse = pltpu.roll(reverse, 0, 1, stride=1, stride_axis=0)
                diag[pl.ds(head, 1), :] = jnp.sum(reverse, axis=0, keepdims=True)
            d_query[first : first + 128, lanes] = (jnp.where(lane < 64, d_q[0], d_q[1]) * 0.125).astype(BF16)
            store_kv(lanes, d_k * 0.125)
            store_kv(values, d_v)
            return carry

        lax.fori_loop(0, HEADS // 2, one_pair, 0)

    def store_long(lanes, value):
        d_long[:, :, lanes] = value.astype(BF16).reshape(4, LONG, 128)

    def store_short(lanes, value):
        d_kv[LONG:, lanes] = value.astype(BF16)

    attend_back(
        0,
        lambda lanes: long_kv[:, :, lanes].reshape(512, 128),
        store_long,
        table_l,
        diag_l,
        iota((1, 512), 1) < long_len[0],
        512,
        TABLE,
        norm_l,
    )

    def kv_move(step):
        dest = lax.rem(row + step, 4)
        return pltpu.make_async_remote_copy(
            d_long.at[dest],
            d_arrived.at[step - 1],
            kv_send.at[step - 1],
            kv_recv.at[step - 1],
            device_id=(dest, col),
            device_id_type=MESH_ID,
        )

    for step in (1, 2, 3):
        kv_move(step).start()

    out_move.wait_recv()

    def return_group(i, carry):
        group = lax.rem(lax.div(col, 4) + i, 8)
        rows = block(group, 320)
        out_sum[rows, :] = (outs[0, rows, :].astype(F32) + out_arrived[rows, :].astype(F32)).astype(BF16)
        for j in range(4):
            dest = group * 4 + j

            @pl.when(dest != col)
            def _():
                message(dest, col).start()

            @pl.when(dest == col)
            def _():
                own_out.start()

        return carry

    lax.fori_loop(0, 8, return_group, 0)

    attend_back(
        LONG,
        lambda lanes: short_kv[:, lanes],
        store_short,
        table_s,
        diag_s,
        iota((1, 128), 1) < short_len[0],
        128,
        256,
        norm_s,
    )
    flip(mixed)
    weight_gradient(3, lambda n: branch[:, block(n, 256)])
    back_l = bucket_hot(iota((1, TABLE), 1) - 127 - row * LONG)
    back_s = bucket_hot(iota((1, 256), 1) - 127)
    small[272:288, 0:32] = nt(diag_l[...], back_l, highest) + nt(diag_s[...], back_s, highest)

    def norm_rows(i, carry):
        rows = block(i, 64)
        x = tokens[rows, :].astype(F32)
        scale = lax.rsqrt(jnp.mean(x * x, axis=1, keepdims=True) + norm_eps)
        normed[rows, :] = (x * scale * gain_a[...]).astype(BF16)
        return carry

    lax.fori_loop(0, 4, norm_rows, 0)
    flip(normed)
    weight_gradient(0, lambda n: d_query[:, block(n, 256)])
    for step in (1, 2, 3):
        kv_move(step).wait()

    def add_kv(i, carry):
        lanes = block(i, 256)
        value = d_long[row, :, lanes].astype(F32)
        for step in range(3):
            value = value + d_arrived[step, :, lanes].astype(F32)
        d_kv[0:LONG, lanes] = value.astype(BF16)
        return carry

    lax.fori_loop(0, 8, add_kv, 0)
    weight_gradient(1, lambda n: d_kv[:, block(n, 256)])
    weight_gradient(2, lambda n: d_kv[:, pl.ds(pl.multiple_of(n * 256 + WIDTH, 256), 256)])

    def back_normed(n, carry):
        rows = block(n, 256)
        value = nt(d_query[...], wq[rows, :]) + nt(d_kv[:, 0:WIDTH], wk[rows, :])
        total[:, rows] = value + nt(d_kv[:, WIDTH:], wv[rows, :])
        return carry

    lax.fori_loop(0, 4, back_normed, 0)
    x = tokens[...].astype(F32)
    scale = lax.rsqrt(jnp.mean(x * x, axis=1, keepdims=True) + norm_eps)
    d_normed = total[...]
    gain_grad = jnp.sum(d_normed * (x * scale), axis=0, keepdims=True)
    for i in range(8):
        small[256 + i : 257 + i, :] = gain_grad[:, i * 128 : (i + 1) * 128]
    d_normed = d_normed * gain_a[...]
    shrink = jnp.mean(d_normed * x, axis=1, keepdims=True)
    tokens_grad[...] = tokens_grad[...] + scale * d_normed - x * (scale * scale * scale * shrink)

    def wait_source(step, carry):
        source = lax.rem(col + step, EXPERTS)
        message(col, source).wait_recv()
        message(source, col).wait_send()
        return carry

    lax.fori_loop(1, EXPERTS, wait_source, 0)
    own_out.wait()
    out_move.wait_send()
    total[...] = jnp.zeros_like(total)
    gates = [picked[k] / picked_sum for k in range(2)]
    gates = [jnp.broadcast_to(gate, (128, ROWS)).T[:, 0:1] for gate in gates]

    def combine(i, carry):
        here = block(i, 512)
        slot_id, quarter = ids_t[0:1, here], ids_t[1:2, here]
        weight = jnp.where(slot_id == place[0], gates[0], 0.0) + jnp.where(slot_id == place[1], gates[1], 0.0)
        high = weight.astype(BF16)
        rest = (weight - high.astype(F32)).astype(BF16)
        values = out_back[here, :]
        for q in range(4):
            here_q = quarter == q
            part = nn(jnp.where(here_q, high, jnp.zeros_like(high)), values)
            part = part + nn(jnp.where(here_q, rest, jnp.zeros_like(rest)), values)
            total[:, q * QUARTER : (q + 1) * QUARTER] += part
        return carry

    lax.fori_loop(0, PIECES // 512, combine, 0)
    branch_m = total[...]
    live = live_column(long_len[0], short_len[0], row)
    resid_now = resid[...]
    result = resid_now + branch_m
    block_out[...] = result
    branch_a = resid_now - tokens[...].astype(F32)
    tallies = [
        jnp.sum(live * jnp.sum(field * field, axis=1, keepdims=True), axis=0, keepdims=True)
        for field in (result, branch_a, branch_m)
    ]
    tallies.append(jnp.sum(live, axis=0, keepdims=True))
    packed = jnp.zeros((8, 128), F32)
    for i, tally in enumerate(tallies):
        packed = jnp.where(iota((8, 128), 1) == i, tally, packed)
    small[288:296, :] = packed


def backward(*args):
    def out(shape, dtype):
        return jax.ShapeDtypeStruct(shape, dtype)

    return pl.pallas_call(
        backward_kernel,
        out_shape=(
            out((ROWS, WIDTH), F32),
            out((ROWS, WIDTH), F32),
            out((2 * SUM_ROWS[0], 128), BF16),
            out((2 * SUM_ROWS[1], 128), F32),
        ),
        in_specs=[SMEM_SPEC] * 2 + [VMEM_SPEC] * (len(args) - 2),
        out_specs=[VMEM_SPEC] * 4,
        scratch_shapes=[
            pltpu.VMEM((ROWS, WIDTH), F32),
            pltpu.VMEM((ROWS, WIDTH), BF16),
            pltpu.VMEM((ROWS, WIDTH), BF16),
            pltpu.VMEM((ROWS, WIDTH), BF16),
            pltpu.VMEM((WIDTH, ROWS), BF16),
            pltpu.VMEM((ROWS, WIDTH), BF16),
            pltpu.VMEM((ROWS, 2 * WIDTH), BF16),
            pltpu.VMEM((4, LONG, 2 * WIDTH), BF16),
            pltpu.VMEM((3, LONG, 2 * WIDTH), BF16),
            pltpu.VMEM((HEADS, TABLE), F32),
            pltpu.VMEM((HEADS, 256), F32),
            pltpu.VMEM((HEADS, TABLE), F32),
            pltpu.VMEM((HEADS, 256), F32),
            pltpu.VMEM((128, 128), BF16),
            pltpu.VMEM((PIECES, QUARTER), BF16),
            pltpu.VMEM((PIECES, QUARTER), BF16),
            pltpu.VMEM((PIECES, QUARTER), BF16),
            DMA,
            DMA,
            DMA((3,)),
            DMA((3,)),
            DMA((EXPERTS,)),
            DMA((EXPERTS,)),
            DMA,
        ],
        compiler_params=pltpu.CompilerParams(
            collective_id=3, has_side_effects=True, vmem_limit_bytes=60 * 1024 * 1024
        ),
        name="backward_local",
    )(*args)


SUM_PARTS = (
    (5120, 0, ("x", "y", "z"), 0),
    (5120, 5120, ("y", "z", "x"), 0),
    (6144, 10240, ("z", "x", "y"), 0),
    (512, 0, ("y", "x", "z"), 1),
)
SUM_ROWS = (16384, 512)


def torus_place():
    row = lax.axis_index("row")
    col = lax.axis_index("col")
    core = lax.rem(col, 2)
    x = lax.rem(lax.div(col, 2), 4)
    z = lax.div(col, 8)
    return row, z, x, core


def axis_peer(axis, step):
    row, z, x, core = torus_place()
    if axis == "y":
        row = lax.rem(row + step, 4)
    elif axis == "x":
        x = lax.rem(x + step, 4)
    elif axis == "z":
        z = lax.rem(z + step, 4)
    else:
        core = 1 - core
    return (row, (z * 4 + x) * 2 + core)


def sum_kernel(*refs):
    inputs = refs[0:2]
    results = refs[2:4]
    held = refs[4:6]
    other = refs[6:8]
    slots = refs[8:8 + 3 * len(SUM_PARTS)]
    load_sem, core_send, core_recv, hop_send, hop_recv, gather_send, gather_recv, copy_sem, last_send, last_recv = refs[
        8 + 3 * len(SUM_PARTS):
    ]
    row, z, x, core = torus_place()
    place = {"x": x, "y": row, "z": z}
    barrier = pltpu.get_barrier_semaphore()
    pl.semaphore_signal(barrier, inc=1, device_id=axis_peer("core", 1), device_id_type=MESH_ID)
    for axis in ("x", "y", "z"):
        for step in (1, 2, 3):
            pl.semaphore_signal(barrier, inc=1, device_id=axis_peer(axis, step), device_id_type=MESH_ID)
    loads = []
    for p, (rows, first, order, kind) in enumerate(SUM_PARTS):
        mine = pl.multiple_of(core * SUM_ROWS[kind] + first, 256)
        load = pltpu.make_async_copy(
            inputs[kind].at[pl.ds(mine, rows)], held[kind].at[pl.ds(first, rows)], load_sem.at[p]
        )
        load.start()
        loads.append(load)
    pl.semaphore_wait(barrier, 10)
    swaps = []
    for p, (rows, first, order, kind) in enumerate(SUM_PARTS):
        yours = pl.multiple_of((1 - core) * SUM_ROWS[kind] + first, 256)
        swap = pltpu.make_async_remote_copy(
            inputs[kind].at[pl.ds(yours, rows)],
            other[kind].at[pl.ds(first, rows)],
            core_send.at[p],
            core_recv.at[p],
            device_id=axis_peer("core", 1),
            device_id_type=MESH_ID,
        )
        swap.start()
        swaps.append(swap)

    def add_rows(kind, start, rows, terms):
        if kind == 1:
            tile = min(rows, 128)
        else:
            tile = 80 if rows % 80 == 0 else 96
            tile = tile * 4 if rows % (tile * 4) == 0 else tile

        def body(i, carry):
            offset = pl.multiple_of(i * tile, 8 if kind == 1 else 16)
            here = pl.ds(pl.multiple_of(start + offset, 8 if kind == 1 else 16), tile)
            total = held[kind][here, :].astype(jnp.float32)
            for ref, base in terms:
                total = total + ref[pl.ds(pl.multiple_of(base + offset, 8 if kind == 1 else 16), tile), :].astype(jnp.float32)
            held[kind][here, :] = total.astype(held[kind].dtype)
            return carry

        lax.fori_loop(0, rows // tile, body, 0)

    def start_hop(p, level):
        rows, first, order, kind = SUM_PARTS[p]
        size = rows // 4 ** (level + 1)
        base = first
        for done in range(level):
            base = base + place[order[done]] * (rows // 4 ** (done + 1))
        axis = order[level]
        hops = []
        for step in (1, 2, 3):
            block = lax.rem(place[axis] + step, 4)
            hop = pltpu.make_async_remote_copy(
                held[kind].at[pl.ds(pl.multiple_of(base + block * size, 8 if kind == 1 else 16), size)],
                slots[p * 3 + level].at[pl.ds((step - 1) * size, size)],
                hop_send.at[p, level, step - 1],
                hop_recv.at[p, level, step - 1],
                device_id=axis_peer(axis, step),
                device_id_type=MESH_ID,
            )
            hop.start()
            hops.append(hop)
        return hops

    def end_hop(p, level, hops):
        rows, first, order, kind = SUM_PARTS[p]
        size = rows // 4 ** (level + 1)
        base = first
        for done in range(level + 1):
            base = base + place[order[done]] * (rows // 4 ** (done + 1))
        for hop in hops:
            hop.wait()
        add_rows(kind, base, size, [(slots[p * 3 + level], step * size) for step in range(3)])

    count = len(SUM_PARTS)
    flight = [None] * count
    for p in range(count):
        rows, first, order, kind = SUM_PARTS[p]
        loads[p].wait()
        swaps[p].wait()
        add_rows(kind, first, rows, [(other[kind], first)])
        flight[p] = start_hop(p, 0)
    for level in (1, 2):
        for p in range(count):
            end_hop(p, level - 1, flight[p])
            flight[p] = start_hop(p, level)

    def place_of(p, levels):
        rows, first, order, kind = SUM_PARTS[p]
        base = first
        for done in range(levels):
            base = base + place[order[done]] * (rows // 4 ** (done + 1))
        return base

    def gather(p, level):
        rows, first, order, kind = SUM_PARTS[p]
        size = rows // 4 ** (level + 1)
        align = 8 if kind == 1 else 16
        here = pl.multiple_of(place_of(p, level + 1), align)
        there = pl.multiple_of(place_of(p, level + 1) + core * SUM_ROWS[kind], align)
        source = held[kind].at[pl.ds(here, size)] if level == 2 else results[kind].at[pl.ds(there, size)]
        moves = []
        for step in (1, 2, 3):
            move = pltpu.make_async_remote_copy(
                source,
                results[kind].at[pl.ds(there, size)],
                gather_send.at[p, level, step - 1],
                gather_recv.at[p, level, step - 1],
                device_id=axis_peer(order[level], step),
                device_id_type=MESH_ID,
            )
            move.start()
            moves.append(move)
        if level == 2:
            keep = pltpu.make_async_copy(source, results[kind].at[pl.ds(there, size)], copy_sem.at[p])
            keep.start()
            keep.wait()
        return moves

    for p in range(count):
        end_hop(p, 2, flight[p])
        flight[p] = gather(p, 2)
    for level in (1, 0):
        for p in range(count):
            for move in flight[p]:
                move.wait()
            flight[p] = gather(p, level)
    lasts = []
    for p in range(count):
        rows, first, order, kind = SUM_PARTS[p]
        size = rows // 4
        for index in range(4):
            if index > 0:
                flight[p][index - 1].wait()
            block = lax.rem(place[order[0]] + 4 - index, 4)
            there = pl.ds(pl.multiple_of(first + block * size + core * SUM_ROWS[kind], 8 if kind == 1 else 16), size)
            last = pltpu.make_async_remote_copy(
                results[kind].at[there],
                results[kind].at[there],
                last_send.at[p, index],
                last_recv.at[p, index],
                device_id=axis_peer("core", 1),
                device_id_type=MESH_ID,
            )
            last.start()
            lasts.append(last)
    for last in lasts:
        last.wait()


def sum_over_devices(weights, small):
    scratch = [
        pltpu.VMEM((SUM_ROWS[0], 128), jnp.bfloat16),
        pltpu.VMEM((SUM_ROWS[1], 128), jnp.float32),
        pltpu.VMEM((SUM_ROWS[0], 128), jnp.bfloat16),
        pltpu.VMEM((SUM_ROWS[1], 128), jnp.float32),
    ]
    for rows, first, order, kind in SUM_PARTS:
        for level in range(3):
            scratch.append(
                pltpu.VMEM((3 * rows // 4 ** (level + 1), 128), jnp.float32 if kind == 1 else jnp.bfloat16)
            )
    count = len(SUM_PARTS)
    dma = pltpu.SemaphoreType.DMA
    scratch += [
        dma((count,)),
        dma((count,)),
        dma((count,)),
        dma((count, 3, 3)),
        dma((count, 3, 3)),
        dma((count, 3, 3)),
        dma((count, 3, 3)),
        dma((count,)),
        dma((count, 4)),
        dma((count, 4)),
    ]
    return pl.pallas_call(
        sum_kernel,
        out_shape=(
            jax.ShapeDtypeStruct((2 * SUM_ROWS[0], 128), jnp.bfloat16),
            jax.ShapeDtypeStruct((2 * SUM_ROWS[1], 128), jnp.float32),
        ),
        in_specs=[pl.BlockSpec(memory_space=pl.ANY)] * 2,
        out_specs=[pl.BlockSpec(memory_space=pl.ANY)] * 2,
        scratch_shapes=scratch,
        compiler_params=pltpu.CompilerParams(
            collective_id=4, has_side_effects=True, vmem_limit_bytes=48 * 1024 * 1024
        ),
        name="sum_over_devices",
    )(weights, small)


def per_device(
    tokens_in, out_cot, long_lengths, short_lengths, routes, gain_attn, w_query, w_key, w_value, w_out, rel_bias,
    gain_moe, router, w_gate, w_up, w_down,
):
    pairs = [(0, 1), (1, 0), (2, 3), (3, 2)]
    own = (jnp.swapaxes(w_gate[0], 0, 1), jnp.swapaxes(w_up[0], 0, 1), w_down[0])
    other = tuple(lax.ppermute(weight, "row", pairs) for weight in own)
    routes_t = jnp.swapaxes(routes, 0, 1)
    router_t = jnp.swapaxes(router, 0, 1)
    rel_bias_t = jnp.swapaxes(rel_bias, 0, 1)
    gain_a, gain_m = gain_attn.reshape(1, WIDTH), gain_moe.reshape(1, WIDTH)
    ids = piece_ids()
    x_slots, o_slots, g_slots, query, long_kv, short_kv, mixed, norm_l, norm_s, resid, probs_t, rnorm_t = forward(
        long_lengths, short_lengths, tokens_in, out_cot, routes_t, gain_a, gain_m, rel_bias_t, router_t,
        jnp.asarray(ids.T), w_query, w_key, w_value, w_out,
    )
    unfold = unfold_matrix()
    row_of = np.arange(640) // SLOTS
    consts = (
        jnp.asarray(unfold, BF16),
        jnp.asarray(unfold.T, BF16),
        jnp.asarray((row_of[:, None] == np.arange(EXPERTS)[None, :]).astype(np.float32)),
        jnp.asarray((np.arange(640) % SLOTS).astype(np.int32)[:, None]),
    )
    dx_back, dg_back, outs, wg_grad, wu_grad, wd_grad, wg_send, wu_send, wd_send = experts(
        x_slots, o_slots, g_slots, consts, own, other
    )
    arrived = [lax.ppermute(part, "row", pairs) for part in (wg_send, wu_send, wd_send)]
    block_out, tokens_grad, grads, small = backward(
        long_lengths, short_lengths, tokens_in, out_cot, routes, routes_t, gain_a, gain_m, rel_bias_t, router_t,
        jnp.asarray(ids), w_query, w_key, w_value, w_out, resid, probs_t, rnorm_t, query, long_kv, short_kv, mixed,
        norm_l, norm_s, dx_back, dg_back, outs,
    )
    grads, small = sum_over_devices(grads, small)
    grads = grads.reshape(4, 8, WIDTH, 128).transpose(0, 2, 1, 3).reshape(4, WIDTH, WIDTH).astype(F32)
    expert_grads = [
        mine + part.astype(F32) for mine, part in zip((wg_grad, wu_grad, wd_grad), arrived)
    ]
    totals = small[288]
    statistics = jnp.sqrt(totals[0:3] / (totals[3] * WIDTH))
    router_grad = small[0:256].reshape(8, EXPERTS, 128).transpose(1, 0, 2).reshape(EXPERTS, WIDTH)
    return (
        block_out,
        tokens_grad,
        small[256:264].reshape(WIDTH),
        grads[0],
        grads[1],
        grads[2],
        grads[3],
        jnp.swapaxes(small[272:288, 0:32], 0, 1),
        small[264:272].reshape(WIDTH),
        jnp.swapaxes(router_grad, 0, 1),
        jnp.swapaxes(expert_grads[0], 0, 1)[None],
        jnp.swapaxes(expert_grads[1], 0, 1)[None],
        expert_grads[2][None],
        statistics,
    )


def solution(mesh):
    tokens = P(("row", "col"), None)
    whole = P()
    wide = P("col", None, "row")
    tall = P("col", "row", None)
    return jax.shard_map(
        per_device,
        mesh=mesh,
        in_specs=(tokens, tokens, P("col"), P(("row", "col")), tokens) + (whole,) * 8 + (wide, wide, tall),
        out_specs=(tokens, tokens) + (whole,) * 8 + (wide, wide, tall, whole),
        check_vma=False,
    )
```

time: 752 us -> 542 us (0.72)
  Pallas kernels: 100 us -> 464 us
  local copies, waits for them, and re-layouts: 225 us -> 38.1 us
  matrix products: 162 us -> 0 us
  waiting for transfers between devices: 159 us -> 0.02 us
  starting transfers between devices: 30.5 us -> 6.24 us
  other arithmetic: 41.5 us -> 20.8 us
  between operations: 20.1 us -> 3.19 us
    pallas_call x0 -> x3, Pallas kernels: none -> 386 us  [the longest x1 178 us: forward(): pl.pallas_call(forward_kernel, out_shape=(out((2, PIECES, QUARTER), BF16)...]
    dot_general x44 -> x0, matrix products: 162 us -> none  [the longest x1 17.5 us: per_device(): jnp.einsum('sjcd,jfd->sjcf', d_received, down_full, preferred_element_typ...]
    unnamed x224 -> x21, local copies, waits for them, and re-layouts: 145 us -> 6.02 us
    all_gather x5 -> x0, waiting for transfers between devices: 137 us -> none  [the longest x1 53 us: per_device(): lax.all_gather(w_down, 'row', axis=1, tiled=True)]
    all_to_all x4 -> x0, starting transfers between devices: 29.5 us -> none  [the longest x1 8.99 us: per_device(): lax.all_to_all(buffer.reshape(experts, capacity, width), 'col', split_axi...]
    pallas_call x1, Pallas kernels: 100 us -> 78.4 us  [sum_over_devices(): pl.pallas_call(sum_kernel, out_shape=(jax.ShapeDtypeStruct((2 * SUM_ROWS[...]
    all_to_all x4 -> x0, waiting for transfers between devices: 20.6 us -> none  [the longest x1 8.58 us: per_device(): lax.all_to_all(buffer.reshape(experts, capacity, width), 'col', split_axi...]
    another operation x5 -> x0, local copies, waits for them, and re-layouts: 15.9 us -> none  [the longest x4 15.9 us: per_device(): jnp.stack([d_w_query, d_w_key, d_w_value, d_w_out]).astype(jnp.bfloat16)]
  transfers between devices with their start and end apart: 14 -> 6, of which waited for: 7 -> 0; matrix products, arithmetic and copies ran while one was open for 50% -> 10% of each run, Pallas kernels for 14% -> 73%
where the time goes in v2:
time: 542 us; the launch traced here: 533 us
  Pallas kernels  464 us (86%)
  local copies, waits for them, and re-layouts  38.1 us (7%)
  other arithmetic  20.8 us (4%)
  starting transfers between devices  6.24 us (1%)
    pallas_call x1, Pallas kernels, forward(): pl.pallas_call(forward_kernel, out_shape=(out((2, PIECES, QUARTER), BF16)...  178 us
    pallas_call x1, Pallas kernels, backward(): pl.pallas_call(backward_kernel, out_shape=(out((ROWS, WIDTH), F32), out((...  132 us
    pallas_call x1, Pallas kernels, sum_over_devices(): pl.pallas_call(sum_kernel, out_shape=(jax.ShapeDtypeStruct((2 * SUM_ROWS[...  78.4 us
    pallas_call x1, Pallas kernels, experts(): pl.pallas_call(expert_kernel, out_shape=(out((PIECES, QUARTER), BF16), ou...  76.7 us
    slice x2, local copies, waits for them, and re-layouts, per_device(): grads[3]  11.2 us
    convert_element_type x1, other arithmetic, per_device(): grads.reshape(4, 8, WIDTH, 128).transpose(0, 2, 1, 3)  11.1 us
  transfers between devices with their start and end apart: 6, of which 0 were waited for; matrix products, arithmetic and copies ran while one was open for 10% of the time, Pallas kernels for 73%

profile of v2, /device:TPU:1, one launch (start us, length us, event | category | flops | bytes accessed | tf_op | source)
XLA Modules:
  0.0 532.8 jit_solution(18086901032716680188)
XLA Ops:
  0.6 2.2 collective-permute-start
  2.9 0.1 collective-permute-start.1
  2.9 1.4 collective-permute-start.2
  5.6 1.5 copy.36.routes
  7.1 177.5 %forward_and_dispatch.1 = (bf16[2,2560,256]{2,1,0:T(8,128)(2,1)}, bf16[2,2560,256]{2,1,0:T(8,128)(2,1)}, f32[2,32,8,128]{3,2,1,0:T(8,128)}, bf16[256,1024]{1,0:T...) custom-call(s32[1]{0:T(128)S(6)} %copy.55.long_len, ...), custom_call_target="tpu_custom_call" | custom-call | tf_op jit(solution)/shard_map/forward_and_dispatch/pallas_call | solution.py:408
  184.7 1.1 copy-done.5
  185.7 0.5 copy-done.6
  186.2 76.7 %experts.1 = (bf16[2560,256]{1,0:T(8,128)(2,1)}, f32[32,8,128]{2,1,0:T(8,128)}, bf16[2,2560,256]{2,1,0:T(8,128)(2,1)}, f32[704,1024]{1,0:T(8,128)}, f32[704,1024...) custom-call(bf16[2,2560,256]{2,1,0:T(8,128)(2,1)} %get-tuple-element, ...), custom_call_target="tpu_custom_call" | custom-call | tf_op jit(solution)/shard_map/experts/pallas_call | solution.py:711
  263.0 1.1 collective-permute-start.3
  264.0 0.5 collective-permute-start.4
  264.5 1.0 collective-permute-start.5
  265.5 131.7 %backward_local.1 = (f32[256,1024]{1,0:T(8,128)}, f32[256,1024]{1,0:T(8,128)}, bf16[32768,128]{1,0:T(8,128)(2,1)}, f32[1024,128]{1,0:T(8,128)}) custom-call(s32[1]{0:T(128)S(6)} %copy.55.long_len, s32[1]{0:T(128)S(6)} %copy.56.short_len, bf16[256,1024]{1,0:T(8,128)(2,1)} %tokens.3, bf16[256,1024]{1,0:T(8,128)(2,1)} %cot.3, s32[256,2]{1,0:T(8,128)} %copy.36.routes, ...), custom_call_target="tpu_custom_call" | custom-call | tf_op jit(solution)/shard_map/backward_local/pallas_call | solution.py:1086
  397.2 1.0 copy-done
  398.3 78.4 %sum_over_devices.1 = (bf16[32768,128]{1,0:T(8,128)(2,1)}, f32[1024,128]{1,0:T(8,128)S(1)}) custom-call(bf16[32768,128]{1,0:T(8,128)(2,1)} %get-tuple-element.58.refs_0_, f32[1024,128]{1,0:T(8,128)S(1)} %copy-done), custom_call_target="tpu_custom_call" | custom-call | tf_op jit(solution)/shard_map/sum_over_devices/pallas_call | solution.py:1351
  476.7 11.1 %convert_bitcast_fusion = f32[4,1024,8,128]{3,1,2,0:T(8,128)} fusion(bf16[4,8,1024,128]{3,2,1,0:T(8,128)(2,1)} %bitcast.65), kind=kLoop, calls=%fused_computation | loop fusion | flops 4194304 | bytes 25165824 | tf_op jit(solution)/shard_map/convert_element_type | solution.py:1401
  487.8 8.7 %fusion = (f32[1,1024,8,128]{3,1,2,0:T(8,128)S(1)}, f32[1,1024,8,128]{3,1,2,0:T(8,128)}, f32[1,1024,8,128]{3,1,2,0:T(8,128)S(1)}, f32[1,1024,8,128]{3,1,2,0:T(8,128)S(1)}) fusion(f32[4,1024,8,128]{3,1,2,0:T(8,128)} %convert_bitcast_fusion), kind=kLoop, calls=%fused_computation.13 | loop fusion | bytes 33554432 | tf_op jit(solution)/shard_map/slice | solution.py:1415
  496.5 2.4 copy.40
  499.0 2.4 copy.39
  501.4 5.5 %copy_bitcast_fusion = (f32[1024,1024]{1,0:T(8,128)}, f32[1024,1024]{1,0:T(8,128)}) fusion(f32[128,8,8,128]{3,2,1,0:T(8,128)S(1)} %bitcast.63, f32[128,8,8,128]{3,2,1,0:T(8,128)S(1)} %bitcast.64), kind=kLoop, calls=%fused_computation.1 | loop fusion | bytes 16777216 | tf_op jit(solution)/shard_map/squeeze | solution.py:1415
  506.9 0.6 slice.48
  507.5 0.7 copy.52
  508.2 2.4 copy.38
  510.6 2.7 copy.37
  513.9 0.6 slice_bitcast_fusion.1
  514.5 0.5 sqrt_bitcast_fusion
  515.1 0.6 slice_bitcast_fusion
  515.7 5.5 %copy_bitcast_fusion.2 = (f32[1024,1024]{1,0:T(8,128)}, f32[1024,1024]{1,0:T(8,128)}) fusion(f32[128,8,8,128]{3,2,1,0:T(8,128)S(1)} %bitcast.61, f32[128,8,8,128]{3,2,1,0:T(8,128)S(1)} %bitcast.62), kind=kLoop, calls=%fused_computation.3 | loop fusion | bytes 16777216 | tf_op jit(solution)/shard_map/squeeze | solution.py:1413
  521.1 3.6 add_bitcast_fusion.2
  524.7 3.6 add_bitcast_fusion.1
  528.3 2.1 add_bitcast_fusion
  530.4 1.0 copy.57
  531.4 1.0 copy.58
  (22 shorter events, 0.1 us)
Async XLA Ops:
  0.6 184.0 %collective-permute-start = (bf16[704,1024]{1,0:T(8,128)(2,1)}, bf16[704,1024]{1,0:T(8,128)(2,1)S(1)}, u32[]{:S(2)}, u32[]{:S(2)}) collective-permute-start(bf16[704,1024]{1,0:T(8,128)(2,1)} %bitcast.66), channel_id=1, source_target_pairs={{0,32},{32,0},{64,96},{96,64},{1,33},{33,1},{65,97},{97,65},{2,34}... | collective-permute-start | bytes 4325384 | tf_op jit(solution)/shard_map/ppermute | solution.py:1373
  2.9 181.8 %collective-permute-start.1 = (bf16[704,1024]{1,0:T(8,128)(2,1)}, bf16[704,1024]{1,0:T(8,128)(2,1)S(1)}, u32[]{:S(2)}, u32[]{:S(2)}) collective-permute-start(bf16[704,1024]{1,0:T(8,128)(2,1)} %bitcast.68), channel_id=1, source_target_pairs={{0,32},{32,0},{64,96},{96,64},{1,33},{33,1},{65,97},{97,65},{2,34}... | collective-permute-start | bytes 4325384 | tf_op jit(solution)/shard_map/ppermute | solution.py:1373
  2.9 181.7 %collective-permute-start.2 = (bf16[704,1024]{1,0:T(8,128)(2,1)}, bf16[704,1024]{1,0:T(8,128)(2,1)}, u32[]{:S(2)}, u32[]{:S(2)}) collective-permute-start(bf16[704,1024]{1,0:T(8,128)(2,1)} %bitcast.70), channel_id=1, source_target_pairs={{0,32},{32,0},{64,96},{96,64},{1,33},{33,1},{65,97},{97,65},{2,34}... | collective-permute-start | bytes 4325384 | tf_op jit(solution)/shard_map/ppermute | solution.py:1373
  184.6 1.1 copy-start.5
  184.7 1.6 copy-start.6
  263.0 258.2 %collective-permute-start.3 = (bf16[704,1024]{1,0:T(8,128)(2,1)}, bf16[704,1024]{1,0:T(8,128)(2,1)}, u32[]{:S(2)}, u32[]{:S(2)}) collective-permute-start(bf16[704,1024]{1,0:T(8,128)(2,1)} %get-tuple-element.63), channel_id=1, source_target_pairs={{0,32},{32,0},{64,96},{96,64},{1,33},{33,1},{65,97},{97,65},{2,34}... | collective-permute-start | bytes 4325384 | tf_op jit(solution)/shard_map/ppermute | solution.py:1394
  264.0 260.7 %collective-permute-start.4 = (bf16[704,1024]{1,0:T(8,128)(2,1)}, bf16[704,1024]{1,0:T(8,128)(2,1)}, u32[]{:S(2)}, u32[]{:S(2)}) collective-permute-start(bf16[704,1024]{1,0:T(8,128)(2,1)} %get-tuple-element.65), channel_id=1, source_target_pairs={{0,32},{32,0},{64,96},{96,64},{1,33},{33,1},{65,97},{97,65},{2,34}... | collective-permute-start | bytes 4325384 | tf_op jit(solution)/shard_map/ppermute | solution.py:1394
  264.5 263.8 %collective-permute-start.5 = (bf16[704,1024]{1,0:T(8,128)(2,1)}, bf16[704,1024]{1,0:T(8,128)(2,1)S(1)}, u32[]{:S(2)}, u32[]{:S(2)}) collective-permute-start(bf16[704,1024]{1,0:T(8,128)(2,1)} %get-tuple-element.67), channel_id=1, source_target_pairs={{0,32},{32,0},{64,96},{96,64},{1,33},{33,1},{65,97},{97,65},{2,34}... | collective-permute-start | bytes 4325384 | tf_op jit(solution)/shard_map/ppermute | solution.py:1394
  397.2 1.0 copy-start
  496.5 2.5 copy-start.1
  515.7 5.5 %copy-start.4 = (f32[704,1024]{1,0:T(8,128)S(1)}, f32[704,1024]{1,0:T(8,128)}, u32[]{:S(2)}) copy-start(f32[704,1024]{1,0:T(8,128)} %get-tuple-element.62) | copy-start | bytes 8650756
  521.1 3.6 copy-start.3
  524.7 3.6 copy-start.2
  528.3 2.1 copy-start.8
  528.3 3.1 copy-start.7

commit v3 on v2

--- a/solution.py
+++ b/solution.py
@@ -20,7 +20,11 @@
 PIECES = EXPERTS * FOLDED
 TABLE = 640
 SHARD = 704
-HALF = 2 * SHARD
+PADDED = 768
+EARLY_DOWN = 352
+GRAD_ROWS = 3 * SHARD
+GRAD_EARLY = 528
+GRAD_LATE = GRAD_ROWS - 2 * GRAD_EARLY
 
 bucket_edges = (1, 2, 3, 4, 5, 6, 7, 8, 12, 16, 23, 32, 46, 64, 91)
 norm_eps = 1e-06
@@ -106,10 +110,10 @@
 
 
 def forward_kernel(
-    long_len, short_len, tokens, cot, routes_t, gain_a, gain_m, rel_bias_t, router_t, ids, wq, wk, wv, wo,
-    x_slots, o_slots, g_slots, query, long_kv, short_kv, mixed, norm_l, norm_s, resid, probs_t, rnorm_t,
+    long_len, short_len, tokens, cot, routes_t, gain_a, gain_m, rel_bias_t, router_t, ids, wq, wk, wv, wo, wg_own, wu_own, wd_own,
+    x_slots, o_slots, g_slots, wg_mate, wu_mate, wd_mate, query, long_kv, short_kv, mixed, norm_l, norm_s, resid, probs_t, rnorm_t,
     normed, buffer_o, buffer_x, gate_out, table_l, table_s,
-    o_send, o_recv, x_send, x_recv, g_send, g_recv, own_sem, kv_send, kv_recv, t_send, t_recv,
+    o_send, o_recv, x_send, x_recv, g_send, g_recv, own_sem, kv_send, kv_recv, t_send, t_recv, w_send, w_recv,
 ):
     row = lax.axis_index("row")
     col = lax.axis_index("col")
@@ -228,6 +232,18 @@
 
     for step in (1, 2, 3):
         kv_move(step).start()
+
+    partner = row + 1 - 2 * lax.rem(row, 2)
+    weight_moves = [
+        pltpu.make_async_remote_copy(
+            source, target, w_send.at[i], w_recv.at[i], device_id=(partner, col), device_id_type=MESH_ID
+        )
+        for i, (source, target) in enumerate(
+            ((wg_own, wg_mate), (wu_own, wu_mate), (wd_own.at[pl.ds(0, EARLY_DOWN)], wd_mate))
+        )
+    ]
+    for move in weight_moves:
+        move.start()
 
     dispatch(cot, buffer_o, o_slots, o_send, o_recv, own_sem.at[0])
 
@@ -399,9 +415,11 @@
 
     lax.fori_loop(0, 8, wait_x, 0)
     g_move.wait()
-
-
-def forward(long_lengths, short_lengths, tokens, cot, routes_t, gain_a, gain_m, rel_bias_t, router_t, ids, wq, wk, wv, wo):
+    for move in weight_moves:
+        move.wait()
+
+
+def forward(long_lengths, short_lengths, tokens, cot, routes_t, gain_a, gain_m, rel_bias_t, router_t, ids, wq, wk, wv, wo, wg, wu, wd):
     def out(shape, dtype):
         return jax.ShapeDtypeStruct(shape, dtype)
 
@@ -411,6 +429,9 @@
             out((2, PIECES, QUARTER), BF16),
             out((2, PIECES, QUARTER), BF16),
             out((2, EXPERTS, 8, 128), F32),
+            out((SHARD, WIDTH), BF16),
+            out((SHARD, WIDTH), BF16),
+            out((EARLY_DOWN, WIDTH), BF16),
             out((ROWS, WIDTH), BF16),
             out((4, LONG, 2 * WIDTH), BF16),
             out((LONG, 2 * WIDTH), BF16),
@@ -421,8 +442,8 @@
             out((EXPERTS, ROWS), F32),
             out((1, ROWS), F32),
         ),
-        in_specs=[SMEM_SPEC] * 2 + [VMEM_SPEC] * 12,
-        out_specs=[HBM_SPEC] * 3 + [VMEM_SPEC] * 9,
+        in_specs=[SMEM_SPEC] * 2 + [VMEM_SPEC] * 12 + [HBM_SPEC] * 3,
+        out_specs=[HBM_SPEC] * 6 + [VMEM_SPEC] * 9,
         scratch_shapes=[
             pltpu.VMEM((ROWS, WIDTH), BF16),
             pltpu.VMEM((PIECES, QUARTER), BF16),
@@ -441,25 +462,33 @@
             DMA((3,)),
             DMA((10,)),
             DMA((10,)),
+            DMA((3,)),
+            DMA((3,)),
         ],
         compiler_params=pltpu.CompilerParams(
             collective_id=1, has_side_effects=True, vmem_limit_bytes=56 * 1024 * 1024
         ),
         name="forward_and_dispatch",
-    )(long_lengths, short_lengths, tokens, cot, routes_t, gain_a, gain_m, rel_bias_t, router_t, ids, wq, wk, wv, wo)
+    )(
+        long_lengths, short_lengths, tokens, cot, routes_t, gain_a, gain_m, rel_bias_t, router_t, ids, wq, wk, wv, wo,
+        wg, wu, wd,
+    )
 
 
 def expert_kernel(
     x_slots, o_slots, g_slots, unfold, fold, row_hot, slot_of, wg_own, wu_own, wd_own, wg_mate, wu_mate, wd_mate,
-    dx_back, dg_back, outs, wg_grad, wu_grad, wd_grad, wg_send, wu_send, wd_send,
-    stage, xs, os, dys, wg, wu, wd, act, dg, du, part, arrived, gate_part, gate_arrived, gate_out, grad_stage, grad_half,
-    stage_sem, weight_sem, t_send, t_recv, m_send, m_recv, r_send, r_recv, own_sem, out_sem,
+    dx_back, dg_back, outs, grad_own, grad_send,
+    stage, xs, os, dys, wg, wu, wd, act, dg, du, part, arrived, dxs, gate_part, gate_arrived, gate_out, grad_stage,
+    grad_half, stage_sem, weight_sem, late_send, late_recv, t_send, t_recv, m_send, m_recv, r_send, r_recv, own_sem,
+    out_sem,
 ):
     row = lax.axis_index("row")
     col = lax.axis_index("col")
     mate = 3 - row
+    partner = row + 1 - 2 * lax.rem(row, 2)
     barrier = pltpu.get_barrier_semaphore()
     pl.semaphore_signal(barrier, inc=1, device_id=(mate, col), device_id_type=MESH_ID)
+    pl.semaphore_signal(barrier, inc=1, device_id=(partner, col), device_id_type=MESH_ID)
 
     def greet(step, carry):
         pl.semaphore_signal(barrier, inc=1, device_id=(row, lax.rem(col + step, EXPERTS)), device_id_type=MESH_ID)
@@ -472,12 +501,27 @@
 
     load(x_slots, 1, 0).start()
     load(o_slots, 1, 1).start()
-    weights = []
-    for i, (own, other, held) in enumerate(((wg_own, wg_mate, wg), (wu_own, wu_mate, wu), (wd_own, wd_mate, wd))):
-        for j, source in enumerate((own, other)):
-            copy = pltpu.make_async_copy(source, held.at[pl.ds(j * SHARD, SHARD)], weight_sem.at[i, j])
+    weights = [[], []]
+    for j, sources in enumerate(((wg_own, wu_own, wd_own), (wg_mate, wu_mate, wd_mate))):
+        for i, (source, held) in enumerate(zip(sources, (wg, wu, wd))):
+            copy = pltpu.make_async_copy(
+                source, held.at[pl.ds(j * PADDED, source.shape[0])], weight_sem.at[i, j]
+            )
             copy.start()
-            weights.append(copy)
+            weights[j].append(copy)
+    for held in (wg, wu, wd):
+        for j in range(2):
+            held[j * PADDED + SHARD : (j + 1) * PADDED, :] = jnp.zeros((PADDED - SHARD, WIDTH), BF16)
+    pl.semaphore_wait(barrier, EXPERTS + 1)
+    late = pltpu.make_async_remote_copy(
+        wd_own.at[pl.ds(EARLY_DOWN, SHARD - EARLY_DOWN)],
+        wd.at[pl.ds(PADDED + EARLY_DOWN, SHARD - EARLY_DOWN)],
+        late_send,
+        late_recv,
+        device_id=(partner, col),
+        device_id_type=MESH_ID,
+    )
+    late.start()
 
     def spread(index, target, first):
         def one(group, carry):
@@ -495,108 +539,88 @@
         lanes = iota((640, 128), 1)
         return jnp.sum(jnp.where(lanes == slot_of[...], wide, 0.0), axis=1, keepdims=True)
 
-    def hidden_tile(first, start, width):
-        lanes = pl.ds(start, width)
-        for part_rows in range(2):
-            rows = pl.ds(first + part_rows * 320, 320)
-            x = xs[rows, :]
-            gate_pre = nt(x, wg[lanes, :])
-            up_pre = nt(x, wu[lanes, :])
-            d_act = nt(dys[rows, :], wd[lanes, :])
-            square = gate_pre * gate_pre
-            bend = jnp.tanh(0.7978845608028654 * gate_pre * (1.0 + 0.044715 * square))
-            half = 0.5 * (1.0 + bend)
-            gelu = gate_pre * half
-            slope = half + 0.5 * gate_pre * (1.0 - bend * bend) * (
-                0.7978845608028654 * (1.0 + 3.0 * 0.044715 * square)
-            )
-            act[rows, lanes] = (gelu * up_pre).astype(BF16)
-            du[rows, lanes] = (d_act * gelu).astype(BF16)
-            dg[rows, lanes] = (d_act * up_pre * slope).astype(BF16)
-
-    def first_half(first):
-        def one(i, carry):
-            hidden_tile(first, pl.multiple_of(i * 256, 256), 256)
-            return carry
-
-        lax.fori_loop(0, 5, one, 0)
-        hidden_tile(first, 1280, 128)
-
-    def input_gradient(first, lanes):
+    def take_tokens(which, first):
+        load(x_slots, which, 0).wait()
+        spread(0, xs, first)
+        load(o_slots, which, 1).wait()
+        spread(1, os, first)
         rows = pl.ds(first, 640)
-        return nn(dg[rows, :], wg[:, lanes]) + nn(du[rows, :], wu[:, lanes])
+        dys[rows, :] = (os[rows, :].astype(F32) * gate_column(which)).astype(BF16)
+
+    def hidden_half(first, half):
+        lanes = slice(half * PADDED, (half + 1) * PADDED)
+        rows = slice(first, first + 640)
+        gate_pre = nt(xs[rows, :], wg[lanes, :])
+        up_pre = nt(xs[rows, :], wu[lanes, :])
+        d_act = nt(dys[rows, :], wd[lanes, :])
+        square = gate_pre * gate_pre
+        bend = jnp.tanh(0.7978845608028654 * gate_pre * (1.0 + 0.044715 * square))
+        level = 0.5 * (1.0 + bend)
+        gelu = gate_pre * level
+        slope = level + 0.5 * gate_pre * (1.0 - bend * bend) * (
+            0.7978845608028654 * (1.0 + 3.0 * 0.044715 * square)
+        )
+        act[rows, lanes] = (gelu * up_pre).astype(BF16)
+        du[rows, lanes] = (d_act * gelu).astype(BF16)
+        dg[rows, lanes] = (d_act * up_pre * slope).astype(BF16)
+
+    def input_gradient(first):
+        rows = pl.ds(first, 320)
+        return nn(dg[rows, :], wg[...]) + nn(du[rows, :], wu[...])
 
     def to_mate(source, target, index):
         return pltpu.make_async_remote_copy(
             source, target, t_send.at[index], t_recv.at[index], device_id=(mate, col), device_id_type=MESH_ID
         )
 
+    def fold_group(source, group):
+        rows = pl.ds(pl.multiple_of(group * 80, 16), 80)
+        tall = jnp.concatenate([source[rows, q * QUARTER : (q + 1) * QUARTER] for q in range(4)], axis=0)
+        return nn(fold[...], tall).astype(BF16)
+
     def output_part(first, which):
-        def one(n, total):
-            lanes = block(n, QUARTER)
-            rows = pl.ds(first, 640)
-            value = nn(act[rows, :], wd[:, lanes])
-            stage[0, block(n, 640), :] = value.astype(BF16)
-            return total + jnp.sum(value * os[rows, lanes].astype(F32), axis=1, keepdims=True)
-
-        total = lax.fori_loop(0, 4, one, jnp.zeros((640, 1), F32))
+        totals = []
+        for i in range(2):
+            rows = slice(first + i * 320, first + (i + 1) * 320)
+            value = nn(act[rows, :], wd[...])
+            dxs[i * 320 : (i + 1) * 320, :] = value.astype(BF16)
+            totals.append(jnp.sum(value * os[rows, :].astype(F32), axis=1, keepdims=True))
+        total = jnp.concatenate(totals, axis=0)
 
         def fold_one(group, carry):
-            tall = jnp.concatenate(
-                [stage[0, pl.ds(pl.multiple_of(q * 640 + group * 80, 16), 80), :] for q in range(4)], axis=0
-            )
-            outs[which, block(group, 320), :] = nn(fold[...], tall).astype(BF16)
+            outs[which, block(group, 320), :] = fold_group(dxs, group)
             return carry
 
         lax.fori_loop(0, 8, fold_one, 0)
-        spread_out = jnp.where(iota((640, 128), 1) == slot_of[...], total, 0.0)
+        wide = jnp.where(iota((640, 128), 1) == slot_of[...], total, 0.0)
         return lax.dot_general(
-            row_hot[...], spread_out, (((0,), (0,)), ((), ())), preferred_element_type=F32, precision=highest
-        )
-
-    load(x_slots, 1, 0).wait()
-    spread(0, xs, 640)
+            row_hot[...], wide, (((0,), (0,)), ((), ())), preferred_element_type=F32, precision=highest
+        )
+
+    def part_move(i):
+        rows = pl.ds(i * 320, 320)
+        return to_mate(part.at[rows], arrived.at[rows], i)
+
+    take_tokens(1, 640)
     load(x_slots, 0, 0).start()
-    load(o_slots, 1, 1).wait()
-    spread(1, os, 640)
     load(o_slots, 0, 1).start()
-    dys[640:1280, :] = (os[640:1280, :].astype(F32) * gate_column(1)).astype(BF16)
-    load(x_slots, 0, 0).wait()
-    spread(0, xs, 0)
-    load(o_slots, 0, 1).wait()
-    spread(1, os, 0)
-    dys[0:640, :] = (os[0:640, :].astype(F32) * gate_column(0)).astype(BF16)
-    for copy in weights:
+    for copy in weights[0]:
         copy.wait()
-    first_half(640)
-    pl.semaphore_wait(barrier, EXPERTS)
-
-    def part_move(n):
-        return to_mate(part.at[block(n, 640)], arrived.at[block(n, 640)], n)
-
-    def mate_gradient(n, carry):
-        part[block(n, 640), :] = input_gradient(640, block(n, QUARTER)).astype(BF16)
-        part_move(n).start()
-        return carry
-
-    lax.fori_loop(0, 4, mate_gradient, 0)
+    hidden_half(640, 0)
+    take_tokens(0, 0)
+    for copy in weights[1]:
+        copy.wait()
+    late.wait_recv()
+    hidden_half(640, 1)
+    for i in range(2):
+        part[i * 320 : (i + 1) * 320, :] = input_gradient(640 + i * 320).astype(BF16)
+        part_move(i).start()
+    hidden_half(0, 0)
+    hidden_half(0, 1)
     gate_part[...] = output_part(640, 1)
-    gate_move = to_mate(gate_part, gate_arrived, 4)
+    gate_move = to_mate(gate_part, gate_arrived, 2)
     gate_move.start()
-    first_half(0)
     gates = output_part(0, 0)
-
-    def own_gradient(n, carry):
-        value = input_gradient(0, block(n, QUARTER))
-        part_move(n).wait_recv()
-        stage[1, block(n, 640), :] = (value + arrived[block(n, 640), :].astype(F32)).astype(BF16)
-        return carry
-
-    lax.fori_loop(0, 4, own_gradient, 0)
-    gate_move.wait_recv()
-    gates = gates + gate_arrived[...]
-    for e in range(EXPERTS):
-        gate_out[e] = jnp.broadcast_to(gates[e : e + 1, :], (8, 128))
 
     def message(dest, source):
         return pltpu.make_async_remote_copy(
@@ -620,68 +644,64 @@
 
     own_dx = pltpu.make_async_copy(stage.at[0, block(col, FOLDED)], dx_back.at[block(col, FOLDED)], own_sem.at[0])
     own_dg = pltpu.make_async_copy(gate_out.at[col], dg_back.at[col], own_sem.at[1])
-
-    def return_group(i, carry):
-        group = lax.rem(lax.div(col, 4) + i, 8)
-        tall = jnp.concatenate(
-            [stage[1, pl.ds(pl.multiple_of(q * 640 + group * 80, 16), 80), :] for q in range(4)], axis=0
-        )
-        stage[0, block(group, 320), :] = nn(fold[...], tall).astype(BF16)
-        for j in range(4):
-            dest = group * 4 + j
-
-            @pl.when(dest != col)
-            def _():
-                message(dest, col).start()
-                gate_message(dest, col).start()
-
-            @pl.when(dest == col)
-            def _():
-                own_dx.start()
-                own_dg.start()
-
-        return carry
-
-    lax.fori_loop(0, 8, return_group, 0)
-
-    grads = ((dg, xs, wg_grad, wg_send), (du, xs, wu_grad, wu_send), (act, dys, wd_grad, wd_send))
-
-    def grad_copies(slot, start, width, result, send):
-        copies = []
-        if start < SHARD:
-            rows = min(width, SHARD - start)
-            copies.append((grad_stage.at[slot, pl.ds(0, rows)], result.at[pl.ds(start, rows)], out_sem.at[slot, 0]))
-        if start + width > SHARD:
-            skip = max(0, SHARD - start)
-            copies.append(
-                (
-                    grad_half.at[slot, pl.ds(skip, width - skip)],
-                    send.at[pl.ds(start + skip - SHARD, width - skip)],
-                    out_sem.at[slot, 1],
+    for i in range(2):
+        rows = slice(i * 320, (i + 1) * 320)
+        value = input_gradient(i * 320)
+        part_move(i).wait_recv()
+        dxs[rows, :] = (value + arrived[rows, :].astype(F32)).astype(BF16)
+
+        def return_group(k, carry, i=i):
+            group = i * 4 + lax.rem(lax.div(col, 4) + k, 4)
+            stage[0, block(group, 320), :] = fold_group(dxs, group)
+            for j in range(4):
+                dest = group * 4 + j
+
+                @pl.when(dest != col)
+                def _():
+                    message(dest, col).start()
+
+                @pl.when(dest == col)
+                def _():
+                    own_dx.start()
+
+            return carry
+
+        lax.fori_loop(0, 4, return_group, 0)
+    gate_move.wait_recv()
+    gates = gates + gate_arrived[...]
+    for e in range(EXPERTS):
+        gate_out[e] = jnp.broadcast_to(gates[e : e + 1, :], (8, 128))
+
+    def send_gates(step, carry):
+        gate_message(lax.rem(col + step, EXPERTS), col).start()
+        return carry
+
+    lax.fori_loop(1, EXPERTS, send_gates, 0)
+    own_dg.start()
+
+    pending = [None, None]
+    turn = 0
+    for which, (left, right) in enumerate(((dg, xs), (du, xs), (act, dys))):
+        for half in (1, 0):
+            for n in range(2):
+                lanes = slice(n * 512, (n + 1) * 512)
+                value = tn(left[:, half * PADDED : (half + 1) * PADDED], right[:, lanes])[0:SHARD]
+                slot = turn % 2
+                turn += 1
+                if pending[slot] is not None:
+                    pending[slot].wait()
+                if half == 0:
+                    grad_stage[slot] = value
+                    source, target = grad_stage.at[slot], grad_own
+                else:
+                    grad_half[slot] = value.astype(BF16)
+                    source, target = grad_half.at[slot], grad_send
+                pending[slot] = pltpu.make_async_copy(
+                    source, target.at[pl.ds(which * SHARD, SHARD), pl.ds(n * 512, 512)], out_sem.at[slot]
                 )
-            )
-        return [pltpu.make_async_copy(*copy) for copy in copies]
-
-    pending = [[], []]
-    turn = 0
-    for left, right, result, send in grads:
-        for start in range(0, HALF, 256):
-            width = min(256, HALF - start)
-            slot = turn % 2
-            turn += 1
-            for copy in pending[slot]:
-                copy.wait()
-            value = tn(left[:, start : start + width], right[...])
-            if start < SHARD:
-                grad_stage[slot, 0:width, :] = value
-            if start + width > SHARD:
-                grad_half[slot, 0:width, :] = value.astype(BF16)
-            pending[slot] = grad_copies(slot, start, width, result, send)
-            for copy in pending[slot]:
-                copy.start()
-    for copies in pending:
-        for copy in copies:
-            copy.wait()
+                pending[slot].start()
+    for copy in pending:
+        copy.wait()
 
     def wait_source(step, carry):
         source = lax.rem(col + step, EXPERTS)
@@ -694,62 +714,62 @@
     lax.fori_loop(1, EXPERTS, wait_source, 0)
     own_dx.wait()
     own_dg.wait()
-
-    def wait_parts(n, carry):
-        part_move(n).wait_send()
-        return carry
-
-    lax.fori_loop(0, 4, wait_parts, 0)
+    for i in range(2):
+        part_move(i).wait_send()
     gate_move.wait_send()
+    late.wait_send()
 
 
 def experts(x_slots, o_slots, g_slots, consts, own, other):
     def out(shape, dtype):
         return jax.ShapeDtypeStruct(shape, dtype)
 
-    hidden = (2 * 640, HALF)
+    hidden = (2 * 640, 2 * PADDED)
     return pl.pallas_call(
         expert_kernel,
         out_shape=(
             out((PIECES, QUARTER), BF16),
             out((EXPERTS, 8, 128), F32),
             out((2, PIECES, QUARTER), BF16),
-        )
-        + (out((SHARD, WIDTH), F32),) * 3
-        + (out((SHARD, WIDTH), BF16),) * 3,
+            out((GRAD_ROWS, WIDTH), F32),
+            out((GRAD_ROWS, WIDTH), BF16),
+        ),
         in_specs=[HBM_SPEC] * 2 + [VMEM_SPEC] * 5 + [HBM_SPEC] * 6,
-        out_specs=[HBM_SPEC] * 2 + [VMEM_SPEC] + [HBM_SPEC] * 6,
+        out_specs=[HBM_SPEC] * 2 + [VMEM_SPEC] + [HBM_SPEC] * 2,
         scratch_shapes=[
             pltpu.VMEM((2, PIECES, QUARTER), BF16),
             pltpu.VMEM((1280, WIDTH), BF16),
             pltpu.VMEM((1280, WIDTH), BF16),
             pltpu.VMEM((1280, WIDTH), BF16),
-            pltpu.VMEM((HALF, WIDTH), BF16),
-            pltpu.VMEM((HALF, WIDTH), BF16),
-            pltpu.VMEM((HALF, WIDTH), BF16),
+            pltpu.VMEM((2 * PADDED, WIDTH), BF16),
+            pltpu.VMEM((2 * PADDED, WIDTH), BF16),
+            pltpu.VMEM((2 * PADDED, WIDTH), BF16),
             pltpu.VMEM(hidden, BF16),
             pltpu.VMEM(hidden, BF16),
             pltpu.VMEM(hidden, BF16),
-            pltpu.VMEM((PIECES, QUARTER), BF16),
-            pltpu.VMEM((PIECES, QUARTER), BF16),
+            pltpu.VMEM((640, WIDTH), BF16),
+            pltpu.VMEM((640, WIDTH), BF16),
+            pltpu.VMEM((640, WIDTH), BF16),
             pltpu.VMEM((EXPERTS, 128), F32),
             pltpu.VMEM((EXPERTS, 128), F32),
             pltpu.VMEM((EXPERTS, 8, 128), F32),
-            pltpu.VMEM((2, 256, WIDTH), F32),
-            pltpu.VMEM((2, 256, WIDTH), BF16),
+            pltpu.VMEM((2, SHARD, 512), F32),
+            pltpu.VMEM((2, SHARD, 512), BF16),
             DMA((2,)),
             DMA((3, 2)),
-            DMA((5,)),
-            DMA((5,)),
+            DMA,
+            DMA,
+            DMA((3,)),
+            DMA((3,)),
             DMA((EXPERTS,)),
             DMA((EXPERTS,)),
             DMA((EXPERTS,)),
             DMA((EXPERTS,)),
             DMA((2,)),
-            DMA((2, 2)),
+            DMA((2,)),
         ],
         compiler_params=pltpu.CompilerParams(
-            collective_id=2, has_side_effects=True, vmem_limit_bytes=60 * 1024 * 1024
+            collective_id=2, has_side_effects=True, vmem_limit_bytes=62 * 1024 * 1024
         ),
         name="experts",
     )(x_slots, o_slots, g_slots, *consts, *own, *other)
@@ -757,11 +777,11 @@
 
 def backward_kernel(
     long_len, short_len, tokens, cot, routes, routes_t, gain_a, gain_m, rel_bias_t, router_t, ids_t, wq, wk, wv, wo,
-    resid, probs_t, rnorm_t, query, long_kv, short_kv, mixed, norm_l, norm_s, dx_back, dg_back, outs,
-    block_out, tokens_grad, grads, small,
+    resid, probs_t, rnorm_t, query, long_kv, short_kv, mixed, norm_l, norm_s, dx_back, dg_back, outs, grad_send,
+    block_out, tokens_grad, grads, small, grad_mate,
     total, branch, d_mixed, normed, flipped, d_query, d_kv, d_long, d_arrived, table_l, table_s, diag_l, diag_s,
     turned, out_arrived, out_sum, out_back,
-    t_send, t_recv, kv_send, kv_recv, m_send, m_recv, own_sem,
+    t_send, t_recv, kv_send, kv_recv, m_send, m_recv, own_sem, w_send, w_recv,
 ):
     row = lax.axis_index("row")
     col = lax.axis_index("col")
@@ -781,6 +801,21 @@
         outs.at[1], out_arrived, t_send, t_recv, device_id=(mate, col), device_id_type=MESH_ID
     )
     out_move.start()
+
+    partner = row + 1 - 2 * lax.rem(row, 2)
+
+    def weight_move(index):
+        rows = pl.ds(index * GRAD_EARLY, GRAD_EARLY)
+        return pltpu.make_async_remote_copy(
+            grad_send.at[rows],
+            grad_mate.at[rows],
+            w_send.at[index],
+            w_recv.at[index],
+            device_id=(partner, col),
+            device_id_type=MESH_ID,
+        )
+
+    weight_move(0).start()
 
     def message(dest, source):
         return pltpu.make_async_remote_copy(
@@ -953,6 +988,7 @@
 
     for step in (1, 2, 3):
         kv_move(step).start()
+    weight_move(1).start()
 
     out_move.wait_recv()
 
@@ -1077,6 +1113,8 @@
     for i, tally in enumerate(tallies):
         packed = jnp.where(iota((8, 128), 1) == i, tally, packed)
     small[288:296, :] = packed
+    weight_move(0).wait()
+    weight_move(1).wait()
 
 
 def backward(*args):
@@ -1090,9 +1128,10 @@
             out((ROWS, WIDTH), F32),
             out((2 * SUM_ROWS[0], 128), BF16),
             out((2 * SUM_ROWS[1], 128), F32),
+            out((2 * GRAD_EARLY, WIDTH), BF16),
         ),
-        in_specs=[SMEM_SPEC] * 2 + [VMEM_SPEC] * (len(args) - 2),
-        out_specs=[VMEM_SPEC] * 4,
+        in_specs=[SMEM_SPEC] * 2 + [VMEM_SPEC] * (len(args) - 3) + [HBM_SPEC],
+        out_specs=[VMEM_SPEC] * 4 + [HBM_SPEC],
         scratch_shapes=[
             pltpu.VMEM((ROWS, WIDTH), F32),
             pltpu.VMEM((ROWS, WIDTH), BF16),
@@ -1118,6 +1157,8 @@
             DMA((EXPERTS,)),
             DMA((EXPERTS,)),
             DMA,
+            DMA((2,)),
+            DMA((2,)),
         ],
         compiler_params=pltpu.CompilerParams(
             collective_id=3, has_side_effects=True, vmem_limit_bytes=60 * 1024 * 1024
@@ -1159,12 +1200,15 @@
 
 def sum_kernel(*refs):
     inputs = refs[0:2]
-    results = refs[2:4]
-    held = refs[4:6]
-    other = refs[6:8]
-    slots = refs[8:8 + 3 * len(SUM_PARTS)]
-    load_sem, core_send, core_recv, hop_send, hop_recv, gather_send, gather_recv, copy_sem, last_send, last_recv = refs[
-        8 + 3 * len(SUM_PARTS):
+    grad_send = refs[2]
+    results = refs[3:5]
+    grad_mate = refs[5]
+    refs = refs[6:]
+    held = refs[0:2]
+    other = refs[2:4]
+    slots = refs[4 : 4 + 3 * len(SUM_PARTS)]
+    load_sem, core_send, core_recv, hop_send, hop_recv, gather_send, gather_recv, copy_sem, last_send, last_recv, w_send, w_recv = refs[
+        4 + 3 * len(SUM_PARTS) :
     ]
     row, z, x, core = torus_place()
     place = {"x": x, "y": row, "z": z}
@@ -1254,6 +1298,16 @@
         swaps[p].wait()
         add_rows(kind, first, rows, [(other[kind], first)])
         flight[p] = start_hop(p, 0)
+    partner = row + 1 - 2 * lax.rem(row, 2)
+    weight_move = pltpu.make_async_remote_copy(
+        grad_send.at[pl.ds(2 * GRAD_EARLY, GRAD_LATE)],
+        grad_mate,
+        w_send,
+        w_recv,
+        device_id=(partner, lax.axis_index("col")),
+        device_id_type=MESH_ID,
+    )
+    weight_move.start()
     for level in (1, 2):
         for p in range(count):
             end_hop(p, level - 1, flight[p])
@@ -1320,9 +1374,10 @@
             lasts.append(last)
     for last in lasts:
         last.wait()
-
-
-def sum_over_devices(weights, small):
+    weight_move.wait()
+
+
+def sum_over_devices(weights, small, grad_send):
     scratch = [
         pltpu.VMEM((SUM_ROWS[0], 128), jnp.bfloat16),
         pltpu.VMEM((SUM_ROWS[1], 128), jnp.float32),
@@ -1347,39 +1402,92 @@
         dma((count,)),
         dma((count, 4)),
         dma((count, 4)),
+        dma,
+        dma,
     ]
     return pl.pallas_call(
         sum_kernel,
         out_shape=(
             jax.ShapeDtypeStruct((2 * SUM_ROWS[0], 128), jnp.bfloat16),
             jax.ShapeDtypeStruct((2 * SUM_ROWS[1], 128), jnp.float32),
+            jax.ShapeDtypeStruct((GRAD_LATE, WIDTH), jnp.bfloat16),
         ),
-        in_specs=[pl.BlockSpec(memory_space=pl.ANY)] * 2,
-        out_specs=[pl.BlockSpec(memory_space=pl.ANY)] * 2,
+        in_specs=[pl.BlockSpec(memory_space=pl.ANY)] * 3,
+        out_specs=[pl.BlockSpec(memory_space=pl.ANY)] * 3,
         scratch_shapes=scratch,
         compiler_params=pltpu.CompilerParams(
             collective_id=4, has_side_effects=True, vmem_limit_bytes=48 * 1024 * 1024
         ),
         name="sum_over_devices",
-    )(weights, small)
+    )(weights, small, grad_send)
+
+
+def finish_sums(grads):
+    def kernel(grads_ref, *results):
+        for which, result in enumerate(results):
+            for i in range(8):
+                result[:, i * 128 : (i + 1) * 128] = grads_ref[which, i].astype(F32)
+
+    return pl.pallas_call(
+        kernel,
+        grid=(8,),
+        out_shape=(jax.ShapeDtypeStruct((WIDTH, WIDTH), F32),) * 4,
+        in_specs=[pl.BlockSpec((4, 8, 128, 128), lambda i: (0, 0, i, 0))],
+        out_specs=(pl.BlockSpec((128, WIDTH), lambda i: (i, 0)),) * 4,
+        name="finish_sums",
+    )(grads.reshape(4, 8, WIDTH, 128))
+
+
+def finish_experts(own, early, late):
+    tile = 176
+    early_steps = 2 * GRAD_EARLY // tile
+    per_matrix = SHARD // tile
+
+    def kernel(own_ref, early_ref, late_ref, *results):
+        step = pl.program_id(0)
+        total = own_ref[...] + jnp.where(step < early_steps, early_ref[...], late_ref[...]).astype(F32)
+        for which, result in enumerate(results):
+
+            @pl.when(step // per_matrix == which)
+            def _():
+                result[...] = total
+
+    def spec(index):
+        return pl.BlockSpec((tile, WIDTH), lambda i: (index(i), 0))
+
+    def result_spec(which):
+        return spec(lambda i: jnp.clip(i - which * per_matrix, 0, per_matrix - 1))
+
+    return pl.pallas_call(
+        kernel,
+        grid=(GRAD_ROWS // tile,),
+        out_shape=(jax.ShapeDtypeStruct((SHARD, WIDTH), F32),) * 3,
+        in_specs=[
+            spec(lambda i: i),
+            spec(lambda i: jnp.minimum(i, early_steps - 1)),
+            spec(lambda i: jnp.maximum(i - early_steps, 0)),
+        ],
+        out_specs=tuple(result_spec(which) for which in range(3)),
+        name="finish_experts",
+    )(own, early, late)
 
 
 def per_device(
     tokens_in, out_cot, long_lengths, short_lengths, routes, gain_attn, w_query, w_key, w_value, w_out, rel_bias,
     gain_moe, router, w_gate, w_up, w_down,
 ):
-    pairs = [(0, 1), (1, 0), (2, 3), (3, 2)]
     own = (jnp.swapaxes(w_gate[0], 0, 1), jnp.swapaxes(w_up[0], 0, 1), w_down[0])
-    other = tuple(lax.ppermute(weight, "row", pairs) for weight in own)
     routes_t = jnp.swapaxes(routes, 0, 1)
     router_t = jnp.swapaxes(router, 0, 1)
     rel_bias_t = jnp.swapaxes(rel_bias, 0, 1)
     gain_a, gain_m = gain_attn.reshape(1, WIDTH), gain_moe.reshape(1, WIDTH)
     ids = piece_ids()
-    x_slots, o_slots, g_slots, query, long_kv, short_kv, mixed, norm_l, norm_s, resid, probs_t, rnorm_t = forward(
+    sent = forward(
         long_lengths, short_lengths, tokens_in, out_cot, routes_t, gain_a, gain_m, rel_bias_t, router_t,
-        jnp.asarray(ids.T), w_query, w_key, w_value, w_out,
+        jnp.asarray(ids.T), w_query, w_key, w_value, w_out, *own,
     )
+    x_slots, o_slots, g_slots, *other = sent[:6]
+    query, long_kv, short_kv, mixed, norm_l, norm_s, resid, probs_t, rnorm_t = sent[6:]
     unfold = unfold_matrix()
     row_of = np.arange(640) // SLOTS
     consts = (
@@ -1388,20 +1496,15 @@
         jnp.asarray((row_of[:, None] == np.arange(EXPERTS)[None, :]).astype(np.float32)),
         jnp.asarray((np.arange(640) % SLOTS).astype(np.int32)[:, None]),
     )
-    dx_back, dg_back, outs, wg_grad, wu_grad, wd_grad, wg_send, wu_send, wd_send = experts(
-        x_slots, o_slots, g_slots, consts, own, other
-    )
-    arrived = [lax.ppermute(part, "row", pairs) for part in (wg_send, wu_send, wd_send)]
-    block_out, tokens_grad, grads, small = backward(
+    dx_back, dg_back, outs, grad_own, grad_send = experts(x_slots, o_slots, g_slots, consts, own, other)
+    block_out, tokens_grad, grads, small, grad_early = backward(
         long_lengths, short_lengths, tokens_in, out_cot, routes, routes_t, gain_a, gain_m, rel_bias_t, router_t,
         jnp.asarray(ids), w_query, w_key, w_value, w_out, resid, probs_t, rnorm_t, query, long_kv, short_kv, mixed,
-        norm_l, norm_s, dx_back, dg_back, outs,
+        norm_l, norm_s, dx_back, dg_back, outs, grad_send,
     )
-    grads, small = sum_over_devices(grads, small)
-    grads = grads.reshape(4, 8, WIDTH, 128).transpose(0, 2, 1, 3).reshape(4, WIDTH, WIDTH).astype(F32)
-    expert_grads = [
-        mine + part.astype(F32) for mine, part in zip((wg_grad, wu_grad, wd_grad), arrived)
-    ]
+    grads, small, grad_late = sum_over_devices(grads, small, grad_send)
+    grads = finish_sums(grads)
+    expert_grads = finish_experts(grad_own, grad_early, grad_late)
     totals = small[288]
     statistics = jnp.sqrt(totals[0:3] / (totals[3] * WIDTH))
     router_grad = small[0:256].reshape(8, EXPERTS, 128).transpose(1, 0, 2).reshape(EXPERTS, WIDTH)

time: 542 us -> 444 us (0.82)
  Pallas kernels: 464 us -> 424 us
  local copies, waits for them, and re-layouts: 38.1 us -> 8.87 us
  other arithmetic: 20.8 us -> 0.53 us
  starting transfers between devices: 6.24 us -> 0 us
    pallas_call x1, Pallas kernels: 178 us -> 120 us  [forward(): pl.pallas_call(forward_kernel, out_shape=(out((2, PIECES, QUARTER), BF16)...]
    pallas_call x1, Pallas kernels: 132 us -> 86 us  [backward(): pl.pallas_call(backward_kernel, out_shape=(out((ROWS, WIDTH), F32), out((...]
    pallas_call x1, Pallas kernels: 78.4 us -> 116 us  [sum_over_devices(): pl.pallas_call(sum_kernel, out_shape=(jax.ShapeDtypeStruct((2 * SUM_ROWS[...]
    pallas_call x0 -> x2, Pallas kernels: none -> 22.7 us  [the longest x1 12.1 us: finish_experts(): pl.pallas_call(kernel, grid=(GRAD_ROWS // tile,), out_shape=(jax.ShapeDty...]
    slice x5 -> x0, local copies, waits for them, and re-layouts: 18.7 us -> none  [the longest x2 11.2 us: per_device(): grads[3]]
    convert_element_type x1 -> x0, other arithmetic: 11.1 us -> none  [per_device(): grads.reshape(4, 8, WIDTH, 128).transpose(0, 2, 1, 3)]
    squeeze x2 -> x0, local copies, waits for them, and re-layouts: 10.9 us -> none  [the longest x1 5.47 us: per_device(): grads[3]]
    broadcast_in_dim x3 -> x0, other arithmetic: 9.21 us -> none  [the longest x1 3.57 us: per_device(): jnp.swapaxes(expert_grads[1], 0, 1)[None]]
  transfers between devices with their start and end apart: 6 -> 0, of which waited for: 0 -> 0; matrix products, arithmetic and copies ran while one was open for 10% -> 0% of each run, Pallas kernels for 73% -> 0%
where the time goes in v3:
time: 444 us; the launch traced here: 437 us
  Pallas kernels  424 us (95%)
  local copies, waits for them, and re-layouts  8.87 us (2%)
    pallas_call x1, Pallas kernels, forward(): pl.pallas_call(forward_kernel, out_shape=(out((2, PIECES, QUARTER), BF16)...  120 us
    pallas_call x1, Pallas kernels, sum_over_devices(): pl.pallas_call(sum_kernel, out_shape=(jax.ShapeDtypeStruct((2 * SUM_ROWS[...  116 us
    pallas_call x1, Pallas kernels, backward(): pl.pallas_call(backward_kernel, out_shape=(out((ROWS, WIDTH), F32), out((...  86 us
    pallas_call x1, Pallas kernels, experts(): pl.pallas_call(expert_kernel, out_shape=(out((PIECES, QUARTER), BF16), ou...  79.1 us
    pallas_call x1, Pallas kernels, finish_experts(): pl.pallas_call(kernel, grid=(GRAD_ROWS // tile,), out_shape=(jax.ShapeDty...  12.1 us
    pallas_call x1, Pallas kernels, finish_sums(): pl.pallas_call(kernel, grid=(8,), out_shape=(jax.ShapeDtypeStruct((WIDTH,...  10.7 us

profile of v3, /device:TPU:1, one launch (start us, length us, event | category | flops | bytes accessed | tf_op | source)
XLA Modules:
  0.0 436.6 jit_solution(11949164237450484618)
XLA Ops:
  1.9 1.5 copy.36.routes
  3.4 120.5 %forward_and_dispatch.1 = (bf16[2,2560,256]{2,1,0:T(8,128)(2,1)}, bf16[2,2560,256]{2,1,0:T(8,128)(2,1)}, f32[2,32,8,128]{3,2,1,0:T(8,128)}, bf16[704,1024]{1,0:T...) custom-call(s32[1]{0:T(128)S(6)} %copy.43.long_len, ...), custom_call_target="tpu_custom_call" | custom-call | tf_op jit(solution)/shard_map/forward_and_dispatch/pallas_call | solution.py:426
  123.9 79.1 %experts.1 = (bf16[2560,256]{1,0:T(8,128)(2,1)}, f32[32,8,128]{2,1,0:T(8,128)}, bf16[2,2560,256]{2,1,0:T(8,128)(2,1)}, f32[2112,1024]{1,0:T(8,128)}, bf16[2112,1024]{1,0:T(8,128)(2,1)}) custom-call(bf16[2,2560,256]{2,1,0:T(8,128)(2,1)} %get-tuple-element.58.x_slots, bf16[2,2560,256]{2,1,0:T(8,128)(2,1)} %get-tuple-element.59.o_slots, ...), custom_call_target="tpu_custom_call" | custom-call | tf_op jit(solution)/shard_map/experts/pallas_call | solution.py:728
  203.0 86.0 %backward_local.1 = (f32[256,1024]{1,0:T(8,128)}, f32[256,1024]{1,0:T(8,128)}, bf16[32768,128]{1,0:T(8,128)(2,1)}, f32[1024,128]{1,0:T(8,128)}, bf16[1056,1024]{1,0:T(8,128)(2,1)}) custom-call(s32[1]{0:T(128)S(6)} %copy.43.long_len, s32[1]{0:T(128)S(6)} %copy.44.short_len, bf16[256,1024]{1,0:T(8,128)(2,1)} %tokens.3, bf16[256,1024]{1,0:T(8,128)(2,1)} %cot.3, ...), custom_call_target="tpu_custom_call" | custom-call | tf_op jit(solution)/shard_map/backward_local/pallas_call | solution.py:1124
  289.0 0.0 copy-start.1
  289.0 1.0 copy-done.1
  290.0 115.9 %sum_over_devices.1 = (bf16[32768,128]{1,0:T(8,128)(2,1)}, f32[1024,128]{1,0:T(8,128)S(1)}, bf16[1056,1024]{1,0:T(8,128)(2,1)S(1)}) custom-call(bf16[32768,128]{1,0:T(8,128)(2,1)} %get-tuple-element.70.refs_0_, f32[1024,128]{1,0:T(8,128)S(1)} %copy-done.1, bf16[2112,1024]{1,0:T(8,128)(2,1)} %get-tuple-element.67.grad_send.refs_2_), custom_call_target="tpu_custom_call" | custom-call | tf_op jit(solution)/shard_map/sum_over_devices/pallas_call | solution.py:1408
  405.9 0.0 copy-start
  405.9 1.3 copy-done
  407.2 0.6 slice.28
  408.5 0.5 sqrt_bitcast_fusion
  409.0 12.1 %finish_experts.1 = (f32[704,1024]{1,0:T(8,128)}, f32[704,1024]{1,0:T(8,128)}, f32[704,1024]{1,0:T(8,128)}) custom-call(f32[2112,1024]{1,0:T(8,128)} %get-tuple-element.78.own_ref, bf16[1056,1024]{1,0:T(8,128)(2,1)} %get-tuple-element.79.early_ref, bf16[1056,1024]{1,0:T(8,128)(2,1)} %copy-done), custom_call_target="tpu_custom_call" | custom-call | tf_op jit(solution)/shard_map/finish_experts/pallas_call | solution.py:1461
  421.1 0.6 slice_bitcast_fusion
  421.7 0.6 slice_bitcast_fusion.1
  422.3 0.7 copy.40
  423.0 0.0 copy-start.3
  423.0 10.7 %finish_sums.1 = (f32[1024,1024]{1,0:T(8,128)}, f32[1024,1024]{1,0:T(8,128)}, f32[1024,1024]{1,0:T(8,128)}, f32[1024,1024]{1,0:T(8,128)}) custom-call(bf16[4,8,1024,128]{3,2,1,0:T(8,128)(2,1)} %bitcast.39), custom_call_target="tpu_custom_call" | custom-call | tf_op jit(solution)/shard_map/finish_sums/pallas_call | solution.py:1431
  433.6 0.0 copy-start.2
  433.6 0.0 copy-done.3
  433.6 1.0 copy.45
  434.6 0.6 copy-done.2
  435.2 1.0 copy.46
  (1 shorter events, 0.0 us)
Async XLA Ops:
  289.0 1.0 copy-start.1
  405.9 1.3 copy-start
  423.0 10.7 %copy-start.3 = (f32[256,1024]{1,0:T(8,128)S(1)}, f32[256,1024]{1,0:T(8,128)}, u32[]{:S(2)}) copy-start(f32[256,1024]{1,0:T(8,128)} %get-tuple-element.100) | copy-start | bytes 3145732
  433.6 1.6 copy-start.2

commit v4 on v3

--- a/solution.py
+++ b/solution.py
@@ -22,9 +22,9 @@
 SHARD = 704
 PADDED = 768
 EARLY_DOWN = 352
+FIRST_DOWN = 176
 GRAD_ROWS = 3 * SHARD
-GRAD_EARLY = 528
-GRAD_LATE = GRAD_ROWS - 2 * GRAD_EARLY
+GRAD_PIECES = (528, 208, 224, 224, 224)
 
 bucket_edges = (1, 2, 3, 4, 5, 6, 7, 8, 12, 16, 23, 32, 46, 64, 91)
 norm_eps = 1e-06
@@ -107,6 +107,232 @@
     here = jnp.where(is_long, position + row * LONG, position - LONG)
     limit = jnp.where(is_long, long_len, short_len)
     return (here < limit).astype(F32)
+
+
+SUM_PARTS = (
+    (4096, 0, ("x", "z", "y"), 0),
+    (4096, 4096, ("z", "x", "y"), 0),
+    (3072, 8192, ("x", "y", "z"), 0),
+    (3072, 11264, ("z", "x", "y"), 0),
+    (2048, 14336, ("y", "z", "x"), 0),
+    (512, 0, ("y", "x", "z"), 1),
+)
+SUM_ROWS = (16384, 512)
+SUM_COUNT = len(SUM_PARTS)
+
+
+def torus_place():
+    row = lax.axis_index("row")
+    col = lax.axis_index("col")
+    return row, lax.div(col, 8), lax.rem(lax.div(col, 2), 4), lax.rem(col, 2)
+
+
+def axis_peer(axis, step):
+    row, z, x, core = torus_place()
+    if axis == "y":
+        row = lax.rem(row + step, 4)
+    elif axis == "x":
+        x = lax.rem(x + step, 4)
+    elif axis == "z":
+        z = lax.rem(z + step, 4)
+    else:
+        core = 1 - core
+    return (row, (z * 4 + x) * 2 + core)
+
+
+class SumSteps:
+    def __init__(self, sources, results, other, slots, sems):
+        self.sources, self.results, self.other, self.slots = sources, results, other, slots
+        (
+            self.core_send, self.core_recv, self.hop_send, self.hop_recv, self.gather_send, self.gather_recv,
+            self.copy_sem, self.last_send, self.last_recv,
+        ) = sems
+        row, z, x, self.core = torus_place()
+        self.place = {"x": x, "y": row, "z": z}
+        self.flight = {}
+
+    def base(self, p, levels):
+        rows, first, order, kind = SUM_PARTS[p]
+        base = self.core * SUM_ROWS[kind] + first
+        for done in range(levels):
+            base = base + self.place[order[done]] * (rows // 4 ** (done + 1))
+        return base
+
+    def at(self, kind, start, rows):
+        return pl.ds(pl.multiple_of(start, 8 if kind else 16), rows)
+
+    def add(self, kind, start, rows, terms):
+        if kind:
+            tile = min(rows, 128)
+        else:
+            tile = next(t for t in (512, 384, 256, 192, 128, 64, 48, 32) if rows % t == 0)
+        source = self.sources[kind]
+
+        def body(i, carry):
+            here = self.at(kind, start + i * tile, tile)
+            total = source[here, :].astype(F32)
+            for ref, first in terms:
+                total = total + ref[self.at(kind, first + i * tile, tile), :].astype(F32)
+            source[here, :] = total.astype(source.dtype)
+            return carry
+
+        lax.fori_loop(0, rows // tile, body, 0)
+
+    def swap(self, p):
+        rows, first, order, kind = SUM_PARTS[p]
+        theirs = (1 - self.core) * SUM_ROWS[kind] + first
+        move = pltpu.make_async_remote_copy(
+            self.sources[kind].at[self.at(kind, theirs, rows)],
+            self.other[kind].at[pl.ds(first, rows)],
+            self.core_send.at[p],
+            self.core_recv.at[p],
+            device_id=axis_peer("core", 1),
+            device_id_type=MESH_ID,
+        )
+        move.start()
+        self.flight[p] = [move]
+
+    def hop(self, p, level):
+        rows, first, order, kind = SUM_PARTS[p]
+        for move in self.flight[p]:
+            move.wait()
+        if level == 0:
+            self.add(kind, self.base(p, 0), rows, [(self.other[kind], first)])
+        else:
+            self.end_hop(p, level - 1)
+        size = rows // 4 ** (level + 1)
+        axis = order[level]
+        self.flight[p] = []
+        for step in (1, 2, 3):
+            block_of = lax.rem(self.place[axis] + step, 4)
+            move = pltpu.make_async_remote_copy(
+                self.sources[kind].at[self.at(kind, self.base(p, level) + block_of * size, size)],
+                self.slots[p * 3 + level].at[pl.ds((step - 1) * size, size)],
+                self.hop_send.at[p, level, step - 1],
+                self.hop_recv.at[p, level, step - 1],
+                device_id=axis_peer(axis, step),
+                device_id_type=MESH_ID,
+            )
+            move.start()
+            self.flight[p].append(move)
+
+    def end_hop(self, p, level):
+        rows, first, order, kind = SUM_PARTS[p]
+        size = rows // 4 ** (level + 1)
+        slots = self.slots[p * 3 + level]
+        self.add(kind, self.base(p, level + 1), size, [(slots, step * size) for step in range(3)])
+
+    def gather(self, p, level):
+        rows, first, order, kind = SUM_PARTS[p]
+        for move in self.flight[p]:
+            move.wait()
+        if level == 2:
+            self.end_hop(p, 2)
+        here = self.at(kind, self.base(p, level + 1), rows // 4 ** (level + 1))
+        source = self.sources[kind].at[here] if level == 2 else self.results[kind].at[here]
+        target = self.results[kind].at[here]
+        self.flight[p] = []
+        for step in (1, 2, 3):
+            move = pltpu.make_async_remote_copy(
+                source,
+                target,
+                self.gather_send.at[p, level, step - 1],
+                self.gather_recv.at[p, level, step - 1],
+                device_id=axis_peer(order[level], step),
+                device_id_type=MESH_ID,
+            )
+            move.start()
+            self.flight[p].append(move)
+        if level == 2:
+            keep = pltpu.make_async_copy(source, target, self.copy_sem.at[p])
+            keep.start()
+            self.flight[p].append(keep)
+
+    def last(self, p):
+        rows, first, order, kind = SUM_PARTS[p]
+        size = rows // 4
+        moves = []
+        for index in range(4):
+            if index > 0:
+                self.flight[p][index - 1].wait()
+            block_of = lax.rem(self.place[order[0]] + 4 - index, 4)
+            here = self.results[kind].at[self.at(kind, self.base(p, 0) + block_of * size, size)]
+            move = pltpu.make_async_remote_copy(
+                here,
+                here,
+                self.last_send.at[p, index],
+                self.last_recv.at[p, index],
+                device_id=axis_peer("core", 1),
+                device_id_type=MESH_ID,
+            )
+            move.start()
+            moves.append(move)
+        self.flight[p] = moves
+
+    def end(self, p):
+        for move in self.flight[p]:
+            move.wait()
+
+
+def sum_scratch():
+    scratch = [
+        pltpu.VMEM((SUM_ROWS[0], 128), BF16),
+        pltpu.VMEM((SUM_ROWS[1], 128), F32),
+    ]
+    for rows, first, order, kind in SUM_PARTS:
+        for level in range(3):
+            scratch.append(pltpu.VMEM((3 * rows // 4 ** (level + 1), 128), F32 if kind else BF16))
+    shapes = [(SUM_COUNT,)] * 2 + [(SUM_COUNT, 3, 3)] * 4 + [(SUM_COUNT,)] + [(SUM_COUNT, 4)] * 2
+    return scratch + [DMA(shape) for shape in shapes]
+
+
+def finish_sums(grads):
+    def kernel(grads_ref, *results):
+        for which, result in enumerate(results):
+            for i in range(8):
+                result[:, i * 128 : (i + 1) * 128] = grads_ref[i // 4, which, i % 4].astype(F32)
+
+    return pl.pallas_call(
+        kernel,
+        grid=(4,),
+        out_shape=(jax.ShapeDtypeStruct((WIDTH, WIDTH), F32),) * 4,
+        in_specs=[pl.BlockSpec((2, 4, 4, 256, 128), lambda i: (0, 0, 0, i, 0))],
+        out_specs=(pl.BlockSpec((256, WIDTH), lambda i: (i, 0)),) * 4,
+        name="finish_sums",
+    )(grads.reshape(2, 4, 4, WIDTH, 128))
+
+
+def finish_experts(own, early, late):
+    tile = 352
+    per_matrix = SHARD // tile
+
+    def kernel(own_ref, early_ref, late_ref, *results):
+        step = pl.program_id(0)
+        total = own_ref[...] + jnp.where(step < per_matrix, early_ref[...], late_ref[...]).astype(F32)
+        for which, result in enumerate(results):
+
+            @pl.when(step // per_matrix == which)
+            def _():
+                result[...] = total
+
+    def spec(index):
+        return pl.BlockSpec((tile, WIDTH), lambda i: (index(i), 0))
+
+    def result_spec(which):
+        return spec(lambda i: jnp.clip(i - which * per_matrix, 0, per_matrix - 1))
+
+    return pl.pallas_call(
+        kernel,
+        grid=(GRAD_ROWS // tile,),
+        out_shape=(jax.ShapeDtypeStruct((SHARD, WIDTH), F32),) * 3,
+        in_specs=[
+            spec(lambda i: i),
+            spec(lambda i: jnp.minimum(i, per_matrix - 1)),
+            spec(lambda i: jnp.maximum(i - per_matrix, 0)),
+        ],
+        out_specs=tuple(result_spec(which) for which in range(3)),
+        name="finish_experts",
+    )(own, early, late)
 
 
 def forward_kernel(
@@ -189,6 +415,23 @@
 
     pl.semaphore_wait(barrier, EXPERTS + 2)
 
+    partner = row + 1 - 2 * lax.rem(row, 2)
+    down_pieces = [pl.ds(0, FIRST_DOWN), pl.ds(FIRST_DOWN, EARLY_DOWN - FIRST_DOWN)]
+    weight_moves = [
+        pltpu.make_async_remote_copy(
+            source, target, w_send.at[i], w_recv.at[i], device_id=(partner, col), device_id_type=MESH_ID
+        )
+        for i, (source, target) in enumerate(
+            (
+                (wd_own.at[down_pieces[0]], wd_mate.at[down_pieces[0]]),
+                (wg_own, wg_mate),
+                (wu_own, wu_mate),
+                (wd_own.at[down_pieces[1]], wd_mate.at[down_pieces[1]]),
+            )
+        )
+    ]
+    weight_moves[0].start()
+
     def norm_rows(i, carry):
         rows = block(i, 64)
         x = tokens[rows, :].astype(F32)
@@ -233,16 +476,7 @@
     for step in (1, 2, 3):
         kv_move(step).start()
 
-    partner = row + 1 - 2 * lax.rem(row, 2)
-    weight_moves = [
-        pltpu.make_async_remote_copy(
-            source, target, w_send.at[i], w_recv.at[i], device_id=(partner, col), device_id_type=MESH_ID
-        )
-        for i, (source, target) in enumerate(
-            ((wg_own, wg_mate), (wu_own, wu_mate), (wd_own.at[pl.ds(0, EARLY_DOWN)], wd_mate))
-        )
-    ]
-    for move in weight_moves:
+    for move in weight_moves[1:]:
         move.start()
 
     dispatch(cot, buffer_o, o_slots, o_send, o_recv, own_sem.at[0])
@@ -462,8 +696,8 @@
             DMA((3,)),
             DMA((10,)),
             DMA((10,)),
-            DMA((3,)),
-            DMA((3,)),
+            DMA((4,)),
+            DMA((4,)),
         ],
         compiler_params=pltpu.CompilerParams(
             collective_id=1, has_side_effects=True, vmem_limit_bytes=56 * 1024 * 1024
@@ -477,9 +711,9 @@
 
 def expert_kernel(
     x_slots, o_slots, g_slots, unfold, fold, row_hot, slot_of, wg_own, wu_own, wd_own, wg_mate, wu_mate, wd_mate,
-    dx_back, dg_back, outs, grad_own, grad_send,
+    dx_back, dg_back, outs, grad_own, grad_send, grad_mate,
     stage, xs, os, dys, wg, wu, wd, act, dg, du, part, arrived, dxs, gate_part, gate_arrived, gate_out, grad_stage,
-    grad_half, stage_sem, weight_sem, late_send, late_recv, t_send, t_recv, m_send, m_recv, r_send, r_recv, own_sem,
+    grad_half, grad_first, stage_sem, weight_sem, late_send, late_recv, first_send, first_recv, t_send, t_recv, m_send, m_recv, r_send, r_recv, own_sem,
     out_sem,
 ):
     row = lax.axis_index("row")
@@ -617,6 +851,13 @@
         part_move(i).start()
     hidden_half(0, 0)
     hidden_half(0, 1)
+    for n in range(2):
+        lanes = slice(n * 512, (n + 1) * 512)
+        grad_first[:, lanes] = tn(dg[:, PADDED:], xs[:, lanes])[0:SHARD].astype(BF16)
+    first_move = pltpu.make_async_remote_copy(
+        grad_first, grad_mate, first_send, first_recv, device_id=(partner, col), device_id_type=MESH_ID
+    )
+    first_move.start()
     gate_part[...] = output_part(640, 1)
     gate_move = to_mate(gate_part, gate_arrived, 2)
     gate_move.start()
@@ -679,28 +920,27 @@
     lax.fori_loop(1, EXPERTS, send_gates, 0)
     own_dg.start()
 
-    pending = [None, None]
+    pending = {}
     turn = 0
-    for which, (left, right) in enumerate(((dg, xs), (du, xs), (act, dys))):
-        for half in (1, 0):
-            for n in range(2):
-                lanes = slice(n * 512, (n + 1) * 512)
-                value = tn(left[:, half * PADDED : (half + 1) * PADDED], right[:, lanes])[0:SHARD]
-                slot = turn % 2
-                turn += 1
-                if pending[slot] is not None:
-                    pending[slot].wait()
-                if half == 0:
-                    grad_stage[slot] = value
-                    source, target = grad_stage.at[slot], grad_own
-                else:
-                    grad_half[slot] = value.astype(BF16)
-                    source, target = grad_half.at[slot], grad_send
-                pending[slot] = pltpu.make_async_copy(
-                    source, target.at[pl.ds(which * SHARD, SHARD), pl.ds(n * 512, 512)], out_sem.at[slot]
-                )
-                pending[slot].start()
-    for copy in pending:
+    pairs = ((dg, xs), (du, xs), (act, dys))
+    for which, half in ((1, 1), (2, 1), (0, 0), (1, 0), (2, 0)):
+        left, right = pairs[which]
+        for n in range(2):
+            lanes = slice(n * 512, (n + 1) * 512)
+            value = tn(left[:, half * PADDED : (half + 1) * PADDED], right[:, lanes])[0:SHARD]
+            slot = turn % 2
+            turn += 1
+            if slot in pending:
+                pending[slot].wait()
+            if half == 0:
+                grad_stage[slot] = value
+                source, target = grad_stage.at[slot], grad_own.at[pl.ds(which * SHARD, SHARD), pl.ds(n * 512, 512)]
+            else:
+                grad_half[slot] = value.astype(BF16)
+                source, target = grad_half.at[slot], grad_send.at[pl.ds((which - 1) * SHARD, SHARD), pl.ds(n * 512, 512)]
+            pending[slot] = pltpu.make_async_copy(source, target, out_sem.at[slot])
+            pending[slot].start()
+    for copy in pending.values():
         copy.wait()
 
     def wait_source(step, carry):
@@ -718,6 +958,7 @@
         part_move(i).wait_send()
     gate_move.wait_send()
     late.wait_send()
+    first_move.wait()
 
 
 def experts(x_slots, o_slots, g_slots, consts, own, other):
@@ -732,10 +973,11 @@
             out((EXPERTS, 8, 128), F32),
             out((2, PIECES, QUARTER), BF16),
             out((GRAD_ROWS, WIDTH), F32),
-            out((GRAD_ROWS, WIDTH), BF16),
+            out((2 * SHARD, WIDTH), BF16),
+            out((SHARD, WIDTH), BF16),
         ),
         in_specs=[HBM_SPEC] * 2 + [VMEM_SPEC] * 5 + [HBM_SPEC] * 6,
-        out_specs=[HBM_SPEC] * 2 + [VMEM_SPEC] + [HBM_SPEC] * 2,
+        out_specs=[HBM_SPEC] * 2 + [VMEM_SPEC] + [HBM_SPEC] * 3,
         scratch_shapes=[
             pltpu.VMEM((2, PIECES, QUARTER), BF16),
             pltpu.VMEM((1280, WIDTH), BF16),
@@ -755,8 +997,11 @@
             pltpu.VMEM((EXPERTS, 8, 128), F32),
             pltpu.VMEM((2, SHARD, 512), F32),
             pltpu.VMEM((2, SHARD, 512), BF16),
+            pltpu.VMEM((SHARD, WIDTH), BF16),
             DMA((2,)),
             DMA((3, 2)),
+            DMA,
+            DMA,
             DMA,
             DMA,
             DMA((3,)),
@@ -778,10 +1023,10 @@
 def backward_kernel(
     long_len, short_len, tokens, cot, routes, routes_t, gain_a, gain_m, rel_bias_t, router_t, ids_t, wq, wk, wv, wo,
     resid, probs_t, rnorm_t, query, long_kv, short_kv, mixed, norm_l, norm_s, dx_back, dg_back, outs, grad_send,
-    block_out, tokens_grad, grads, small, grad_mate,
-    total, branch, d_mixed, normed, flipped, d_query, d_kv, d_long, d_arrived, table_l, table_s, diag_l, diag_s,
+    block_out, tokens_grad, grads_sum, small_sum, grad_mate,
+    grads, small, total, branch, d_mixed, normed, flipped, d_query, d_kv, d_long, d_arrived, table_l, table_s, diag_l, diag_s,
     turned, out_arrived, out_sum, out_back,
-    t_send, t_recv, kv_send, kv_recv, m_send, m_recv, own_sem, w_send, w_recv,
+    t_send, t_recv, kv_send, kv_recv, m_send, m_recv, own_sem, w_send, w_recv, *sum_refs,
 ):
     row = lax.axis_index("row")
     col = lax.axis_index("col")
@@ -796,6 +1041,10 @@
 
     lax.fori_loop(1, EXPERTS, greet, 0)
     pl.semaphore_wait(barrier, EXPERTS + 2)
+    slots_end = 2 + 3 * SUM_COUNT
+    sums = SumSteps(
+        (grads, small), (grads_sum, small_sum), sum_refs[0:2], sum_refs[2:slots_end], sum_refs[slots_end:]
+    )
 
     out_move = pltpu.make_async_remote_copy(
         outs.at[1], out_arrived, t_send, t_recv, device_id=(mate, col), device_id_type=MESH_ID
@@ -805,7 +1054,7 @@
     partner = row + 1 - 2 * lax.rem(row, 2)
 
     def weight_move(index):
-        rows = pl.ds(index * GRAD_EARLY, GRAD_EARLY)
+        rows = pl.ds(sum(GRAD_PIECES[:index]), GRAD_PIECES[index])
         return pltpu.make_async_remote_copy(
             grad_send.at[rows],
             grad_mate.at[rows],
@@ -896,19 +1145,25 @@
     def weight_gradient(which, value_of):
         def one(n, carry):
             out = nn(flipped[...], value_of(n)).astype(BF16)
-            first = which * 8192 + n * 2048
+            first = lax.div(n, 2) * SUM_ROWS[0] + which * 4096 + lax.rem(n, 2) * 2048
             grads[pl.ds(pl.multiple_of(first, 1024), 1024), :] = out[:, 0:128]
             grads[pl.ds(pl.multiple_of(first + 1024, 1024), 1024), :] = out[:, 128:256]
             return carry
 
         lax.fori_loop(0, 4, one, 0)
 
+    flip(mixed)
+    weight_gradient(0, lambda n: branch[:, block(n, 256)])
+    sums.swap(0)
+
     def back_mixed(n, carry):
         rows = block(n, 256)
         d_mixed[:, rows] = nt(branch[...], wo[rows, :]).astype(BF16)
         return carry
 
     lax.fori_loop(0, 4, back_mixed, 0)
+
+    sums.hop(0, 0)
 
     place_l = iota((1, TABLE), 1)
     place_l = jnp.where(place_l < 512, place_l, place_l - TABLE) - row * LONG
@@ -989,6 +1244,7 @@
     for step in (1, 2, 3):
         kv_move(step).start()
     weight_move(1).start()
+    sums.hop(0, 1)
 
     out_move.wait_recv()
 
@@ -1022,8 +1278,8 @@
         256,
         norm_s,
     )
-    flip(mixed)
-    weight_gradient(3, lambda n: branch[:, block(n, 256)])
+    sums.hop(0, 2)
+    weight_move(2).start()
     back_l = bucket_hot(iota((1, TABLE), 1) - 127 - row * LONG)
     back_s = bucket_hot(iota((1, 256), 1) - 127)
     small[272:288, 0:32] = nt(diag_l[...], back_l, highest) + nt(diag_s[...], back_s, highest)
@@ -1037,7 +1293,10 @@
 
     lax.fori_loop(0, 4, norm_rows, 0)
     flip(normed)
-    weight_gradient(0, lambda n: d_query[:, block(n, 256)])
+    weight_gradient(1, lambda n: d_query[:, block(n, 256)])
+    sums.swap(1)
+    sums.gather(0, 2)
+    weight_move(3).start()
     for step in (1, 2, 3):
         kv_move(step).wait()
 
@@ -1050,8 +1309,12 @@
         return carry
 
     lax.fori_loop(0, 8, add_kv, 0)
-    weight_gradient(1, lambda n: d_kv[:, block(n, 256)])
-    weight_gradient(2, lambda n: d_kv[:, pl.ds(pl.multiple_of(n * 256 + WIDTH, 256), 256)])
+    sums.hop(1, 0)
+    weight_gradient(2, lambda n: d_kv[:, block(n, 256)])
+    weight_gradient(3, lambda n: d_kv[:, pl.ds(pl.multiple_of(n * 256 + WIDTH, 256), 256)])
+    for part in (2, 3, 4):
+        sums.swap(part)
+    sums.gather(0, 1)
 
     def back_normed(n, carry):
         rows = block(n, 256)
@@ -1060,6 +1323,10 @@
         return carry
 
     lax.fori_loop(0, 4, back_normed, 0)
+    for part in (2, 3, 4):
+        sums.hop(part, 0)
+    weight_move(4).start()
+    sums.hop(1, 1)
     x = tokens[...].astype(F32)
     scale = lax.rsqrt(jnp.mean(x * x, axis=1, keepdims=True) + norm_eps)
     d_normed = total[...]
@@ -1069,6 +1336,9 @@
     d_normed = d_normed * gain_a[...]
     shrink = jnp.mean(d_normed * x, axis=1, keepdims=True)
     tokens_grad[...] = tokens_grad[...] + scale * d_normed - x * (scale * scale * scale * shrink)
+
+    sums.gather(0, 0)
+    sums.hop(1, 2)
 
     def wait_source(step, carry):
         source = lax.rem(col + step, EXPERTS)
@@ -1113,8 +1383,36 @@
     for i, tally in enumerate(tallies):
         packed = jnp.where(iota((8, 128), 1) == i, tally, packed)
     small[288:296, :] = packed
-    weight_move(0).wait()
-    weight_move(1).wait()
+    sums.swap(5)
+
+    for part in (2, 3, 4):
+        sums.hop(part, 1)
+    sums.gather(1, 2)
+    sums.hop(5, 0)
+    sums.last(0)
+    for part in (2, 3, 4):
+        sums.hop(part, 2)
+    sums.gather(1, 1)
+    sums.hop(5, 1)
+    for part in (2, 3, 4):
+        sums.gather(part, 2)
+    sums.gather(1, 0)
+    sums.hop(5, 2)
+    for part in (2, 3, 4):
+        sums.gather(part, 1)
+    sums.last(1)
+    sums.gather(5, 2)
+    for part in (2, 3, 4):
+        sums.gather(part, 0)
+    sums.gather(5, 1)
+    for part in (2, 3, 4):
+        sums.last(part)
+    sums.gather(5, 0)
+    sums.last(5)
+    for part in range(SUM_COUNT):
+        sums.end(part)
+    for index in range(len(GRAD_PIECES)):
+        weight_move(index).wait()
 
 
 def backward(*args):
@@ -1128,11 +1426,13 @@
             out((ROWS, WIDTH), F32),
             out((2 * SUM_ROWS[0], 128), BF16),
             out((2 * SUM_ROWS[1], 128), F32),
-            out((2 * GRAD_EARLY, WIDTH), BF16),
+            out((2 * SHARD, WIDTH), BF16),
         ),
         in_specs=[SMEM_SPEC] * 2 + [VMEM_SPEC] * (len(args) - 3) + [HBM_SPEC],
-        out_specs=[VMEM_SPEC] * 4 + [HBM_SPEC],
+        out_specs=[VMEM_SPEC] * 2 + [HBM_SPEC] * 3,
         scratch_shapes=[
+            pltpu.VMEM((2 * SUM_ROWS[0], 128), BF16),
+            pltpu.VMEM((2 * SUM_ROWS[1], 128), F32),
             pltpu.VMEM((ROWS, WIDTH), F32),
             pltpu.VMEM((ROWS, WIDTH), BF16),
             pltpu.VMEM((ROWS, WIDTH), BF16),
@@ -1157,319 +1457,15 @@
             DMA((EXPERTS,)),
             DMA((EXPERTS,)),
             DMA,
-            DMA((2,)),
-            DMA((2,)),
-        ],
+            DMA((len(GRAD_PIECES),)),
+            DMA((len(GRAD_PIECES),)),
+        ]
+        + sum_scratch(),
         compiler_params=pltpu.CompilerParams(
             collective_id=3, has_side_effects=True, vmem_limit_bytes=60 * 1024 * 1024
         ),
-        name="backward_local",
+        name="backward_and_sums",
     )(*args)
-
-
-SUM_PARTS = (
-    (5120, 0, ("x", "y", "z"), 0),
-    (5120, 5120, ("y", "z", "x"), 0),
-    (6144, 10240, ("z", "x", "y"), 0),
-    (512, 0, ("y", "x", "z"), 1),
-)
-SUM_ROWS = (16384, 512)
-
-
-def torus_place():
-    row = lax.axis_index("row")
-    col = lax.axis_index("col")
-    core = lax.rem(col, 2)
-    x = lax.rem(lax.div(col, 2), 4)
-    z = lax.div(col, 8)
-    return row, z, x, core
-
-
-def axis_peer(axis, step):
-    row, z, x, core = torus_place()
-    if axis == "y":
-        row = lax.rem(row + step, 4)
-    elif axis == "x":
-        x = lax.rem(x + step, 4)
-    elif axis == "z":
-        z = lax.rem(z + step, 4)
-    else:
-        core = 1 - core
-    return (row, (z * 4 + x) * 2 + core)
-
-
-def sum_kernel(*refs):
-    inputs = refs[0:2]
-    grad_send = refs[2]
-    results = refs[3:5]
-    grad_mate = refs[5]
-    refs = refs[6:]
-    held = refs[0:2]
-    other = refs[2:4]
-    slots = refs[4 : 4 + 3 * len(SUM_PARTS)]
-    load_sem, core_send, core_recv, hop_send, hop_recv, gather_send, gather_recv, copy_sem, last_send, last_recv, w_send, w_recv = refs[
-        4 + 3 * len(SUM_PARTS) :
-    ]
-    row, z, x, core = torus_place()
-    place = {"x": x, "y": row, "z": z}
-    barrier = pltpu.get_barrier_semaphore()
-    pl.semaphore_signal(barrier, inc=1, device_id=axis_peer("core", 1), device_id_type=MESH_ID)
-    for axis in ("x", "y", "z"):
-        for step in (1, 2, 3):
-            pl.semaphore_signal(barrier, inc=1, device_id=axis_peer(axis, step), device_id_type=MESH_ID)
-    loads = []
-    for p, (rows, first, order, kind) in enumerate(SUM_PARTS):
-        mine = pl.multiple_of(core * SUM_ROWS[kind] + first, 256)
-        load = pltpu.make_async_copy(
-            inputs[kind].at[pl.ds(mine, rows)], held[kind].at[pl.ds(first, rows)], load_sem.at[p]
-        )
-        load.start()
-        loads.append(load)
-    pl.semaphore_wait(barrier, 10)
-    swaps = []
-    for p, (rows, first, order, kind) in enumerate(SUM_PARTS):
-        yours = pl.multiple_of((1 - core) * SUM_ROWS[kind] + first, 256)
-        swap = pltpu.make_async_remote_copy(
-            inputs[kind].at[pl.ds(yours, rows)],
-            other[kind].at[pl.ds(first, rows)],
-            core_send.at[p],
-            core_recv.at[p],
-            device_id=axis_peer("core", 1),
-            device_id_type=MESH_ID,
-        )
-        swap.start()
-        swaps.append(swap)
-
-    def add_rows(kind, start, rows, terms):
-        if kind == 1:
-            tile = min(rows, 128)
-        else:
-            tile = 80 if rows % 80 == 0 else 96
-            tile = tile * 4 if rows % (tile * 4) == 0 else tile
-
-        def body(i, carry):
-            offset = pl.multiple_of(i * tile, 8 if kind == 1 else 16)
-            here = pl.ds(pl.multiple_of(start + offset, 8 if kind == 1 else 16), tile)
-            total = held[kind][here, :].astype(jnp.float32)
-            for ref, base in terms:
-                total = total + ref[pl.ds(pl.multiple_of(base + offset, 8 if kind == 1 else 16), tile), :].astype(jnp.float32)
-            held[kind][here, :] = total.astype(held[kind].dtype)
-            return carry
-
-        lax.fori_loop(0, rows // tile, body, 0)
-
-    def start_hop(p, level):
-        rows, first, order, kind = SUM_PARTS[p]
-        size = rows // 4 ** (level + 1)
-        base = first
-        for done in range(level):
-            base = base + place[order[done]] * (rows // 4 ** (done + 1))
-        axis = order[level]
-        hops = []
-        for step in (1, 2, 3):
-            block = lax.rem(place[axis] + step, 4)
-            hop = pltpu.make_async_remote_copy(
-                held[kind].at[pl.ds(pl.multiple_of(base + block * size, 8 if kind == 1 else 16), size)],
-                slots[p * 3 + level].at[pl.ds((step - 1) * size, size)],
-                hop_send.at[p, level, step - 1],
-                hop_recv.at[p, level, step - 1],
-                device_id=axis_peer(axis, step),
-                device_id_type=MESH_ID,
-            )
-            hop.start()
-            hops.append(hop)
-        return hops
-
-    def end_hop(p, level, hops):
-        rows, first, order, kind = SUM_PARTS[p]
-        size = rows // 4 ** (level + 1)
-        base = first
-        for done in range(level + 1):
-            base = base + place[order[done]] * (rows // 4 ** (done + 1))
-        for hop in hops:
-            hop.wait()
-        add_rows(kind, base, size, [(slots[p * 3 + level], step * size) for step in range(3)])
-
-    count = len(SUM_PARTS)
-    flight = [None] * count
-    for p in range(count):
-        rows, first, order, kind = SUM_PARTS[p]
-        loads[p].wait()
-        swaps[p].wait()
-        add_rows(kind, first, rows, [(other[kind], first)])
-        flight[p] = start_hop(p, 0)
-    partner = row + 1 - 2 * lax.rem(row, 2)
-    weight_move = pltpu.make_async_remote_copy(
-        grad_send.at[pl.ds(2 * GRAD_EARLY, GRAD_LATE)],
-        grad_mate,
-        w_send,
-        w_recv,
-        device_id=(partner, lax.axis_index("col")),
-        device_id_type=MESH_ID,
-    )
-    weight_move.start()
-    for level in (1, 2):
-        for p in range(count):
-            end_hop(p, level - 1, flight[p])
-            flight[p] = start_hop(p, level)
-
-    def place_of(p, levels):
-        rows, first, order, kind = SUM_PARTS[p]
-        base = first
-        for done in range(levels):
-            base = base + place[order[done]] * (rows // 4 ** (done + 1))
-        return base
-
-    def gather(p, level):
-        rows, first, order, kind = SUM_PARTS[p]
-        size = rows // 4 ** (level + 1)
-        align = 8 if kind == 1 else 16
-        here = pl.multiple_of(place_of(p, level + 1), align)
-        there = pl.multiple_of(place_of(p, level + 1) + core * SUM_ROWS[kind], align)
-        source = held[kind].at[pl.ds(here, size)] if level == 2 else results[kind].at[pl.ds(there, size)]
-        moves = []
-        for step in (1, 2, 3):
-            move = pltpu.make_async_remote_copy(
-                source,
-                results[kind].at[pl.ds(there, size)],
-                gather_send.at[p, level, step - 1],
-                gather_recv.at[p, level, step - 1],
-                device_id=axis_peer(order[level], step),
-                device_id_type=MESH_ID,
-            )
-            move.start()
-            moves.append(move)
-        if level == 2:
-            keep = pltpu.make_async_copy(source, results[kind].at[pl.ds(there, size)], copy_sem.at[p])
-            keep.start()
-            keep.wait()
-        return moves
-
-    for p in range(count):
-        end_hop(p, 2, flight[p])
-        flight[p] = gather(p, 2)
-    for level in (1, 0):
-        for p in range(count):
-            for move in flight[p]:
-                move.wait()
-            flight[p] = gather(p, level)
-    lasts = []
-    for p in range(count):
-        rows, first, order, kind = SUM_PARTS[p]
-        size = rows // 4
-        for index in range(4):
-            if index > 0:
-                flight[p][index - 1].wait()
-            block = lax.rem(place[order[0]] + 4 - index, 4)
-            there = pl.ds(pl.multiple_of(first + block * size + core * SUM_ROWS[kind], 8 if kind == 1 else 16), size)
-            last = pltpu.make_async_remote_copy(
-                results[kind].at[there],
-                results[kind].at[there],
-                last_send.at[p, index],
-                last_recv.at[p, index],
-                device_id=axis_peer("core", 1),
-                device_id_type=MESH_ID,
-            )
-            last.start()
-            lasts.append(last)
-    for last in lasts:
-        last.wait()
-    weight_move.wait()
-
-
-def sum_over_devices(weights, small, grad_send):
-    scratch = [
-        pltpu.VMEM((SUM_ROWS[0], 128), jnp.bfloat16),
-        pltpu.VMEM((SUM_ROWS[1], 128), jnp.float32),
-        pltpu.VMEM((SUM_ROWS[0], 128), jnp.bfloat16),
-        pltpu.VMEM((SUM_ROWS[1], 128), jnp.float32),
-    ]
-    for rows, first, order, kind in SUM_PARTS:
-        for level in range(3):
-            scratch.append(
-                pltpu.VMEM((3 * rows // 4 ** (level + 1), 128), jnp.float32 if kind == 1 else jnp.bfloat16)
-            )
-    count = len(SUM_PARTS)
-    dma = pltpu.SemaphoreType.DMA
-    scratch += [
-        dma((count,)),
-        dma((count,)),
-        dma((count,)),
-        dma((count, 3, 3)),
-        dma((count, 3, 3)),
-        dma((count, 3, 3)),
-        dma((count, 3, 3)),
-        dma((count,)),
-        dma((count, 4)),
-        dma((count, 4)),
-        dma,
-        dma,
-    ]
-    return pl.pallas_call(
-        sum_kernel,
-        out_shape=(
-            jax.ShapeDtypeStruct((2 * SUM_ROWS[0], 128), jnp.bfloat16),
-            jax.ShapeDtypeStruct((2 * SUM_ROWS[1], 128), jnp.float32),
-            jax.ShapeDtypeStruct((GRAD_LATE, WIDTH), jnp.bfloat16),
-        ),
-        in_specs=[pl.BlockSpec(memory_space=pl.ANY)] * 3,
-        out_specs=[pl.BlockSpec(memory_space=pl.ANY)] * 3,
-        scratch_shapes=scratch,
-        compiler_params=pltpu.CompilerParams(
-            collective_id=4, has_side_effects=True, vmem_limit_bytes=48 * 1024 * 1024
-        ),
-        name="sum_over_devices",
-    )(weights, small, grad_send)
-
-
-def finish_sums(grads):
-    def kernel(grads_ref, *results):
-        for which, result in enumerate(results):
-            for i in range(8):
-                result[:, i * 128 : (i + 1) * 128] = grads_ref[which, i].astype(F32)
-
-    return pl.pallas_call(
-        kernel,
-        grid=(8,),
-        out_shape=(jax.ShapeDtypeStruct((WIDTH, WIDTH), F32),) * 4,
-        in_specs=[pl.BlockSpec((4, 8, 128, 128), lambda i: (0, 0, i, 0))],
-        out_specs=(pl.BlockSpec((128, WIDTH), lambda i: (i, 0)),) * 4,
-        name="finish_sums",
-    )(grads.reshape(4, 8, WIDTH, 128))
-
-
-def finish_experts(own, early, late):
-    tile = 176
-    early_steps = 2 * GRAD_EARLY // tile
-    per_matrix = SHARD // tile
-
-    def kernel(own_ref, early_ref, late_ref, *results):
-        step = pl.program_id(0)
-        total = own_ref[...] + jnp.where(step < early_steps, early_ref[...], late_ref[...]).astype(F32)
-        for which, result in enumerate(results):
-
-            @pl.when(step // per_matrix == which)
-            def _():
-                result[...] = total
-
-    def spec(index):
-        return pl.BlockSpec((tile, WIDTH), lambda i: (index(i), 0))
-
-    def result_spec(which):
-        return spec(lambda i: jnp.clip(i - which * per_matrix, 0, per_matrix - 1))
-
-    return pl.pallas_call(
-        kernel,
-        grid=(GRAD_ROWS // tile,),
-        out_shape=(jax.ShapeDtypeStruct((SHARD, WIDTH), F32),) * 3,
-        in_specs=[
-            spec(lambda i: i),
-            spec(lambda i: jnp.minimum(i, early_steps - 1)),
-            spec(lambda i: jnp.maximum(i - early_steps, 0)),
-        ],
-        out_specs=tuple(result_spec(which) for which in range(3)),
-        name="finish_experts",
-    )(own, early, late)
 
 
 def per_device(
@@ -1496,13 +1492,12 @@
         jnp.asarray((row_of[:, None] == np.arange(EXPERTS)[None, :]).astype(np.float32)),
         jnp.asarray((np.arange(640) % SLOTS).astype(np.int32)[:, None]),
     )
-    dx_back, dg_back, outs, grad_own, grad_send = experts(x_slots, o_slots, g_slots, consts, own, other)
-    block_out, tokens_grad, grads, small, grad_early = backward(
+    dx_back, dg_back, outs, grad_own, grad_send, grad_early = experts(x_slots, o_slots, g_slots, consts, own, other)
+    block_out, tokens_grad, grads, small, grad_late = backward(
         long_lengths, short_lengths, tokens_in, out_cot, routes, routes_t, gain_a, gain_m, rel_bias_t, router_t,
         jnp.asarray(ids), w_query, w_key, w_value, w_out, resid, probs_t, rnorm_t, query, long_kv, short_kv, mixed,
         norm_l, norm_s, dx_back, dg_back, outs, grad_send,
     )
-    grads, small, grad_late = sum_over_devices(grads, small, grad_send)
     grads = finish_sums(grads)
     expert_grads = finish_experts(grad_own, grad_early, grad_late)
     totals = small[288]
@@ -1512,10 +1507,10 @@
         block_out,
         tokens_grad,
         small[256:264].reshape(WIDTH),
-        grads[0],
         grads[1],
         grads[2],
         grads[3],
+        grads[0],
         jnp.swapaxes(small[272:288, 0:32], 0, 1),
         small[264:272].reshape(WIDTH),
         jnp.swapaxes(router_grad, 0, 1),

time: 444 us -> 387 us (0.87)
  Pallas kernels: 424 us -> 366 us
    pallas_call x2 -> x1, Pallas kernels: 127 us -> 9.89 us  [finish_sums(): pl.pallas_call(kernel, grid=(4,), out_shape=(jax.ShapeDtypeStruct((WIDTH,...]
    pallas_call x1, Pallas kernels: 86 us -> 151 us  [backward(): pl.pallas_call(backward_kernel, out_shape=(out((ROWS, WIDTH), F32), out((...]
where the time goes in v4:
time: 387 us; the launch traced here: 380 us
  Pallas kernels  366 us (95%)
  local copies, waits for them, and re-layouts  9.46 us (2%)
    pallas_call x1, Pallas kernels, backward(): pl.pallas_call(backward_kernel, out_shape=(out((ROWS, WIDTH), F32), out((...  151 us
    pallas_call x1, Pallas kernels, forward(): pl.pallas_call(forward_kernel, out_shape=(out((2, PIECES, QUARTER), BF16)...  118 us
    pallas_call x1, Pallas kernels, experts(): pl.pallas_call(expert_kernel, out_shape=(out((PIECES, QUARTER), BF16), ou...  77 us
    pallas_call x1, Pallas kernels, finish_sums(): pl.pallas_call(kernel, grid=(4,), out_shape=(jax.ShapeDtypeStruct((WIDTH,...  9.89 us
    pallas_call x1, Pallas kernels, finish_experts(): pl.pallas_call(kernel, grid=(GRAD_ROWS // tile,), out_shape=(jax.ShapeDty...  9.63 us

profile of v4, /device:TPU:1, one launch (start us, length us, event | category | flops | bytes accessed | tf_op | source)
XLA Modules:
  0.0 379.6 jit_solution(8751451230388633936)
XLA Ops:
  1.9 1.5 copy.36.routes
  3.4 118.3 %forward_and_dispatch.1 = (bf16[2,2560,256]{2,1,0:T(8,128)(2,1)}, bf16[2,2560,256]{2,1,0:T(8,128)(2,1)}, f32[2,32,8,128]{3,2,1,0:T(8,128)}, bf16[704,1024]{1,0:T...) custom-call(s32[1]{0:T(128)S(6)} %copy.43.long_len, ...), custom_call_target="tpu_custom_call" | custom-call | tf_op jit(solution)/shard_map/forward_and_dispatch/pallas_call | solution.py:660
  121.7 77.0 %experts.1 = (bf16[2560,256]{1,0:T(8,128)(2,1)}, f32[32,8,128]{2,1,0:T(8,128)}, bf16[2,2560,256]{2,1,0:T(8,128)(2,1)}, f32[2112,1024]{1,0:T(8,128)}, bf16[1408,1...) custom-call(bf16[2,2560,256]{2,1,0:T(8,128)(2,1)} %get-tuple-element.56.x_slots, ...), custom_call_target="tpu_custom_call" | custom-call | tf_op jit(solution)/shard_map/experts/pallas_call | solution.py:969
  198.7 151.2 %backward_and_sums.1 = (f32[256,1024]{1,0:T(8,128)}, f32[256,1024]{1,0:T(8,128)}, bf16[32768,128]{1,0:T(8,128)(2,1)}, f32[1024,128]{1,0:T(8,128)}, bf16[1408,1024]{1,0:T(8,128)(2,1)}) custom-call(s32[1]{0:T(128)S(6)} %copy.43.long_len, s32[1]{0:T(128)S(6)} %copy.44.short_len, bf16[256,1024]{1,0:T(8,128)(2,1)} %tokens.3, bf16[256,1024]{1,0:T(8,128)(2,1)} %cot.3, ...), custom_call_target="tpu_custom_call" | custom-call | tf_op jit(solution)/shard_map/backward_and_sums/pallas_call | solution.py:1422
  349.8 1.3 slice.28
  351.7 1.2 sqrt_bitcast_fusion
  352.9 9.6 %finish_experts.1 = (f32[704,1024]{1,0:T(8,128)}, f32[704,1024]{1,0:T(8,128)}, f32[704,1024]{1,0:T(8,128)}) custom-call(f32[2112,1024]{1,0:T(8,128)} %get-tuple-element.74.own_ref, bf16[704,1024]{1,0:T(8,128)(2,1)} %get-tuple-element.75.early_ref, bf16[1408,1024]{1,0:T(8,128)(2,1)} %get-tuple-element.76.late_ref), custom_call_target="tpu_custom_call" | custom-call | tf_op jit(solution)/shard_map/finish_experts/pallas_call | solution.py:324
  362.6 1.3 slice_bitcast_fusion
  363.9 1.3 slice_bitcast_fusion.1
  365.2 0.9 slice.26
  366.1 0.7 copy.40
  366.7 0.0 copy-start.1
  366.7 9.9 %finish_sums.1 = (f32[1024,1024]{1,0:T(8,128)}, f32[1024,1024]{1,0:T(8,128)}, f32[1024,1024]{1,0:T(8,128)}, f32[1024,1024]{1,0:T(8,128)}) custom-call(bf16[2,4,4,1024,128]{4,3,2,1,0:T(8,128)(2,1)} %bitcast.39), custom_call_target="tpu_custom_call" | custom-call | tf_op jit(solution)/shard_map/finish_sums/pallas_call | solution.py:295
  376.6 0.0 copy-start
  376.6 0.0 copy-done.1
  376.6 1.0 copy.45
  377.6 0.6 copy-done
  378.2 1.0 copy.46
Async XLA Ops:
  366.7 9.9 %copy-start.1 = (f32[256,1024]{1,0:T(8,128)S(1)}, f32[256,1024]{1,0:T(8,128)}, u32[]{:S(2)}) copy-start(f32[256,1024]{1,0:T(8,128)} %get-tuple-element.96) | copy-start | bytes 3145732
  376.6 1.6 copy-start
